TPU v7x, 128 devices: a whole 4x4x4 slice. The times are simulated.
128 devices in a mesh: expert: 16 (over x, y_lo, core), dp: 8 (over y_hi, z).
Axes of the slice: x: 4, y: 4 (y_hi: 2, y_lo: 2; y = y_hi * 2 + y_lo), z: 4, core: 2. Of those that a mesh axis runs over, the one named last changes fastest.
Arguments:
- tokens: bfloat16 [8, 8192, 2048], P('dp', 'expert'), may hold values from -6 to 6
- cotangent: bfloat16 [8, 8192, 2048], P('dp', 'expert'), may hold values from -0.09375 to 0.09375
- routes: int32 [8, 8192, 1], P('dp', 'expert'), may hold values from 0 to 15; in each aligned block of 512 rows (0 to 511, 512 to 1023, ..., all dimensions but the last counted through in order) at most 64 rows name the same one
- owner: int32 [16], replicated, may hold values from 0 to 15, as said below
- master: float32 [16, 2048, 2304], P('expert', 'dp'), may hold values from -0.125 to 0.125
- moment1: float32 [16, 2048, 2304], P('expert', 'dp'), may hold values from -1.8 to 1.8
- moment2: float32 [16, 2048, 2304], P('expert', 'dp'), may hold values from 0.01 to 1
Outputs:
- token_grad: bfloat16 [8, 8192, 2048], P('dp', 'expert')
- new_master: float32 [16, 2048, 2304], P('expert', 'dp')
- new_moment1: float32 [16, 2048, 2304], P('expert', 'dp')
- new_moment2: float32 [16, 2048, 2304], P('expert', 'dp')
Inputs may be any that keep to these rules, and one draw needn't show every extreme that they name: owner[j] is j or j xor (8), and owner[j] == j exactly when the same holds for j xor (8); at least one pair moves. `routes`: among the 512 tokens of one device at most 64 choose one expert, and some expert is chosen by exactly 64.
All inputs are finite; a program needn't handle non-finite values.
Results may differ from a plain program's by a relative error of at most 0.012.
Values may be sent and summed in bfloat16 or wider, within the bound.
No kernel may reach another device: no remote copies, remote signals or barrier semaphores. Data moves between devices by JAX's collectives and lax.ppermute only.
A program may use at most 128 MiB of HBM per device.

v0:
```python
import jax
import jax.numpy as jnp
from jax import lax
from jax.sharding import PartitionSpec as P


def swapped(value, axis, apart):
    return lax.ppermute(value, axis, [(i, i ^ 1 << apart) for i in range(lax.axis_size(axis))])


def per_device(tokens, cotangent, routes, owner, master, moment1, moment2):
    experts = lax.axis_size("expert")
    bit = experts.bit_length() - 2
    position = lax.axis_index("expert")
    keep = owner[position] == position
    hidden_units = master.shape[2] // 3
    partner = (
        swapped(master.astype(jnp.bfloat16), "expert", bit).astype(master.dtype),
        swapped(moment1.astype(jnp.bfloat16), "expert", bit).astype(moment1.dtype),
        swapped(moment2.astype(jnp.bfloat16), "expert", bit).astype(moment2.dtype),
    )
    placed_master = jnp.where(keep, master, partner[0])
    placed_first = jnp.where(keep, moment1, partner[1])
    placed_second = jnp.where(keep, moment2, partner[2])
    weights = lax.all_gather(placed_master[0].astype(jnp.bfloat16), "dp", axis=0, tiled=True)
    features = weights.shape[0]
    tok_count = tokens.shape[1]
    capacity = 2 * tok_count // experts
    route_ids = routes[0, :, 0]
    columns = jnp.arange(experts, dtype=jnp.int32)
    onehot = (route_ids[:, None] == columns[None, :]).astype(jnp.int32)
    slot = jnp.sum((jnp.cumsum(onehot, axis=0) - 1) * onehot, axis=1)
    flat = route_ids * capacity + slot
    send_x = jnp.zeros((experts * capacity, features), jnp.bfloat16).at[flat].set(tokens[0])
    send_dy = jnp.zeros((experts * capacity, features), jnp.bfloat16).at[flat].set(cotangent[0])
    gate_up = weights[:, : 2 * hidden_units]
    down = weights[:, 2 * hidden_units :]
    got_x, got_dy = (
        lax.all_to_all(
            send_x.reshape(experts, capacity, features),
            "expert",
            split_axis=0,
            concat_axis=0,
            tiled=True,
        ),
        lax.all_to_all(
            send_dy.reshape(experts, capacity, features),
            "expert",
            split_axis=0,
            concat_axis=0,
            tiled=True,
        ),
    )
    rows_x = got_x.reshape(experts * capacity, features)
    rows_dy = got_dy.reshape(experts * capacity, features)
    pre = jnp.dot(rows_x, gate_up, preferred_element_type=jnp.float32)
    gate_pre = pre[:, :hidden_units]
    up_pre = pre[:, hidden_units:]
    sig = jax.nn.sigmoid(gate_pre)
    act = gate_pre * sig
    hidden = (act * up_pre).astype(jnp.bfloat16)
    d_hidden = jnp.dot(rows_dy, down, preferred_element_type=jnp.float32)
    d_gate = (d_hidden * up_pre * sig * (1.0 + gate_pre * (1.0 - sig))).astype(jnp.bfloat16)
    d_up = (d_hidden * act).astype(jnp.bfloat16)
    d_both = jnp.concatenate([d_gate, d_up], axis=1)
    left = jnp.einsum("rd,rk->dk", rows_x, d_both, preferred_element_type=jnp.float32)
    right = jnp.einsum("rd,rk->dk", rows_dy, hidden, preferred_element_type=jnp.float32)
    grad = lax.psum_scatter(
        jnp.concatenate([left, right], axis=1).astype(jnp.bfloat16),
        "dp",
        scatter_dimension=0,
        tiled=True,
    ).astype(jnp.float32)
    in_grad = jnp.einsum("rk,dk->rd", d_both, gate_up, preferred_element_type=jnp.float32).astype(
        jnp.bfloat16
    )
    returned = lax.all_to_all(
        in_grad.reshape(experts, capacity, features),
        "expert",
        split_axis=0,
        concat_axis=0,
        tiled=True,
    )
    token_grad = returned.reshape(experts * capacity, features)[flat]
    new_first = 0.9 * placed_first[0] + 0.1 * grad
    new_second = 0.95 * placed_second[0] + 0.05 * grad * grad
    update = new_first / (1.0 - 0.9**10) / (jnp.sqrt(new_second / (1.0 - 0.95**10)) + 1e-08)
    new_master = placed_master[0] - 0.003 * (update + 0.1 * placed_master[0])
    return (token_grad[None], new_master[None], new_first[None], new_second[None])


def solution(mesh):
    placed = (
        P("dp", "expert", None),
        P("dp", "expert", None),
        P("dp", "expert", None),
        P(),
        P("expert", "dp", None),
        P("expert", "dp", None),
        P("expert", "dp", None),
    )
    return jax.shard_map(
        per_device,
        mesh=mesh,
        in_specs=placed,
        out_specs=(
            P("dp", "expert", None),
            P("expert", "dp", None),
            P("expert", "dp", None),
            P("expert", "dp", None),
        ),
        check_vma=False,
    )
```

profile of v0, /device:TPU:1, one launch (start us, length us, event | category | flops | bytes accessed | tf_op | source)
XLA Modules:
  0.0 480.2 jit_solution(11759934221335328963)
XLA Ops:
  7.2 0.0 copy-start
  7.2 0.0 copy-start.4
  7.2 0.0 all-gather.2.cloned.1.call-start
  7.2 3.2 copy.24
  10.4 2.8 convert_element_type.43
  13.2 3.6 collective-permute-start
  16.8 0.0 copy-done.4
  16.8 0.6 dynamic_slice.3
  18.0 24.2 %collective-permute-done = bf16[1,256,2304]{1,2,0:T(8,128)(2,1)S(1)} collective-permute-done((bf16[1,256,2304]{1,2,0:T(8,128)(2,1)}, bf16[1,256,2304]{1,2,0:T(8,128)(2,1)S(1)}, u32[]{:S(2)}, u32[]{:S(2)}) %collective-permute-start) | collective-permute-done | bytes 1179680 | tf_op jit(solution)/shard_map/ppermute | solution.py:8
  42.2 2.9 bitcast_convert_fusion
  45.2 0.0 all-gather.2.cloned.1.call-update
  45.2 0.0 copy-done.3
  45.2 1.2 reduce-window.6
  46.4 0.2 slice_reduce_fusion
  46.6 0.1 fusion.25
  46.7 6.2 %scatter_custom_fusion.1 = bf16[1024,2048]{1,0:T(8,128)(2,1)} fusion(s32[512]{0:T(512)S(1)} %bitcast.77, bf16[1,512,2048]{2,1,0:T(8,128)(2,1)S(1)} %copy-done, bf16[]{:T(256)} %constant.17.clone.1), kind=kCustom, calls=%fused_computation.30 | custom fusion | bytes 6291458 | tf_op jit(solution)/shard_map/scatter | solution.py:34
  53.0 5.7 %all-to-all-start.1 = ((bf16[16,64,2048]{2,1,0:T(8,128)(2,1)}), bf16[16,64,2048]{2,1,0:T(8,128)(2,1)}, u32[]{:S(2)}, u32[]{:S(2)}) async-start(bf16[16,64,2048]{2,1,0:T(8,128)(2,1)} %bitcast.72), calls=%async_computation.1 | async-start | bytes 8388608 | tf_op jit(solution)/shard_map/all_to_all | solution.py:39
  58.7 6.3 %scatter_custom_fusion = bf16[1024,2048]{1,0:T(8,128)(2,1)} fusion(s32[512]{0:T(512)S(1)} %bitcast.78, bf16[1,512,2048]{2,1,0:T(8,128)(2,1)S(1)} %copy-done.2, bf16[]{:T(256)} %constant.17.clone.1), kind=kCustom, calls=%fused_computation.32 | custom fusion | bytes 6291458 | tf_op jit(solution)/shard_map/scatter | solution.py:35
  65.0 52.7 %all-to-all-done.1 = bf16[16,64,2048]{2,1,0:T(8,128)(2,1)} async-done(((bf16[16,64,2048]{2,1,0:T(8,128)(2,1)}), bf16[16,64,2048]{2,1,0:T(8,128)(2,1)}, u32[]{:S(2)}, u32[]{:S(2)}) %all-to-all-start.1) | async-done | bytes 4194336 | tf_op jit(solution)/shard_map/all_to_all | solution.py:39
  117.8 6.0 %all-to-all-start = ((bf16[16,64,2048]{2,1,0:T(8,128)(2,1)}), bf16[16,64,2048]{2,1,0:T(8,128)(2,1)}, u32[]{:S(2)}, u32[]{:S(2)}) async-start(bf16[16,64,2048]{2,1,0:T(8,128)(2,1)} %bitcast.71), calls=%async_computation | async-start | bytes 8388608 | tf_op jit(solution)/shard_map/all_to_all | solution.py:46
  123.8 0.0 reduce-scatter.2.cloned.1.call-start
  123.8 119.3 %all-gather.2.cloned.1.call-done = bf16[2048,2304]{0,1:T(8,128)(2,1)} async-done(((bf16[256,2304]{0,1:T(8,128)(2,1)}), bf16[2048,2304]{0,1:T(8,128)(2,1)}) %all-gather.2.cloned.1.call-update) | async-done | bytes 9437200 | tf_op jit(solution)/shard_map/all_gather | solution.py:25
  243.1 11.7 %fusion.2 = f32[1024,1536]{0,1:T(8,128)} fusion(bf16[1024,2048]{1,0:T(8,128)(2,1)} %bitcast.13, bf16[2048,2304]{0,1:T(8,128)(2,1)} %all-gather.2.cloned.1.call-done), kind=kOutput, calls=%fused_computation.7 | convolution fusion | flops 6442450944 | bytes 16777216 | tf_op jit(solution)/shard_map/dot_general | solution.py:56
  254.8 0.0 all-to-all-done
  254.8 7.6 %convolution_convert_fusion.1 = bf16[2048,768]{0,1:T(8,128)(2,1)S(1)} fusion(bf16[1024,2048]{1,0:T(8,128)(2,1)} %bitcast.8, f32[1024,1536]{0,1:T(8,128)} %fusion.2), kind=kOutput, calls=%fused_computation.11 | convolution fusion | flops 3227516928 | bytes 13631488 | tf_op jit(solution)/shard_map/rd,rk->dk/dot_general | solution.py:67
  262.5 7.5 %multiply_convert_fusion.2 = (bf16[1024,768]{0,1:T(8,128)(2,1)S(1)}, bf16[1024,768]{0,1:T(8,128)(2,1)S(1)}) fusion(f32[1024,1536]{0,1:T(8,128)S(1)} %copy-done.5, bf16[1024,2048]{1,0:T(8,128)(2,1)} %bitcast.8, bf16[2048,2304]{0,1:T(8,128)(2,1)} %all-gather.2.cloned.1.call-done), kind=kOutput, calls=%fused_computation.17 | convolution fusion | flops 3231449088 | bytes 16777216 | tf_op jit(solution)/shard_map/dot_general | solution.py:62
  270.0 0.0 copy-start.6
  270.0 11.1 %convolution_convert_fusion = bf16[2048,1536]{0,1:T(8,128)(2,1)S(1)} fusion(bf16[1024,2048]{1,0:T(8,128)(2,1)} %bitcast.13, bf16[1024,768]{0,1:T(8,128)(2,1)S(1)} %get-tuple-element.13, bf16[1024,768]{0,1:T(8,128)(2,1)S(1)} %get-tuple-element.12), kind=kOutput, calls=%fused_computation.4 | convolution fusion | flops 6451888128 | bytes 13631488 | tf_op jit(solution)/shard_map/rd,rk->dk/dot_general | solution.py:66
  281.2 0.0 copy-done.6
  281.2 11.7 %pad_maximum_fusion = bf16[2048,2304]{0,1:T(8,128)(2,1)} fusion(bf16[2048,768]{0,1:T(8,128)(2,1)S(1)} %convolution_convert_fusion.1, bf16[2048,1536]{0,1:T(8,128)(2,1)S(1)} %convolution_convert_fusion), kind=kLoop, calls=%fused_computation.3 | loop fusion | flops 18874368 | bytes 18874368 | tf_op jit(solution)/shard_map/concatenate | solution.py:69
  292.9 0.0 reduce-scatter.2.cloned.1.call-update
  292.9 10.8 %fusion.4 = bf16[1024,2048]{1,0:T(8,128)(2,1)} fusion(bf16[2048,2304]{0,1:T(8,128)(2,1)} %all-gather.2.cloned.1.call-done, bf16[1024,768]{0,1:T(8,128)(2,1)} %copy-done.6, bf16[1024,768]{0,1:T(8,128)(2,1)S(1)} %get-tuple-element.12), kind=kOutput, calls=%fused_computation.9 | convolution fusion | flops 6450839552 | bytes 13631488 | tf_op jit(solution)/shard_map/rk,dk->rd/dot_general | solution.py:74
  303.7 5.1 %all-to-all-start.2 = ((bf16[16,64,2048]{2,1,0:T(8,128)(2,1)}), bf16[16,64,2048]{2,1,0:T(8,128)(2,1)}, u32[]{:S(2)}, u32[]{:S(2)}) async-start(bf16[16,64,2048]{2,1,0:T(8,128)(2,1)} %bitcast.73), calls=%async_computation.2 | async-start | bytes 8388608 | tf_op jit(solution)/shard_map/all_to_all | solution.py:77
  308.8 3.0 copy.30
  311.8 1.8 convert_element_type.53
  313.6 3.0 collective-permute-start.2
  316.6 3.0 copy.28
  319.7 2.8 convert_element_type.49
  322.5 0.0 collective-permute-start.1
  322.5 39.6 %all-to-all-done.2 = bf16[16,64,2048]{2,1,0:T(8,128)(2,1)} async-done(((bf16[16,64,2048]{2,1,0:T(8,128)(2,1)}), bf16[16,64,2048]{2,1,0:T(8,128)(2,1)}, u32[]{:S(2)}, u32[]{:S(2)}) %all-to-all-start.2) | async-done | bytes 4194336 | tf_op jit(solution)/shard_map/all_to_all | solution.py:77
  362.1 8.2 %gather_fusion = bf16[512,2048]{1,0:T(8,128)(2,1)} fusion(bf16[1024,2048]{1,0:T(8,128)(2,1)} %bitcast.15, s32[1024]{0:T(1024)S(1)} %pad_clamp_fusion), kind=kCustom, calls=%fused_computation | custom fusion | bytes 4196352 | tf_op jit(solution)/shard_map/gather | solution.py:84
  370.3 21.7 %collective-permute-done.2 = bf16[1,256,2304]{1,2,0:T(8,128)(2,1)} collective-permute-done((bf16[1,256,2304]{1,2,0:T(8,128)(2,1)S(1)}, bf16[1,256,2304]{1,2,0:T(8,128)(2,1)}, u32[]{:S(2)}, u32[]{:S(2)}) %collective-permute-start.2) | collective-permute-done | bytes 1179680 | tf_op jit(solution)/shard_map/ppermute | solution.py:8
  392.1 25.3 %collective-permute-done.1 = bf16[1,256,2304]{1,2,0:T(8,128)(2,1)} collective-permute-done((bf16[1,256,2304]{1,2,0:T(8,128)(2,1)}, bf16[1,256,2304]{1,2,0:T(8,128)(2,1)}, u32[]{:S(2)}, u32[]{:S(2)}) %collective-permute-start.1) | collective-permute-done | bytes 1179680 | tf_op jit(solution)/shard_map/ppermute | solution.py:8
  417.3 37.2 %reduce-scatter.2.cloned.1.call-done = bf16[256,2304]{0,1:T(8,128)(2,1)} async-done(((bf16[2048,2304]{0,1:T(8,128)(2,1)}), bf16[256,2304]{0,1:T(8,128)(2,1)}) %reduce-scatter.2.cloned.1.call-update) | async-done | bytes 1179664 | tf_op jit(solution)/shard_map/reduce_scatter | solution.py:68
  454.5 9.3 %fusion.22 = (f32[1,256,2304]{1,2,0:T(8,128)}, f32[1,256,2304]{1,2,0:T(8,128)}, f32[1,256,2304]{1,2,0:T(8,128)}) fusion(bf16[256,2304]{0,1:T(8,128)(2,1)} %reduce-scatter.2.cloned.1.call-done, f32[1,256,2304]{1,2,0:T(8,128)} %copy.30, bf16[1,256,2304]{1,2,0:T(8,128)(2,1)} %collective-permute-done.2, pred[]{:T(512)S(6)} %eq.36, f32[1,256,2304]{1,2,0:T(8,128)} %copy.28, ...), kind=kLoop, calls=%fused_computation.37 | loop fusion | flops 12976128 | bytes 18874368 | tf_op jit(solution)/shard_map/broadcast_in_dim | solution.py:89
  463.9 3.0 copy.31
  466.9 3.2 copy.32
  470.1 3.0 copy.33
  (13 shorter events, 0.1 us)
Async XLA Ops:
  7.2 39.6 %copy-start = (bf16[1,512,2048]{2,1,0:T(8,128)(2,1)S(1)}, bf16[1,512,2048]{2,1,0:T(8,128)(2,1)}, u32[]{:S(2)}) copy-start(bf16[1,512,2048]{2,1,0:T(8,128)(2,1)} %param.7) | copy-start | bytes 6291460
  7.2 9.6 %copy-start.4 = (s32[16]{0:T(128)S(1)}, s32[16]{0:T(128)}, u32[]{:S(2)}) copy-start(s32[16]{0:T(128)} %param.10) | copy-start | bytes 196
  7.2 235.9 %all-gather.2.cloned.1.call-start = ((), (), s32[]{:S(2)}) async-start(), calls=%async_computation.4 | async-start | bytes 10616832 | tf_op jit(solution)/shard_map/all_gather | solution.py:25
  13.2 32.0 %copy-start.3 = (s32[1,512,1]{1,2,0:T(1,128)S(1)}, s32[1,512,1]{1,2,0:T(1,128)}, u32[]{:S(2)}) copy-start(s32[1,512,1]{1,2,0:T(1,128)} %param.9) | copy-start | bytes 6148
  13.2 29.0 %collective-permute-start = (bf16[1,256,2304]{1,2,0:T(8,128)(2,1)}, bf16[1,256,2304]{1,2,0:T(8,128)(2,1)S(1)}, u32[]{:S(2)}, u32[]{:S(2)}) collective-permute-start(bf16[1,256,2304]{1,2,0:T(8,128)(2,1)} %convert_element_type.43), channel_id=1, source_target_pairs={{0,64},{8,72},{16,80},{24,88},{32,96},{40,104},{48,112},{56,120},{... | collective-permute-start | bytes 3538952 | tf_op jit(solution)/shard_map/ppermute | solution.py:8
  53.0 5.7 %copy-start.2 = (bf16[1,512,2048]{2,1,0:T(8,128)(2,1)S(1)}, bf16[1,512,2048]{2,1,0:T(8,128)(2,1)}, u32[]{:S(2)}) copy-start(bf16[1,512,2048]{2,1,0:T(8,128)(2,1)} %param.8) | copy-start | bytes 6291460
  53.0 64.8 %all-to-all-start.1 = ((bf16[16,64,2048]{2,1,0:T(8,128)(2,1)}), bf16[16,64,2048]{2,1,0:T(8,128)(2,1)}, u32[]{:S(2)}, u32[]{:S(2)}) async-start(bf16[16,64,2048]{2,1,0:T(8,128)(2,1)} %bitcast.72), calls=%async_computation.1 | async-start | bytes 8388608 | tf_op jit(solution)/shard_map/all_to_all | solution.py:39
  117.8 137.0 %all-to-all-start = ((bf16[16,64,2048]{2,1,0:T(8,128)(2,1)}), bf16[16,64,2048]{2,1,0:T(8,128)(2,1)}, u32[]{:S(2)}, u32[]{:S(2)}) async-start(bf16[16,64,2048]{2,1,0:T(8,128)(2,1)} %bitcast.71), calls=%async_computation | async-start | bytes 8388608 | tf_op jit(solution)/shard_map/all_to_all | solution.py:46
  123.8 330.8 %reduce-scatter.2.cloned.1.call-start = ((), (), s32[]{:S(2)}) async-start(), calls=%async_computation.5 | async-start | bytes 10616832 | tf_op jit(solution)/shard_map/reduce_scatter | solution.py:68
  254.8 7.7 %copy-start.5 = (f32[1024,1536]{0,1:T(8,128)S(1)}, f32[1024,1536]{0,1:T(8,128)}, u32[]{:S(2)}) copy-start(f32[1024,1536]{0,1:T(8,128)} %fusion.2) | copy-start | bytes 18874372
  270.0 11.1 %copy-start.6 = (bf16[1024,768]{0,1:T(8,128)(2,1)}, bf16[1024,768]{0,1:T(8,128)(2,1)S(1)}, u32[]{:S(2)}) copy-start(bf16[1024,768]{0,1:T(8,128)(2,1)S(1)} %get-tuple-element.13) | copy-start | bytes 4718596
  303.7 58.4 %all-to-all-start.2 = ((bf16[16,64,2048]{2,1,0:T(8,128)(2,1)}), bf16[16,64,2048]{2,1,0:T(8,128)(2,1)}, u32[]{:S(2)}, u32[]{:S(2)}) async-start(bf16[16,64,2048]{2,1,0:T(8,128)(2,1)} %bitcast.73), calls=%async_computation.2 | async-start | bytes 8388608 | tf_op jit(solution)/shard_map/all_to_all | solution.py:77
  313.6 78.4 %collective-permute-start.2 = (bf16[1,256,2304]{1,2,0:T(8,128)(2,1)S(1)}, bf16[1,256,2304]{1,2,0:T(8,128)(2,1)}, u32[]{:S(2)}, u32[]{:S(2)}) collective-permute-start(bf16[1,256,2304]{1,2,0:T(8,128)(2,1)S(1)} %convert_element_type.53), channel_id=1, source_target_pairs={{0,64},{8,72},{16,80},{24,88},{32,96},{40,104},{48,112},{56,120},{... | collective-permute-start | bytes 3538952 | tf_op jit(solution)/shard_map/ppermute | solution.py:8
  322.5 94.8 %collective-permute-start.1 = (bf16[1,256,2304]{1,2,0:T(8,128)(2,1)}, bf16[1,256,2304]{1,2,0:T(8,128)(2,1)}, u32[]{:S(2)}, u32[]{:S(2)}) collective-permute-start(bf16[1,256,2304]{1,2,0:T(8,128)(2,1)} %convert_element_type.49), channel_id=1, source_target_pairs={{0,64},{8,72},{16,80},{24,88},{32,96},{40,104},{48,112},{56,120},{... | collective-permute-start | bytes 3538952 | tf_op jit(solution)/shard_map/ppermute | solution.py:8
  466.9 6.2 %copy-start.1 = (bf16[1,512,2048]{2,1,0:T(8,128)(2,1)S(1)}, bf16[1,512,2048]{2,1,0:T(8,128)(2,1)}, u32[]{:S(2)}) copy-start(bf16[1,512,2048]{2,1,0:T(8,128)(2,1)} %param.7) | copy-start | bytes 6291460
Sparse Core Ops, SparseCore 0:
  45.3 197.7 all-gather.1
  293.0 161.4 reduce-scatter.1
where the time goes:
time: 489 us; the launch traced here: 480 us
  waiting for transfers between devices  320 us (65%)
  matrix products  48.8 us (10%)
  local copies, waits for them, and re-layouts  40.2 us (8%)
  other arithmetic  32.7 us (7%)
  starting transfers between devices  23.5 us (5%)
  between operations  15 us (3%)
    all_gather x1, waiting for transfers between devices, per_device(): lax.all_gather(placed_master[0].astype(jnp.bfloat16), 'dp', axis=0, tiled...  119 us
    ppermute x3, waiting for transfers between devices, swapped(): lax.ppermute(value, axis, [(i, i ^ 1 << apart) for i in range(lax.axis_si...  71.2 us
    all_to_all x1, waiting for transfers between devices, per_device(): lax.all_to_all(send_x.reshape(experts, capacity, features), 'expert', spl...  52.7 us
    all_to_all x1, waiting for transfers between devices, per_device(): lax.all_to_all(in_grad.reshape(experts, capacity, features), 'expert', sp...  39.6 us
    reduce_scatter x1, waiting for transfers between devices, per_device(): lax.psum_scatter(jnp.concatenate([left, right], axis=1).astype(jnp.bfloat...  37.2 us
    unnamed x20, local copies, waits for them, and re-layouts  18.6 us
    scatter x2, local copies, waits for them, and re-layouts, per_device(): jnp.zeros((experts * capacity, features), jnp.bfloat16).at[flat]  12.6 us
    concatenate x1, other arithmetic, per_device(): jnp.concatenate([left, right], axis=1).astype(jnp.bfloat16)  11.7 us
  transfers between devices with their start and end apart: 8, of which 7 were waited for; matrix products, arithmetic and copies ran while one was open for 12% of the time, Pallas kernels for 0%

commit v1 on v0

v1 whole, which is shorter than its diff:
```python
import functools
import jax
import jax.numpy as jnp
from jax import lax
from jax.experimental import pallas as pl
from jax.experimental.pallas import tpu as pltpu
from jax.sharding import PartitionSpec as P

BF = jnp.bfloat16
F32 = jnp.float32
VMEM_LIMIT = 56 * 1024 * 1024
ZN = 4


def params():
    return pltpu.CompilerParams(vmem_limit_bytes=VMEM_LIMIT)


def cost(flops, nbytes):
    return pl.CostEstimate(flops=int(flops), bytes_accessed=int(nbytes), transcendentals=0)


def permuted(value, axis, target):
    return lax.ppermute(value, axis, [(i, target(i)) for i in range(lax.axis_size(axis))])


def mm(a, b, dims):
    return lax.dot_general(a, b, (dims, ((), ())), preferred_element_type=F32)


def dispatch_kernel(flat_ref, tok_ref, out_ref, onehot_ref):
    @pl.when(pl.program_id(0) == 0)
    def _():
        rows, count = onehot_ref.shape
        ids = lax.broadcasted_iota(jnp.int32, (rows, count), 0)
        onehot_ref[...] = (ids == flat_ref[...]).astype(F32).astype(BF)

    out_ref[...] = mm(onehot_ref[...], tok_ref[...], ((1,), (0,))).astype(BF)


def dispatch(flat, tok, rows, first, blocks, place):
    count, features = tok.shape
    width = features // (2 * ZN)
    return pl.pallas_call(
        dispatch_kernel,
        grid=(blocks,),
        in_specs=[
            pl.BlockSpec((1, count), lambda i: (0, 0)),
            pl.BlockSpec((count, width), lambda i: (0, first + i)),
        ],
        out_specs=pl.BlockSpec((rows, width), lambda i: (0, place(i))),
        out_shape=jax.ShapeDtypeStruct((rows, blocks * width), BF),
        scratch_shapes=[pltpu.VMEM((rows, count), BF)],
        compiler_params=params(),
        cost_estimate=cost(2 * rows * count * blocks * width, 2 * blocks * width * (rows + count)),
        name="dispatch",
    )(flat.reshape(1, count), tok)


def combine_kernel(flat_ref, back_ref, out_ref, onehot_ref):
    @pl.when(pl.program_id(0) == 0)
    def _():
        count, rows = onehot_ref.shape
        ids = lax.broadcasted_iota(jnp.int32, (count, rows), 1)
        onehot_ref[...] = (ids == flat_ref[...]).astype(F32).astype(BF)

    out_ref[...] = mm(onehot_ref[...], back_ref[...], ((1,), (0,))).astype(BF)


def combine(flat, back, count):
    rows, features = back.shape
    groups = 2 * ZN
    width = features // groups
    return pl.pallas_call(
        combine_kernel,
        grid=(groups,),
        in_specs=[
            pl.BlockSpec((count, 1), lambda i: (0, 0)),
            pl.BlockSpec((rows, width), lambda i: (0, (i % ZN) * 2 + i // ZN)),
        ],
        out_specs=pl.BlockSpec((count, width), lambda i: (0, i)),
        out_shape=jax.ShapeDtypeStruct((count, features), BF),
        scratch_shapes=[pltpu.VMEM((count, rows), BF)],
        compiler_params=params(),
        cost_estimate=cost(2 * rows * count * features, 2 * features * (rows + count)),
        name="combine",
    )(flat.reshape(count, 1), back)


def forward_kernel(x_ref, gate_ref, up_ref, h_ref, p_ref, s_ref):
    x = x_ref[...]
    g = mm(x, gate_ref[...], ((1,), (0,)))
    u = mm(x, up_ref[...], ((1,), (0,)))
    sig = jax.nn.sigmoid(g)
    s = g * sig
    h_ref[...] = (s * u).astype(BF)
    p_ref[...] = u * sig * (1.0 + g * (1.0 - sig))
    s_ref[...] = s


def forward(x, gate_up):
    rows, features = x.shape
    hidden = gate_up.shape[1] // 2
    tile = min(256, hidden)
    tiles = hidden // tile
    out = pl.BlockSpec((rows, tile), lambda j: (0, j))
    return pl.pallas_call(
        forward_kernel,
        grid=(hidden // tile,),
        in_specs=[
            pl.BlockSpec((rows, features), lambda j: (0, 0)),
            pl.BlockSpec((features, tile), lambda j: (0, j)),
            pl.BlockSpec((features, tile), lambda j: (0, j + tiles)),
        ],
        out_specs=[out, out, out],
        out_shape=[
            jax.ShapeDtypeStruct((rows, hidden), BF),
            jax.ShapeDtypeStruct((rows, hidden), F32),
            jax.ShapeDtypeStruct((rows, hidden), F32),
        ],
        compiler_params=params(),
        cost_estimate=cost(4 * rows * features * hidden, 20e6),
        name="forward",
    )(x, gate_up, gate_up)


def hidden_first_kernel(dy_ref, down_ref, dh_ref):
    dh_ref[...] = mm(dy_ref[...], down_ref[...], ((1,), (0,)))


def hidden_kernel(dy_ref, down_ref, dh_ref, p_ref, s_ref, dg_ref, du_ref):
    dh = dh_ref[...] + mm(dy_ref[...], down_ref[...], ((1,), (0,)))
    dg_ref[...] = (dh * p_ref[...]).astype(BF)
    du_ref[...] = (dh * s_ref[...]).astype(BF)


def hidden_call(kernel, dy, down, more, outs, name):
    rows, features = dy.shape
    hidden = down.shape[1]
    tile = min(256, hidden)
    out = pl.BlockSpec((rows, tile), lambda j: (0, j))
    return pl.pallas_call(
        kernel,
        grid=(hidden // tile,),
        in_specs=[
            pl.BlockSpec((rows, features), lambda j: (0, 0)),
            pl.BlockSpec((features, tile), lambda j: (0, j)),
        ]
        + [out] * len(more),
        out_specs=[out] * len(outs),
        out_shape=[jax.ShapeDtypeStruct((rows, hidden), t) for t in outs],
        compiler_params=params(),
        cost_estimate=cost(2 * rows * features * hidden, 17e6),
        name=name,
    )(dy, down, *more)


def weight_kernel(a_ref, b_ref, out_ref):
    out_ref[...] = mm(a_ref[...], b_ref[...], ((0,), (0,))).astype(BF)


def weight_grad(a, b, name):
    rows, features = a.shape
    hidden = b.shape[1]
    tile = 512
    return pl.pallas_call(
        weight_kernel,
        grid=(features // tile,),
        in_specs=[
            pl.BlockSpec((rows, tile), lambda i: (0, i)),
            pl.BlockSpec((rows, hidden), lambda i: (0, 0)),
        ],
        out_specs=pl.BlockSpec((tile, hidden), lambda i: (i, 0)),
        out_shape=jax.ShapeDtypeStruct((features, hidden), BF),
        compiler_params=params(),
        cost_estimate=cost(2 * rows * features * hidden, 9e6),
        name=name,
    )(a, b)


def input_kernel(dg_ref, du_ref, gate_ref, up_ref, out_ref):
    acc = mm(dg_ref[...], gate_ref[...], ((1,), (1,)))
    acc = acc + mm(du_ref[...], up_ref[...], ((1,), (1,)))
    out_ref[...] = acc.astype(BF)


def input_grad(dg, du, gate_up):
    rows, hidden = dg.shape
    features = gate_up.shape[0]
    tile = 512
    left = pl.BlockSpec((rows, hidden), lambda i: (0, 0))
    gate = pl.BlockSpec((tile, hidden), lambda i: (i, 0))
    up = pl.BlockSpec((tile, hidden), lambda i: (i, 1))
    return pl.pallas_call(
        input_kernel,
        grid=(features // tile,),
        in_specs=[left, left, gate, up],
        out_specs=pl.BlockSpec((rows, tile), lambda i: (0, i)),
        out_shape=jax.ShapeDtypeStruct((rows, features), BF),
        compiler_params=params(),
        cost_estimate=cost(4 * rows * features * hidden, 14e6),
        name="input_grad",
    )(dg, du, gate_up, gate_up)


def adam_kernel(info_ref, own_ref, far_ref, w_ref, m_ref, v_ref, wb_ref, mb_ref, vb_ref, *rest):
    nw_ref, nm_ref, nv_ref = rest[-3:]
    keep = info_ref[0] != 0
    grad = own_ref[...].astype(F32) + far_ref[...].astype(F32)
    w = jnp.where(keep, w_ref[...], wb_ref[...].astype(F32))
    m = jnp.where(keep, m_ref[...], mb_ref[...].astype(F32))
    v = jnp.where(keep, v_ref[...], vb_ref[...].astype(F32))
    m = 0.9 * m + 0.1 * grad
    v = 0.95 * v + 0.05 * grad * grad
    update = m / (1.0 - 0.9**10) / (jnp.sqrt(v / (1.0 - 0.95**10)) + 1e-08)
    nw_ref[...] = w - 0.003 * (update + 0.1 * w)
    nm_ref[...] = m
    nv_ref[...] = v


def adam(info, near, far, state, moved, k, before):
    rows, hidden = far.shape
    tile = min(64, rows)
    chunk = pl.BlockSpec((tile, hidden), lambda i, info: (i, 0))
    column = pl.BlockSpec((tile, hidden), lambda i, info: (i, k))
    shape = jax.ShapeDtypeStruct(state[0].shape, F32)
    return pl.pallas_call(
        adam_kernel,
        grid_spec=pltpu.PrefetchScalarGridSpec(
            num_scalar_prefetch=1,
            grid=(rows // tile,),
            in_specs=[chunk, chunk]
            + [column] * 3
            + [chunk] * 3
            + [pl.BlockSpec(memory_space=pl.ANY)] * len(before),
            out_specs=[column] * 3,
        ),
        out_shape=[shape] * 3,
        input_output_aliases={9 + i: i for i in range(len(before))},
        compiler_params=params(),
        cost_estimate=cost(20 * rows * hidden, 34 * rows * hidden),
        name="adam",
    )(info, near, far, *state, *moved, *before)


def per_device(tokens, cotangent, routes, owner, master, moment1, moment2):
    experts = lax.axis_size("expert")
    half = experts // 2
    position = lax.axis_index("expert")
    high = lax.axis_index("dp") // ZN
    keep = owner[position] == position
    info = keep.astype(jnp.int32).reshape(1)
    hidden = master.shape[2] // 3
    features = tokens.shape[2]
    count = tokens.shape[1]
    capacity = 2 * count // experts
    rows = experts * capacity
    replicas = lax.axis_size("dp")
    z_groups = [[h * ZN + z for z in range(ZN)] for h in range(replicas // ZN)]

    route_ids = routes[0, :, 0]
    columns = jnp.arange(experts, dtype=jnp.int32)
    onehot = (route_ids[:, None] == columns[None, :]).astype(jnp.int32)
    slot = jnp.sum((jnp.cumsum(onehot, axis=0) - 1) * onehot, axis=1)
    flat = route_ids * capacity + slot
    groups = 2 * ZN
    send_x = dispatch(flat, tokens[0], rows, 0, groups, lambda i: (i % ZN) * 2 + i // ZN)
    send_dy = [dispatch(flat, cotangent[0], rows, n * ZN, ZN, lambda i: i) for n in range(2)]

    def over_owners(value):
        return permuted(value, "expert", lambda i: i ^ half)

    def over_high(value):
        return permuted(value, "dp", lambda i: i ^ ZN)

    def over_experts(value):
        boxes = value.reshape(experts, capacity, value.shape[1])
        out = lax.all_to_all(boxes, "expert", split_axis=0, concat_axis=0, tiled=True)
        return out.reshape(value.shape)

    def gathered(value):
        return lax.all_gather(value, "dp", axis=0, tiled=True, axis_index_groups=z_groups)

    def scattered(grad):
        return lax.psum_scatter(
            grad, "dp", scatter_dimension=0, tiled=True, axis_index_groups=z_groups
        )

    def both(near, far):
        return jnp.where(high == 0, near, far), jnp.where(high == 0, far, near)

    split = 2 * hidden
    own_a, own_b = master[0, :, :split].astype(BF), master[0, :, split:].astype(BF)
    other_a = over_owners(own_a)
    own_b, other_a = lax.optimization_barrier((own_b, other_a))
    other_b = over_owners(own_b)
    placed_a = jnp.where(keep, own_a, other_a)
    far_a = over_high(placed_a)
    placed_a, far_a, other_b, send_x = lax.optimization_barrier((placed_a, far_a, other_b, send_x))
    gate_up = gathered(jnp.concatenate(both(placed_a, far_a), axis=0))
    x = over_experts(send_x)
    placed_b = jnp.where(keep, own_b, other_b)
    far_b = over_high(placed_b)
    down = [gathered(v) for v in both(placed_b, far_b)]

    send_first, x = lax.optimization_barrier((send_dy[0], x))
    dy_first = over_experts(send_first)
    h, p, s = forward(x, gate_up)
    send_second, h = lax.optimization_barrier((send_dy[1], h))
    dy_second = over_experts(send_second)
    part_first = scattered(weight_grad(dy_first, h, "grad_down"))
    (dh,) = hidden_call(hidden_first_kernel, dy_first, down[0], [], [F32], "hidden_first")

    m_own, v_own = moment1[0].astype(BF), moment2[0].astype(BF)
    m_own = [m_own[:, :hidden], m_own[:, hidden:]]
    dy_second, *m_own, v_own = lax.optimization_barrier((dy_second, *m_own, v_own))
    m_other = [over_owners(v) for v in m_own]
    v_other = over_owners(v_own)
    part_second = scattered(weight_grad(dy_second, h, "grad_down"))
    dg, du = hidden_call(
        hidden_kernel, dy_second, down[1], [dh, p, s], [BF, BF], "hidden_grads"
    )
    grad, m_other[0] = lax.optimization_barrier((weight_grad(x, dg, "grad_gate"), m_other[0]))
    part_gate = scattered(grad).reshape(2, -1, hidden)
    grad, m_other[1] = lax.optimization_barrier((weight_grad(x, du, "grad_up"), m_other[1]))
    part_up = scattered(grad).reshape(2, -1, hidden)
    near, away = both(part_first, part_second)
    sums = {2: (near, over_high(away))}
    for k, part in ((0, part_gate), (1, part_up)):
        near, away = both(part[0], part[1])
        sums[k] = (near, over_high(away))
    send_back = input_grad(dg, du, gate_up)
    send_back, v_other = lax.optimization_barrier((send_back, v_other))
    token_grad = combine(flat, over_experts(send_back), count)

    m_other = (m_other[0], m_other[1][:, :hidden], m_other[1][:, hidden:])
    other = (other_a[:, :hidden], other_a[:, hidden:], other_b)
    state = (master[0], moment1[0], moment2[0])
    new = ()
    for k in (2, 0, 1):
        near, far = sums[k]
        shifted = (other[k], m_other[k], v_other[:, k * hidden : (k + 1) * hidden])
        new = adam(info, near, far, state, shifted, k, new)
    return (token_grad[None], new[0][None], new[1][None], new[2][None])


def solution(mesh):
    placed = (
        P("dp", "expert", None),
        P("dp", "expert", None),
        P("dp", "expert", None),
        P(),
        P("expert", "dp", None),
        P("expert", "dp", None),
        P("expert", "dp", None),
    )
    return jax.shard_map(
        per_device,
        mesh=mesh,
        in_specs=placed,
        out_specs=(
            P("dp", "expert", None),
            P("expert", "dp", None),
            P("expert", "dp", None),
            P("expert", "dp", None),
        ),
        check_vma=False,
    )
```

time: 489 us -> 366 us (0.75); the launches traced: 480 us -> 363 us
  waiting for transfers between devices: 320 us -> 160 us
  Pallas kernels: 0 us -> 100 us
  matrix products: 48.8 us -> 0 us
  starting transfers between devices: 23.5 us -> 63.5 us
  local copies, waits for them, and re-layouts: 40.2 us -> 11 us
  other arithmetic: 32.7 us -> 12.2 us
    all_gather x1 -> x3, waiting for transfers between devices: 119 us -> 0.02 us  [gathered(): lax.all_gather(value, 'dp', axis=0, tiled=True, axis_index_groups=z_groups)]
    pallas_call x0 -> x15, Pallas kernels: none -> 100 us  [the longest x4 24.1 us: weight_grad(): pl.pallas_call(weight_kernel, grid=(features // tile,), in_specs=[pl.Bloc...]
    all_to_all x3 -> x4, waiting for transfers between devices: 92.3 us -> 37.9 us  [over_experts(): lax.all_to_all(boxes, 'expert', split_axis=0, concat_axis=0, tiled=True)]
    dot_general x5 -> x0, matrix products: 48.8 us -> none  [the longest x1 11.7 us: per_device(): pre = jnp.dot(rows_x, gate_up, preferred_element_type=jnp.float32)]
    ppermute x3 -> x10, waiting for transfers between devices: 71.2 us -> 94.6 us  [permuted(): lax.ppermute(value, axis, [(i, target(i)) for i in range(lax.axis_size(ax...]
    all_to_all x3 -> x4, starting transfers between devices: 16.8 us -> 39.6 us  [over_experts(): lax.all_to_all(boxes, 'expert', split_axis=0, concat_axis=0, tiled=True)]
    ppermute x3 -> x10, starting transfers between devices: 6.62 us -> 23.6 us  [permuted(): lax.ppermute(value, axis, [(i, target(i)) for i in range(lax.axis_size(ax...]
    unnamed x20, local copies, waits for them, and re-layouts: 18.6 us -> 5.09 us
  transfers between devices with their start and end apart: 8 -> 21, of which waited for: 7 -> 13; matrix products, arithmetic and copies ran while one was open for 12% -> 4% of each run, Pallas kernels for 0% -> 26%
where the time goes in v1:
time: 366 us; the launch traced here: 363 us
  waiting for transfers between devices  160 us (44%)
  Pallas kernels  100 us (27%)
  starting transfers between devices  63.5 us (17%)
  between operations  15 us (4%)
  other arithmetic  12.2 us (3%)
  local copies, waits for them, and re-layouts  11 us (3%)
    ppermute x10, waiting for transfers between devices, permuted(): lax.ppermute(value, axis, [(i, target(i)) for i in range(lax.axis_size(ax...  94.6 us
    all_to_all x4, starting transfers between devices, over_experts(): lax.all_to_all(boxes, 'expert', split_axis=0, concat_axis=0, tiled=True)  39.6 us
    all_to_all x4, waiting for transfers between devices, over_experts(): lax.all_to_all(boxes, 'expert', split_axis=0, concat_axis=0, tiled=True)  37.9 us
    reduce_scatter x4, waiting for transfers between devices, scattered(): lax.psum_scatter(grad, 'dp', scatter_dimension=0, tiled=True, axis_index_...  27.1 us
    pallas_call x4, Pallas kernels, weight_grad(): pl.pallas_call(weight_kernel, grid=(features // tile,), in_specs=[pl.Bloc...  24.1 us
    ppermute x10, starting transfers between devices, permuted(): lax.ppermute(value, axis, [(i, target(i)) for i in range(lax.axis_size(ax...  23.6 us
    pallas_call x3, Pallas kernels, dispatch(): pl.pallas_call(dispatch_kernel, grid=(blocks,), in_specs=[pl.BlockSpec((1...  17 us
    pallas_call x2, Pallas kernels, hidden_call(): pl.pallas_call(kernel, grid=(hidden // tile,), in_specs=[pl.BlockSpec((ro...  14.3 us
  transfers between devices with their start and end apart: 21, of which 13 were waited for; matrix products, arithmetic and copies ran while one was open for 4% of the time, Pallas kernels for 26%

profile of v1, /device:TPU:1, one launch (start us, length us, event | category | flops | bytes accessed | tf_op | source)
XLA Modules:
  0.0 362.6 jit_solution(7216416221525349045)
XLA Ops:
  7.2 1.8 convert.5
  9.1 3.7 %collective-permute-start = (bf16[256,1536]{1,0:T(8,128)(2,1)S(1)}, bf16[256,1536]{1,0:T(8,128)(2,1)S(1)}, u32[]{:S(2)}, u32[]{:S(2)}) collective-permute-start(bf16[256,1536]{1,0:T(8,128)(2,1)S(1)} %slice_bitcast_fusion), channel_id=1, source_target_pairs={{0,64},{8,72},{16,80},{24,88},{32,96},{40,104},{48,112},{56,120},{... | collective-permute-start | bytes 2359304 | tf_op jit(solution)/shard_map/ppermute | solution.py:24
  14.0 15.5 %collective-permute-done = bf16[256,1536]{1,0:T(8,128)(2,1)S(1)} collective-permute-done((bf16[256,1536]{1,0:T(8,128)(2,1)S(1)}, bf16[256,1536]{1,0:T(8,128)(2,1)S(1)}, u32[]{:S(2)}, u32[]{:S(2)}) %collective-permute-start) | collective-permute-done | bytes 786464 | tf_op jit(solution)/shard_map/ppermute | solution.py:24
  29.6 3.4 collective-permute-start.1
  34.5 2.8 collective-permute-start.2
  37.9 7.8 %dispatch.5 = bf16[1024,2048]{1,0:T(8,128)(2,1)} custom-call(s32[1,512]{1,0:T(1,128)} %bitcast_add_fusion.flat_ref, bf16[512,2048]{1,0:T(8,128)(2,1)} %bitcast.74), custom_call_target="tpu_custom_call" | custom-call | flops 2147483648 | bytes 6291456 | tf_op jit(solution)/shard_map/dispatch/pallas_call | solution.py:44
  45.8 3.4 collective-permute-done.1
  49.3 1.2 pad_maximum_fusion
  50.6 7.7 %all-to-all-start = ((bf16[16,64,2048]{2,1,0:T(8,128)(2,1)}), bf16[16,64,2048]{2,1,0:T(8,128)(2,1)}, u32[]{:S(2)}, u32[]{:S(2)}) async-start(bf16[16,64,2048]{2,1,0:T(8,128)(2,1)} %bitcast.69), calls=%async_computation | async-start | bytes 8388608 | tf_op jit(solution)/shard_map/all_to_all | solution.py:278
  58.4 2.7 collective-permute-start.3
  61.1 43.6 %collective-permute-done.3 = bf16[256,768]{1,0:T(8,128)(2,1)S(1)} collective-permute-done((bf16[256,768]{1,0:T(8,128)(2,1)S(1)}, bf16[256,768]{1,0:T(8,128)(2,1)S(1)}, u32[]{:S(2)}, u32[]{:S(2)}) %collective-permute-start.3) | collective-permute-done | bytes 393248 | tf_op jit(solution)/shard_map/ppermute | solution.py:24
  106.4 4.6 %dispatch.4 = bf16[1024,1024]{1,0:T(8,128)(2,1)} custom-call(s32[1,512]{1,0:T(1,128)} %bitcast_add_fusion.flat_ref, bf16[512,2048]{1,0:T(8,128)(2,1)} %bitcast.66), custom_call_target="tpu_custom_call" | custom-call | flops 1073741824 | bytes 3145728 | tf_op jit(solution)/shard_map/dispatch/pallas_call | solution.py:44
  111.3 15.9 %all-to-all-start.2 = ((bf16[16,64,1024]{2,1,0:T(8,128)(2,1)}), bf16[16,64,1024]{2,1,0:T(8,128)(2,1)S(1)}, u32[]{:S(2)}, u32[]{:S(2)}) async-start(bf16[16,64,1024]{2,1,0:T(8,128)(2,1)} %bitcast.65), calls=%async_computation.2 | async-start | bytes 4194304 | tf_op jit(solution)/shard_map/all_to_all | solution.py:278
  127.2 4.6 %dispatch.3 = bf16[1024,1024]{1,0:T(8,128)(2,1)} custom-call(s32[1,512]{1,0:T(1,128)} %bitcast_add_fusion.flat_ref, bf16[512,2048]{1,0:T(8,128)(2,1)} %bitcast.67), custom_call_target="tpu_custom_call" | custom-call | flops 1073741824 | bytes 3145728 | tf_op jit(solution)/shard_map/dispatch/pallas_call | solution.py:44
  131.8 12.4 %forward.1 = (bf16[1024,768]{1,0:T(8,128)(2,1)}, f32[1024,768]{1,0:T(8,128)}, f32[1024,768]{1,0:T(8,128)}) custom-call(bf16[1024,2048]{1,0:T(8,128)(2,1)} %bitcast.13.x_ref.a_ref, bf16[2048,1536]{1,0:T(8,128)(2,1)} %all-gather.4.cloned.1.call-done.gate_ref.up_ref, bf16[2048,1536]{1,0:T(8,128)(2,1)} %all-gather.4.cloned.1.call-done.gate_ref.up_ref), custom_call_target="tpu_custom_call" | custom-call | flops 6442450944 | bytes 20000000 | tf_op jit(solution)/shard_map/forward/pallas_call | solution.py:107
  144.2 9.9 %all-to-all-done.2 = bf16[16,64,1024]{2,1,0:T(8,128)(2,1)S(1)} async-done(((bf16[16,64,1024]{2,1,0:T(8,128)(2,1)}), bf16[16,64,1024]{2,1,0:T(8,128)(2,1)S(1)}, u32[]{:S(2)}, u32[]{:S(2)}) %all-to-all-start.2) | async-done | bytes 2097184 | tf_op jit(solution)/shard_map/all_to_all | solution.py:278
  154.1 1.3 copy-done.2
  155.4 4.7 %grad_down.2 = bf16[1024,768]{1,0:T(8,128)(2,1)} custom-call(bf16[1024,1024]{1,0:T(8,128)(2,1)} %bitcast.62, bf16[1024,768]{1,0:T(8,128)(2,1)} %get-tuple-element.62.b_ref), custom_call_target="tpu_custom_call" | custom-call | flops 1610612736 | bytes 9000000 | tf_op jit(solution)/shard_map/grad_down/pallas_call | solution.py:166
  160.1 5.9 %all-to-all-start.1 = ((bf16[16,64,1024]{2,1,0:T(8,128)(2,1)}), bf16[16,64,1024]{2,1,0:T(8,128)(2,1)}, u32[]{:S(2)}, u32[]{:S(2)}) async-start(bf16[16,64,1024]{2,1,0:T(8,128)(2,1)} %bitcast.64), calls=%async_computation.1 | async-start | bytes 4194304 | tf_op jit(solution)/shard_map/all_to_all | solution.py:278
  166.4 1.5 copy-done.1
  168.0 25.2 %all-to-all-done.1 = bf16[16,64,1024]{2,1,0:T(8,128)(2,1)} async-done(((bf16[16,64,1024]{2,1,0:T(8,128)(2,1)}), bf16[16,64,1024]{2,1,0:T(8,128)(2,1)}, u32[]{:S(2)}, u32[]{:S(2)}) %all-to-all-start.1) | async-done | bytes 2097184 | tf_op jit(solution)/shard_map/all_to_all | solution.py:278
  193.1 4.7 %grad_down.3 = bf16[1024,768]{1,0:T(8,128)(2,1)} custom-call(bf16[1024,1024]{1,0:T(8,128)(2,1)} %bitcast.15.dy_ref.a_ref, bf16[1024,768]{1,0:T(8,128)(2,1)} %get-tuple-element.62.b_ref), custom_call_target="tpu_custom_call" | custom-call | flops 1610612736 | bytes 9000000 | tf_op jit(solution)/shard_map/grad_down/pallas_call | solution.py:166
  197.9 5.8 %hidden_first.1.dh_ref = f32[1024,768]{1,0:T(8,128)} custom-call(bf16[1024,1024]{1,0:T(8,128)(2,1)} %bitcast.63, bf16[1024,768]{1,0:T(8,128)(2,1)} %all-gather.8.cloned.1.call-done.down_ref), custom_call_target="tpu_custom_call" | custom-call | flops 1610612736 | bytes 17000000 | tf_op jit(solution)/shard_map/hidden_first/pallas_call | solution.py:142
  204.7 8.5 %hidden_grads.1 = (bf16[1024,768]{1,0:T(8,128)(2,1)}, bf16[1024,768]{1,0:T(8,128)(2,1)}) custom-call(bf16[1024,1024]{1,0:T(8,128)(2,1)} %bitcast.15.dy_ref.a_ref, bf16[1024,768]{1,0:T(8,128)(2,1)} %all-gather.6.cloned.1.call-done.down_ref, f32[1024,768]{1,0:T(8,128)} %hidden_first.1.dh_ref, f32[1024,768]{1,0:T(8,128)} %get-tuple-element.49.p_ref, ...), custom_call_target="tpu_custom_call" | custom-call | flops 1610612736 | bytes 17000000 | tf_op jit(solution)/shard_map/hidden_grads/pallas_call | solution.py:142
  213.2 7.4 %grad_gate.1 = bf16[2048,768]{1,0:T(8,128)(2,1)} custom-call(bf16[1024,2048]{1,0:T(8,128)(2,1)} %bitcast.13.x_ref.a_ref, bf16[1024,768]{1,0:T(8,128)(2,1)} %get-tuple-element.51.dg_ref.b_ref), custom_call_target="tpu_custom_call" | custom-call | flops 3221225472 | bytes 9000000 | tf_op jit(solution)/shard_map/grad_gate/pallas_call | solution.py:166
  220.7 2.3 collective-permute-start.5
  223.0 7.4 %grad_up.1 = bf16[2048,768]{1,0:T(8,128)(2,1)} custom-call(bf16[1024,2048]{1,0:T(8,128)(2,1)} %bitcast.13.x_ref.a_ref, bf16[1024,768]{1,0:T(8,128)(2,1)} %get-tuple-element.52.du_ref.b_ref), custom_call_target="tpu_custom_call" | custom-call | flops 3221225472 | bytes 9000000 | tf_op jit(solution)/shard_map/grad_up/pallas_call | solution.py:166
  230.4 10.0 %collective-permute-done.5 = bf16[256,1536]{1,0:T(8,128)(2,1)} collective-permute-done((bf16[256,1536]{1,0:T(8,128)(2,1)S(1)}, bf16[256,1536]{1,0:T(8,128)(2,1)}, u32[]{:S(2)}, u32[]{:S(2)}) %collective-permute-start.5) | collective-permute-done | bytes 786464 | tf_op jit(solution)/shard_map/ppermute | solution.py:24
  240.4 2.2 collective-permute-start.4
  242.6 10.8 %input_grad.1 = bf16[1024,2048]{1,0:T(8,128)(2,1)} custom-call(bf16[1024,768]{1,0:T(8,128)(2,1)} %get-tuple-element.51.dg_ref.b_ref, bf16[1024,768]{1,0:T(8,128)(2,1)} %get-tuple-element.52.du_ref.b_ref, bf16[2048,1536]{1,0:T(8,128)(2,1)} %all-gather.4.cloned.1.call-done.gate_ref.up_ref, bf16[2048,1536]{1,0:T(8,128)(2,1)} %all-gather.4.cloned.1.call-done.gate_ref.up_ref), custom_call_target="tpu_custom_call" | custom-call | flops 6442450944 | bytes 14000000 | tf_op jit(solution)/shard_map/input_grad/pallas_call | solution.py:194
  253.4 13.9 %collective-permute-done.4 = bf16[256,2304]{1,0:T(8,128)(2,1)S(1)} collective-permute-done((bf16[256,2304]{1,0:T(8,128)(2,1)S(1)}, bf16[256,2304]{1,0:T(8,128)(2,1)S(1)}, u32[]{:S(2)}, u32[]{:S(2)}) %collective-permute-start.4) | collective-permute-done | bytes 1179680 | tf_op jit(solution)/shard_map/ppermute | solution.py:24
  267.4 10.1 %all-to-all-start.3 = ((bf16[16,64,2048]{2,1,0:T(8,128)(2,1)}), bf16[16,64,2048]{2,1,0:T(8,128)(2,1)}, u32[]{:S(2)}, u32[]{:S(2)}) async-start(bf16[16,64,2048]{2,1,0:T(8,128)(2,1)} %bitcast.68), calls=%async_computation.3 | async-start | bytes 8388608 | tf_op jit(solution)/shard_map/all_to_all | solution.py:278
  279.3 2.0 fusion.4
  281.4 1.9 broadcast_select_fusion.4
  283.3 1.5 collective-permute-start.9
  284.8 2.1 broadcast_select_fusion.6
  286.8 1.3 collective-permute-start.8
  288.2 27.1 %reduce-scatter.5.cloned.1.call-done = bf16[512,768]{1,0:T(8,128)(2,1)} async-done(((bf16[2048,768]{1,0:T(8,128)(2,1)}), bf16[512,768]{1,0:T(8,128)(2,1)}) %reduce-scatter.5.cloned.1.call-update) | async-done | bytes 786448 | tf_op jit(solution)/shard_map/reduce_scatter | solution.py:285
  315.3 1.9 broadcast_select_fusion.8
  317.2 2.7 collective-permute-start.6
  321.0 1.7 collective-permute-done.9.far_ref
  323.5 4.6 %adam.3 = (f32[256,2304]{1,0:T(8,128)}, f32[256,2304]{1,0:T(8,128)}, f32[256,2304]{1,0:T(8,128)}) custom-call(s32[1]{0:T(128)} %bitcast.23.info_ref, bf16[256,768]{1,0:T(8,128)(2,1)} %get-tuple-element.80.own_ref, bf16[256,768]{1,0:T(8,128)(2,1)} %copy-done.4, f32[256,2304]{1,0:T(8,128)} %bitcast.50, f32[256,2304]{1,0:T(8,128)} %bitcast.53, ...), custom_call_target="tpu_custom_call" | custom-call | flops 3932160 | bytes 6684672 | tf_op jit(solution)/shard_map/adam/pallas_call | solution.py:227
  328.1 2.6 all-to-all-done.3
  330.7 8.0 %combine.1 = bf16[512,2048]{1,0:T(8,128)(2,1)} custom-call(s32[512,1]{1,0:T(8,128)} %copy.21.flat_ref, bf16[1024,2048]{1,0:T(8,128)(2,1)} %bitcast.21.back_ref), custom_call_target="tpu_custom_call" | custom-call | flops 2147483648 | bytes 6291456 | tf_op jit(solution)/shard_map/combine/pallas_call | solution.py:74
  338.7 3.3 collective-permute-done.8.far_ref
  342.7 4.6 %adam.4 = (f32[256,2304]{1,0:T(8,128)}, f32[256,2304]{1,0:T(8,128)}, f32[256,2304]{1,0:T(8,128)}) custom-call(s32[1]{0:T(128)} %bitcast.23.info_ref, bf16[256,768]{1,0:T(8,128)(2,1)} %get-tuple-element.84.own_ref, bf16[256,768]{1,0:T(8,128)(2,1)} %copy-done.7, f32[256,2304]{1,0:T(8,128)} %bitcast.51, ...), custom_call_target="tpu_custom_call", output_to_operand_aliasing={{0}: (9, {}), {1}: (10, {}), {2}: (11, {})} | custom-call | flops 3932160 | bytes 6684672 | tf_op jit(solution)/shard_map/adam/pallas_call | solution.py:227
  347.3 3.1 collective-permute-done.6.far_ref
  351.1 4.6 %adam.5 = (f32[256,2304]{1,0:T(8,128)}, f32[256,2304]{1,0:T(8,128)}, f32[256,2304]{1,0:T(8,128)}) custom-call(s32[1]{0:T(128)} %bitcast.23.info_ref, bf16[256,768]{1,0:T(8,128)(2,1)} %get-tuple-element.86.own_ref, bf16[256,768]{1,0:T(8,128)(2,1)} %copy-done.6, f32[256,2304]{1,0:T(8,128)} %bitcast.52, ...), custom_call_target="tpu_custom_call", output_to_operand_aliasing={{0}: (9, {}), {1}: (10, {}), {2}: (11, {})} | custom-call | flops 3932160 | bytes 6684672 | tf_op jit(solution)/shard_map/adam/pallas_call | solution.py:227
  (64 shorter events, 11.9 us)
Async XLA Ops:
  7.2 5.6 %copy-start.9 = (s32[16]{0:T(128)S(1)}, s32[16]{0:T(128)}, u32[]{:S(2)}) copy-start(s32[16]{0:T(128)} %param.10) | copy-start | bytes 196
  7.2 124.6 %all-gather.4.cloned.1.call-start = ((), (), s32[]{:S(2)}) async-start(), calls=%async_computation.8 | async-start | bytes 7864320 | tf_op jit(solution)/shard_map/all_gather | solution.py:282
  9.0 24.0 %copy-start.8 = (s32[1,512,1]{1,2,0:T(1,128)S(1)}, s32[1,512,1]{1,2,0:T(1,128)}, u32[]{:S(2)}) copy-start(s32[1,512,1]{1,2,0:T(1,128)} %param.9) | copy-start | bytes 6148
  9.1 20.4 %collective-permute-start = (bf16[256,1536]{1,0:T(8,128)(2,1)S(1)}, bf16[256,1536]{1,0:T(8,128)(2,1)S(1)}, u32[]{:S(2)}, u32[]{:S(2)}) collective-permute-start(bf16[256,1536]{1,0:T(8,128)(2,1)S(1)} %slice_bitcast_fusion), channel_id=1, source_target_pairs={{0,64},{8,72},{16,80},{24,88},{32,96},{40,104},{48,112},{56,120},{... | collective-permute-start | bytes 2359304 | tf_op jit(solution)/shard_map/ppermute | solution.py:24
  29.6 19.6 %collective-permute-start.1 = (bf16[256,1536]{1,0:T(8,128)(2,1)S(1)}, bf16[256,1536]{1,0:T(8,128)(2,1)S(1)}, u32[]{:S(2)}, u32[]{:S(2)}) collective-permute-start(bf16[256,1536]{1,0:T(8,128)(2,1)S(1)} %broadcast_select_fusion.2), channel_id=1, source_target_pairs={{0,4},{1,5},{2,6},{3,7},{4,0},{5,1},{6,2},{7,3},{8,12},{9,13},{10,... | collective-permute-start | bytes 2359304 | tf_op jit(solution)/shard_map/ppermute | solution.py:24
  34.5 11.3 %collective-permute-start.2 = (bf16[256,768]{1,0:T(8,128)(2,1)S(1)}, bf16[256,768]{1,0:T(8,128)(2,1)S(1)}, u32[]{:S(2)}, u32[]{:S(2)}) collective-permute-start(bf16[256,768]{1,0:T(8,128)(2,1)S(1)} %slice_bitcast_fusion.1), channel_id=1, source_target_pairs={{0,64},{8,72},{16,80},{24,88},{32,96},{40,104},{48,112},{56,120},{... | collective-permute-start | bytes 1179656 | tf_op jit(solution)/shard_map/ppermute | solution.py:24
  45.8 12.5 %copy-start.3 = (bf16[256,768]{1,0:T(8,128)(2,1)}, bf16[256,768]{1,0:T(8,128)(2,1)S(1)}, u32[]{:S(2)}) copy-start(bf16[256,768]{1,0:T(8,128)(2,1)S(1)} %collective-permute-done.2.wb_ref) | copy-start | bytes 1179652
  50.6 60.7 %all-to-all-start = ((bf16[16,64,2048]{2,1,0:T(8,128)(2,1)}), bf16[16,64,2048]{2,1,0:T(8,128)(2,1)}, u32[]{:S(2)}, u32[]{:S(2)}) async-start(bf16[16,64,2048]{2,1,0:T(8,128)(2,1)} %bitcast.69), calls=%async_computation | async-start | bytes 8388608 | tf_op jit(solution)/shard_map/all_to_all | solution.py:278
  58.2 139.7 %all-gather.8.cloned.1.call-start = ((), (), s32[]{:S(2)}) async-start(), calls=%async_computation.10 | async-start | bytes 1966080 | tf_op jit(solution)/shard_map/all_gather | solution.py:282
  58.4 46.3 %collective-permute-start.3 = (bf16[256,768]{1,0:T(8,128)(2,1)S(1)}, bf16[256,768]{1,0:T(8,128)(2,1)S(1)}, u32[]{:S(2)}, u32[]{:S(2)}) collective-permute-start(bf16[256,768]{1,0:T(8,128)(2,1)S(1)} %broadcast_select_fusion.3), channel_id=1, source_target_pairs={{0,4},{1,5},{2,6},{3,7},{4,0},{5,1},{6,2},{7,3},{8,12},{9,13},{10,... | collective-permute-start | bytes 1179656 | tf_op jit(solution)/shard_map/ppermute | solution.py:24
  105.7 99.1 %all-gather.6.cloned.1.call-start = ((), (), s32[]{:S(2)}) async-start(), calls=%async_computation.9 | async-start | bytes 1966080 | tf_op jit(solution)/shard_map/all_gather | solution.py:282
  111.3 42.8 %all-to-all-start.2 = ((bf16[16,64,1024]{2,1,0:T(8,128)(2,1)}), bf16[16,64,1024]{2,1,0:T(8,128)(2,1)S(1)}, u32[]{:S(2)}, u32[]{:S(2)}) async-start(bf16[16,64,1024]{2,1,0:T(8,128)(2,1)} %bitcast.65), calls=%async_computation.2 | async-start | bytes 4194304 | tf_op jit(solution)/shard_map/all_to_all | solution.py:278
  127.1 154.2 %reduce-scatter.9.cloned.1.call-start = ((), (), s32[]{:S(2)}) async-start(), calls=%async_computation.13 | async-start | bytes 1966080 | tf_op jit(solution)/shard_map/reduce_scatter | solution.py:285
  154.1 1.3 copy-start.2
  160.1 6.0 %copy-start = (f32[1,256,2304]{2,1,0:T(8,128)S(1)}, f32[1,256,2304]{2,1,0:T(8,128)}, u32[]{:S(2)}) copy-start(f32[1,256,2304]{2,1,0:T(8,128)} %param.12) | copy-start | bytes 7077892
  160.1 33.0 %all-to-all-start.1 = ((bf16[16,64,1024]{2,1,0:T(8,128)(2,1)}), bf16[16,64,1024]{2,1,0:T(8,128)(2,1)}, u32[]{:S(2)}, u32[]{:S(2)}) async-start(bf16[16,64,1024]{2,1,0:T(8,128)(2,1)} %bitcast.64), calls=%async_computation.1 | async-start | bytes 4194304 | tf_op jit(solution)/shard_map/all_to_all | solution.py:278
  166.1 115.3 %reduce-scatter.11.cloned.1.call-start = ((), (), s32[]{:S(2)}) async-start(), calls=%async_computation.14 | async-start | bytes 1966080 | tf_op jit(solution)/shard_map/reduce_scatter | solution.py:285
  166.1 1.7 copy-start.1
  197.9 86.9 %reduce-scatter.7.cloned.1.call-start = ((), (), s32[]{:S(2)}) async-start(), calls=%async_computation.12 | async-start | bytes 3932160 | tf_op jit(solution)/shard_map/reduce_scatter | solution.py:285
  203.7 16.8 %collective-permute-start.7 = (bf16[256,768]{1,0:T(8,128)(2,1)S(1)}, bf16[256,768]{1,0:T(8,128)(2,1)S(1)}, u32[]{:S(2)}, u32[]{:S(2)}) collective-permute-start(bf16[256,768]{1,0:T(8,128)(2,1)S(1)} %slice.77), channel_id=1, source_target_pairs={{0,64},{8,72},{16,80},{24,88},{32,96},{40,104},{48,112},{56,120},{... | collective-permute-start | bytes 1179656 | tf_op jit(solution)/shard_map/ppermute | solution.py:24
  220.6 9.8 %copy-start.5 = (bf16[256,768]{1,0:T(8,128)(2,1)}, bf16[256,768]{1,0:T(8,128)(2,1)S(1)}, u32[]{:S(2)}) copy-start(bf16[256,768]{1,0:T(8,128)(2,1)S(1)} %collective-permute-done.7.mb_ref) | copy-start | bytes 1179652
  220.6 94.7 %reduce-scatter.5.cloned.1.call-start = ((), (), s32[]{:S(2)}) async-start(), calls=%async_computation.11 | async-start | bytes 3932160 | tf_op jit(solution)/shard_map/reduce_scatter | solution.py:285
  220.7 19.7 %collective-permute-start.5 = (bf16[256,1536]{1,0:T(8,128)(2,1)S(1)}, bf16[256,1536]{1,0:T(8,128)(2,1)}, u32[]{:S(2)}, u32[]{:S(2)}) collective-permute-start(bf16[256,1536]{1,0:T(8,128)(2,1)S(1)} %slice.78), channel_id=1, source_target_pairs={{0,64},{8,72},{16,80},{24,88},{32,96},{40,104},{48,112},{56,120},{... | collective-permute-start | bytes 2359304 | tf_op jit(solution)/shard_map/ppermute | solution.py:24
  240.4 26.9 %collective-permute-start.4 = (bf16[256,2304]{1,0:T(8,128)(2,1)S(1)}, bf16[256,2304]{1,0:T(8,128)(2,1)S(1)}, u32[]{:S(2)}, u32[]{:S(2)}) collective-permute-start(bf16[256,2304]{1,0:T(8,128)(2,1)S(1)} %bitcast_convert_fusion), channel_id=1, source_target_pairs={{0,64},{8,72},{16,80},{24,88},{32,96},{40,104},{48,112},{56,120},{... | collective-permute-start | bytes 3538952 | tf_op jit(solution)/shard_map/ppermute | solution.py:24
  267.4 63.3 %all-to-all-start.3 = ((bf16[16,64,2048]{2,1,0:T(8,128)(2,1)}), bf16[16,64,2048]{2,1,0:T(8,128)(2,1)}, u32[]{:S(2)}, u32[]{:S(2)}) async-start(bf16[16,64,2048]{2,1,0:T(8,128)(2,1)} %bitcast.68), calls=%async_computation.3 | async-start | bytes 8388608 | tf_op jit(solution)/shard_map/all_to_all | solution.py:278
  283.3 39.5 %collective-permute-start.9 = (bf16[256,768]{1,0:T(8,128)(2,1)S(1)}, bf16[256,768]{1,0:T(8,128)(2,1)S(1)}, u32[]{:S(2)}, u32[]{:S(2)}) collective-permute-start(bf16[256,768]{1,0:T(8,128)(2,1)S(1)} %get-tuple-element.79), channel_id=1, source_target_pairs={{0,4},{1,5},{2,6},{3,7},{4,0},{5,1},{6,2},{7,3},{8,12},{9,13},{10,... | collective-permute-start | bytes 1179656 | tf_op jit(solution)/shard_map/ppermute | solution.py:24
  286.8 55.1 %collective-permute-start.8 = (bf16[256,768]{1,0:T(8,128)(2,1)S(1)}, bf16[256,768]{1,0:T(8,128)(2,1)S(1)}, u32[]{:S(2)}, u32[]{:S(2)}) collective-permute-start(bf16[256,768]{1,0:T(8,128)(2,1)S(1)} %get-tuple-element.83), channel_id=1, source_target_pairs={{0,4},{1,5},{2,6},{3,7},{4,0},{5,1},{6,2},{7,3},{8,12},{9,13},{10,... | collective-permute-start | bytes 1179656 | tf_op jit(solution)/shard_map/ppermute | solution.py:24
  317.2 33.1 %collective-permute-start.6 = (bf16[256,768]{1,0:T(8,128)(2,1)S(1)}, bf16[256,768]{1,0:T(8,128)(2,1)S(1)}, u32[]{:S(2)}, u32[]{:S(2)}) collective-permute-start(bf16[256,768]{1,0:T(8,128)(2,1)S(1)} %get-tuple-element.85), channel_id=1, source_target_pairs={{0,4},{1,5},{2,6},{3,7},{4,0},{5,1},{6,2},{7,3},{8,12},{9,13},{10,... | collective-permute-start | bytes 1179656 | tf_op jit(solution)/shard_map/ppermute | solution.py:24
  322.7 0.8 copy-start.4
  341.9 0.8 copy-start.7
  350.4 0.8 copy-start.6
Sparse Core Ops, SparseCore 0:
  50.7 69.9 all-gather.3
  122.3 27.2 all-gather.7
  151.3 26.6 all-gather.5
  180.3 25.0 reduce-scatter.8
  208.2 25.4 reduce-scatter.10
  235.9 38.8 reduce-scatter.6
  277.2 38.0 reduce-scatter.4

commit v2 on v1

v2 whole, which is shorter than its diff:
```python
import functools
import jax
import jax.numpy as jnp
from jax import lax
from jax.experimental import pallas as pl
from jax.experimental.pallas import tpu as pltpu
from jax.sharding import PartitionSpec as P

BF = jnp.bfloat16
F32 = jnp.float32
VMEM_LIMIT = 56 * 1024 * 1024
ZN = 4


def params():
    return pltpu.CompilerParams(vmem_limit_bytes=VMEM_LIMIT)


def cost(flops, nbytes):
    return pl.CostEstimate(flops=int(flops), bytes_accessed=int(nbytes), transcendentals=0)


def permuted(value, axis, target):
    return lax.ppermute(value, axis, [(i, target(i)) for i in range(lax.axis_size(axis))])


def mm(a, b, dims):
    return lax.dot_general(a, b, (dims, ((), ())), preferred_element_type=F32)


def columns_of(i, high, width):
    other = high if i < ZN else 1 - high
    return pl.ds(pl.multiple_of(((i % ZN) * 2 + other) * width, width), width)


def dispatch_kernel(high_ref, flat_ref, tok_ref, out_ref):
    tile, features = out_ref.shape
    count = tok_ref.shape[0]
    width = features // (2 * ZN)
    ids = lax.broadcasted_iota(jnp.int32, (tile, count), 0) + pl.program_id(0) * tile
    onehot = (ids == flat_ref[...]).astype(F32).astype(BF)
    for i in range(2 * ZN):
        block = mm(onehot, tok_ref[:, i * width : (i + 1) * width], ((1,), (0,)))
        out_ref[:, columns_of(i, high_ref[0], width)] = block.astype(BF)


def dispatch(high, flat, tok, rows):
    count, features = tok.shape
    tile = min(512, rows)
    return pl.pallas_call(
        dispatch_kernel,
        grid_spec=pltpu.PrefetchScalarGridSpec(
            num_scalar_prefetch=1,
            grid=(rows // tile,),
            in_specs=[
                pl.BlockSpec((1, count), lambda i, high: (0, 0)),
                pl.BlockSpec((count, features), lambda i, high: (0, 0)),
            ],
            out_specs=pl.BlockSpec((tile, features), lambda i, high: (i, 0)),
        ),
        out_shape=jax.ShapeDtypeStruct((rows, features), BF),
        compiler_params=params(),
        cost_estimate=cost(2 * rows * count * features, 2 * features * (rows + count)),
        name="dispatch",
    )(high, flat.reshape(1, count), tok)


def combine_kernel(high_ref, flat_ref, back_ref, out_ref):
    rows, features = back_ref.shape
    width = features // (2 * ZN)
    ids = lax.broadcasted_iota(jnp.int32, (out_ref.shape[0], rows), 1)
    onehot = (ids == flat_ref[...]).astype(F32).astype(BF)
    for i in range(2 * ZN):
        block = mm(onehot, back_ref[:, columns_of(i, high_ref[0], width)], ((1,), (0,)))
        out_ref[:, i * width : (i + 1) * width] = block.astype(BF)


def combine(high, flat, back, count):
    rows, features = back.shape
    tile = min(256, count)
    return pl.pallas_call(
        combine_kernel,
        grid_spec=pltpu.PrefetchScalarGridSpec(
            num_scalar_prefetch=1,
            grid=(count // tile,),
            in_specs=[
                pl.BlockSpec((tile, 1), lambda i, high: (i, 0)),
                pl.BlockSpec((rows, features), lambda i, high: (0, 0)),
            ],
            out_specs=pl.BlockSpec((tile, features), lambda i, high: (i, 0)),
        ),
        out_shape=jax.ShapeDtypeStruct((count, features), BF),
        compiler_params=params(),
        cost_estimate=cost(2 * rows * count * features, 2 * features * (rows + count)),
        name="combine",
    )(high, flat.reshape(count, 1), back)


def forward_kernel(x_ref, gate_ref, up_ref, h_ref, p_ref, s_ref):
    x = x_ref[...]
    g = mm(x, gate_ref[...], ((1,), (0,)))
    u = mm(x, up_ref[...], ((1,), (0,)))
    sig = jax.nn.sigmoid(g)
    s = g * sig
    h_ref[...] = (s * u).astype(BF)
    p_ref[...] = u * sig * (1.0 + g * (1.0 - sig))
    s_ref[...] = s


def forward(x, gate_up):
    rows, features = x.shape
    hidden = gate_up.shape[1] // 2
    tile = min(256, hidden)
    tiles = hidden // tile
    out = pl.BlockSpec((rows, tile), lambda j: (0, j))
    return pl.pallas_call(
        forward_kernel,
        grid=(hidden // tile,),
        in_specs=[
            pl.BlockSpec((rows, features), lambda j: (0, 0)),
            pl.BlockSpec((features, tile), lambda j: (0, j)),
            pl.BlockSpec((features, tile), lambda j: (0, j + tiles)),
        ],
        out_specs=[out, out, out],
        out_shape=[
            jax.ShapeDtypeStruct((rows, hidden), BF),
            jax.ShapeDtypeStruct((rows, hidden), F32),
            jax.ShapeDtypeStruct((rows, hidden), F32),
        ],
        compiler_params=params(),
        cost_estimate=cost(4 * rows * features * hidden, 20e6),
        name="forward",
    )(x, gate_up, gate_up)


def hidden_kernel(z_ref, dy_ref, own_ref, next_ref, last_ref, top_ref, low_ref, p_ref, s_ref, dg_ref, du_ref):
    size = own_ref.shape[0]
    half = size // 2

    def part(away, start, ref):
        block = lax.rem(z_ref[0] + away, ZN)
        columns = pl.ds(pl.multiple_of(block * size + start, half), ref.shape[0])
        return mm(dy_ref[:, columns], ref[...], ((1,), (0,)))

    dh = part(0, 0, own_ref) + part(1, 0, next_ref) + part(ZN - 1, 0, last_ref)
    dh = dh + part(2, 0, top_ref) + part(2, half, low_ref)
    dg_ref[...] = (dh * p_ref[...]).astype(BF)
    du_ref[...] = (dh * s_ref[...]).astype(BF)


def hidden_grads(z, dy, down, p, s):
    rows, features = dy.shape
    hidden = p.shape[1]
    tile = min(256, rows)
    out = pl.BlockSpec((tile, hidden), lambda i, z: (i, 0))
    return pl.pallas_call(
        hidden_kernel,
        grid_spec=pltpu.PrefetchScalarGridSpec(
            num_scalar_prefetch=1,
            grid=(rows // tile,),
            in_specs=[pl.BlockSpec((tile, features), lambda i, z: (i, 0))]
            + [pl.BlockSpec(v.shape, lambda i, z: (0, 0)) for v in down]
            + [out, out],
            out_specs=[out, out],
        ),
        out_shape=[jax.ShapeDtypeStruct((rows, hidden), BF)] * 2,
        compiler_params=params(),
        cost_estimate=cost(2 * rows * features * hidden, 17e6),
        name="hidden_grads",
    )(z, dy, *down, p, s)


def weight_kernel(shift_ref, a_ref, b_ref, out_ref):
    out_ref[...] = mm(a_ref[...], b_ref[...], ((0,), (0,))).astype(BF)


def weight_grad(shift, a, b, name):
    rows, features = a.shape
    hidden = b.shape[1]
    tile = features // ZN
    return pl.pallas_call(
        weight_kernel,
        grid_spec=pltpu.PrefetchScalarGridSpec(
            num_scalar_prefetch=1,
            grid=(ZN,),
            in_specs=[
                pl.BlockSpec((rows, tile), lambda i, shift: (0, (i + shift[0]) % ZN)),
                pl.BlockSpec((rows, hidden), lambda i, shift: (0, 0)),
            ],
            out_specs=pl.BlockSpec((tile, hidden), lambda i, shift: (i, 0)),
        ),
        out_shape=jax.ShapeDtypeStruct((features, hidden), BF),
        compiler_params=params(),
        cost_estimate=cost(2 * rows * features * hidden, 9e6),
        name=name,
    )(shift, a, b)


def input_kernel(dg_ref, du_ref, gate_ref, up_ref, out_ref):
    acc = mm(dg_ref[...], gate_ref[...], ((1,), (1,)))
    acc = acc + mm(du_ref[...], up_ref[...], ((1,), (1,)))
    out_ref[...] = acc.astype(BF)


def input_grad(dg, du, gate_up):
    rows, hidden = dg.shape
    features = gate_up.shape[0]
    tile = 512
    left = pl.BlockSpec((rows, hidden), lambda i: (0, 0))
    gate = pl.BlockSpec((tile, hidden), lambda i: (i, 0))
    up = pl.BlockSpec((tile, hidden), lambda i: (i, 1))
    return pl.pallas_call(
        input_kernel,
        grid=(features // tile,),
        in_specs=[left, left, gate, up],
        out_specs=pl.BlockSpec((rows, tile), lambda i: (0, i)),
        out_shape=jax.ShapeDtypeStruct((rows, features), BF),
        compiler_params=params(),
        cost_estimate=cost(4 * rows * features * hidden, 14e6),
        name="input_grad",
    )(dg, du, gate_up, gate_up)


def adam_kernel(n_sums, keep_ref, *refs):
    w_ref, m_ref, v_ref, wb_ref, mb_ref, vb_ref = refs[n_sums : n_sums + 6]
    nw_ref, nm_ref, nv_ref = refs[-3:]
    keep = keep_ref[0] != 0
    grad = sum(ref[...].astype(F32) for ref in refs[:n_sums])
    w = jnp.where(keep, w_ref[...], wb_ref[...].astype(F32))
    m = jnp.where(keep, m_ref[...], mb_ref[...].astype(F32))
    v = jnp.where(keep, v_ref[...], vb_ref[...].astype(F32))
    m = 0.9 * m + 0.1 * grad
    v = 0.95 * v + 0.05 * grad * grad
    update = m / (1.0 - 0.9**10) / (jnp.sqrt(v / (1.0 - 0.95**10)) + 1e-08)
    nw_ref[...] = w - 0.003 * (update + 0.1 * w)
    nm_ref[...] = m
    nv_ref[...] = v


def adam(keep, sums, state, moved, k, before):
    rows, hidden = sums[0].shape
    tile = min(128, rows)
    chunk = pl.BlockSpec((tile, hidden), lambda i, keep: (i, 0))
    column = pl.BlockSpec((tile, hidden), lambda i, keep: (i, k))
    shape = jax.ShapeDtypeStruct(state[0].shape, F32)

    def at(block):
        return pl.BlockSpec((tile, hidden), lambda i, keep: (i, block))

    return pl.pallas_call(
        functools.partial(adam_kernel, len(sums)),
        grid_spec=pltpu.PrefetchScalarGridSpec(
            num_scalar_prefetch=1,
            grid=(rows // tile,),
            in_specs=[chunk] * len(sums)
            + [column] * 3
            + [at(block) for _, block in moved]
            + [pl.BlockSpec(memory_space=pl.ANY)] * len(before),
            out_specs=[column] * 3,
        ),
        out_shape=[shape] * 3,
        input_output_aliases={len(sums) + 7 + i: i for i in range(len(before))},
        compiler_params=params(),
        cost_estimate=cost(20 * rows * hidden, 34 * rows * hidden),
        name="adam",
    )(keep, *sums, *state, *[v for v, _ in moved], *before)


def per_device(tokens, cotangent, routes, owner, master, moment1, moment2):
    experts = lax.axis_size("expert")
    half = experts // 2
    position = lax.axis_index("expert")
    high = (lax.axis_index("dp") // ZN).astype(jnp.int32).reshape(1)
    keep = owner[position] == position
    info = keep.astype(jnp.int32).reshape(1)
    hidden = master.shape[2] // 3
    features = tokens.shape[2]
    count = tokens.shape[1]
    capacity = 2 * count // experts
    rows = experts * capacity
    replicas = lax.axis_size("dp")
    z_groups = [[h * ZN + z for z in range(ZN)] for h in range(replicas // ZN)]

    route_ids = routes[0, :, 0]
    columns = jnp.arange(experts, dtype=jnp.int32)
    onehot = (route_ids[:, None] == columns[None, :]).astype(jnp.int32)
    slot = jnp.sum((jnp.cumsum(onehot, axis=0) - 1) * onehot, axis=1)
    flat = route_ids * capacity + slot
    send_x = dispatch(high, flat, tokens[0], rows)
    send_dy = dispatch(high, flat, cotangent[0], rows)

    def over_owners(value):
        return permuted(value, "expert", lambda i: i ^ half)

    def over_high(value):
        return permuted(value, "dp", lambda i: i ^ ZN)

    def over_experts(value):
        boxes = value.reshape(experts, capacity, value.shape[1])
        out = lax.all_to_all(boxes, "expert", split_axis=0, concat_axis=0, tiled=True)
        return out.reshape(value.shape)

    def gathered(value):
        return lax.all_gather(value, "dp", axis=0, tiled=True, axis_index_groups=z_groups)

    def scattered(grad):
        return lax.psum_scatter(
            grad, "dp", scatter_dimension=0, tiled=True, axis_index_groups=z_groups
        )

    def to_next(value):
        return permuted(value, "dp", lambda i: i // ZN * ZN + (i + 1) % ZN)

    def to_last(value):
        return permuted(value, "dp", lambda i: i // ZN * ZN + (i - 1) % ZN)

    z = (lax.axis_index("dp") % ZN).astype(jnp.int32).reshape(1)
    nought = jnp.zeros((1,), jnp.int32)

    split = 2 * hidden
    own_a, own_b = master[0, :, :split].astype(BF), master[0, :, split:].astype(BF)
    other_a = over_owners(own_a)
    own_b, other_a = lax.optimization_barrier((own_b, other_a))
    other_b = over_owners(own_b)
    placed_a = lax.optimization_barrier(jnp.where(keep, own_a, other_a))
    far_a = over_high(placed_a)
    placed_a, far_a, other_b, send_x = lax.optimization_barrier((placed_a, far_a, other_b, send_x))
    gate_up = gathered(jnp.concatenate([placed_a, far_a], axis=0))
    x = over_experts(send_x)
    placed_b = jnp.where(keep, own_b, other_b)
    far_b = over_high(placed_b)
    down_own = jnp.concatenate([placed_b, far_b], axis=0)
    send_dy, x, down_own = lax.optimization_barrier((send_dy, x, down_own))
    dy = over_experts(send_dy)
    down_last, down_next = to_next(down_own), to_last(down_own)
    h, p, s = forward(x, gate_up)
    down_last, down_next, h = lax.optimization_barrier((down_last, down_next, h))
    quarter = down_own.shape[0] // 2
    down = (down_own, down_next, down_last, to_next(down_last[:quarter]), to_last(down_next[quarter:]))

    def ring_first(grad):
        return to_next(grad[2, 0]), to_last(grad[2, 1])

    def ring_second(grad, top, low):
        top = (grad[1, 0].astype(F32) + top.astype(F32)).astype(BF)
        low = (grad[ZN - 1, 1].astype(F32) + low.astype(F32)).astype(BF)
        return to_next(jnp.stack([top, grad[1, 1]])), to_last(jnp.stack([grad[ZN - 1, 0], low]))

    def ring_sum(grad, ahead, behind):
        part = grad[0].astype(F32) + ahead.astype(F32) + behind.astype(F32)
        return part.astype(BF)

    def blocks(grad):
        return grad.reshape(ZN, 2, -1, hidden)

    together = lax.optimization_barrier

    m_all, v_all = moment1[0].astype(BF), moment2[0].astype(BF)
    m_own = jnp.concatenate([m_all[:, :hidden], m_all[:, split:]], axis=1)
    v_own = [v_all[:, split:], v_all[:, :hidden]]
    v_own.append(jnp.concatenate([m_all[:, hidden:split], v_all[:, hidden:split]], axis=1))
    dy, m_own, *others = together((dy, m_own, *v_own, *down[3:]))
    v_own, down = others[:3], (*down[:3], *others[3:])
    part_down = scattered(weight_grad(nought, dy, h, "grad_down")).reshape(2, -1, hidden)
    m_other = over_owners(m_own)
    dg, du = hidden_grads(z, dy, down, p, s)
    send_back = input_grad(dg, du, gate_up)
    send_back, m_other, dg, du = together((send_back, m_other, dg, du))
    returned = over_experts(send_back)

    gate = blocks(weight_grad(z, x, dg, "grad_gate"))
    gate, du = together((gate, du))
    first = ring_first(gate)
    up = blocks(weight_grad(z, x, du, "grad_up"))
    first, up, *v_own = together((first, up, *v_own))
    second = ring_second(gate, *first)
    first = ring_first(up)
    first, second, part_down = together((first, second, part_down))
    part_gate = ring_sum(gate, *second)
    far_gate, far_down = over_high(part_gate[1]), over_high(part_down[1])
    v_other = [over_owners(v) for v in v_own]
    second = ring_second(up, *first)
    second, v_other[0] = together((second, v_other[0]))
    part_up = ring_sum(up, *second)
    far_up = over_high(part_up[1])
    token_grad = combine(high, flat, returned, count)

    state = (master[0], moment1[0], moment2[0])
    steps = (
        (2, part_down[0], far_down, ((other_b, 0), (m_other, 1), (v_other[0], 0))),
        (0, part_gate[0], far_gate, ((other_a, 0), (m_other, 0), (v_other[1], 0))),
        (1, part_up[0], far_up, ((other_a, 1), (v_other[2], 0), (v_other[2], 1))),
    )
    new = ()
    for k, near, far, moved in steps:
        new = adam(info, (near, far), state, moved, k, new)
    return (token_grad[None], new[0][None], new[1][None], new[2][None])


def solution(mesh):
    placed = (
        P("dp", "expert", None),
        P("dp", "expert", None),
        P("dp", "expert", None),
        P(),
        P("expert", "dp", None),
        P("expert", "dp", None),
        P("expert", "dp", None),
    )
    return jax.shard_map(
        per_device,
        mesh=mesh,
        in_specs=placed,
        out_specs=(
            P("dp", "expert", None),
            P("expert", "dp", None),
            P("expert", "dp", None),
            P("expert", "dp", None),
        ),
        check_vma=False,
    )
```

time: 366 us -> 332 us (0.907)
  waiting for transfers between devices: 160 us -> 134 us
  Pallas kernels: 100 us -> 82.8 us
  starting transfers between devices: 63.5 us -> 73 us
    reduce_scatter x4 -> x1, waiting for transfers between devices: 27.1 us -> 0.01 us  [scattered(): lax.psum_scatter(grad, 'dp', scatter_dimension=0, tiled=True, axis_index_...]
    ppermute x10 -> x23, starting transfers between devices: 23.6 us -> 44.6 us  [permuted(): lax.ppermute(value, axis, [(i, target(i)) for i in range(lax.axis_size(ax...]
    pallas_call x13 -> x10, Pallas kernels: 77.2 us -> 59.9 us  [the longest x3 22.5 us: weight_grad(): pl.pallas_call(weight_kernel, grid_spec=pltpu.PrefetchScalarGridSpec(num_...]
    all_to_all x4 -> x3, starting transfers between devices: 39.6 us -> 28.3 us  [over_experts(): lax.all_to_all(boxes, 'expert', split_axis=0, concat_axis=0, tiled=True)]
    ppermute x10 -> x23, waiting for transfers between devices: 94.6 us -> 104 us  [permuted(): lax.ppermute(value, axis, [(i, target(i)) for i in range(lax.axis_size(ax...]
    all_to_all x4 -> x3, waiting for transfers between devices: 37.9 us -> 29.1 us  [over_experts(): lax.all_to_all(boxes, 'expert', split_axis=0, concat_axis=0, tiled=True)]
    select_n x6 -> x1, other arithmetic: 7.06 us -> 0.08 us  [per_device(): placed_a = lax.optimization_barrier(jnp.where(keep, own_a, other_a))]
  transfers between devices with their start and end apart: 21 -> 28, of which waited for: 13 -> 14; matrix products, arithmetic and copies ran while one was open for 4% -> 5% of each run, Pallas kernels for 26% -> 22%
where the time goes in v2:
time: 332 us; the launch traced here: 329 us
  waiting for transfers between devices  134 us (40%)
  Pallas kernels  82.8 us (25%)
  starting transfers between devices  73 us (22%)
  between operations  15 us (5%)
  local copies, waits for them, and re-layouts  12.7 us (4%)
  other arithmetic  11.7 us (4%)
    ppermute x23, waiting for transfers between devices, permuted(): lax.ppermute(value, axis, [(i, target(i)) for i in range(lax.axis_size(ax...  104 us
    ppermute x23, starting transfers between devices, permuted(): lax.ppermute(value, axis, [(i, target(i)) for i in range(lax.axis_size(ax...  44.6 us
    all_to_all x3, waiting for transfers between devices, over_experts(): lax.all_to_all(boxes, 'expert', split_axis=0, concat_axis=0, tiled=True)  29.1 us
    all_to_all x3, starting transfers between devices, over_experts(): lax.all_to_all(boxes, 'expert', split_axis=0, concat_axis=0, tiled=True)  28.3 us
    pallas_call x3, Pallas kernels, weight_grad(): pl.pallas_call(weight_kernel, grid_spec=pltpu.PrefetchScalarGridSpec(num_...  22.5 us
    pallas_call x1, Pallas kernels, forward(): pl.pallas_call(forward_kernel, grid=(hidden // tile,), in_specs=[pl.Block...  12.2 us
    pallas_call x2, Pallas kernels, dispatch(): pl.pallas_call(dispatch_kernel, grid_spec=pltpu.PrefetchScalarGridSpec(nu...  11.6 us
    pallas_call x3, Pallas kernels, adam(): pl.pallas_call(functools.partial(adam_kernel, len(sums)), grid_spec=pltpu...  10.9 us
  transfers between devices with their start and end apart: 28, of which 14 were waited for; matrix products, arithmetic and copies ran while one was open for 5% of the time, Pallas kernels for 22%

profile of v2, /device:TPU:1, one launch (start us, length us, event | category | flops | bytes accessed | tf_op | source)
XLA Modules:
  0.0 328.8 jit_solution(3886612316104996914)
XLA Ops:
  7.2 1.8 convert.11
  9.1 3.7 %collective-permute-start = (bf16[256,1536]{1,0:T(8,128)(2,1)S(1)}, bf16[256,1536]{1,0:T(8,128)(2,1)S(1)}, u32[]{:S(2)}, u32[]{:S(2)}) collective-permute-start(bf16[256,1536]{1,0:T(8,128)(2,1)S(1)} %slice_bitcast_fusion), channel_id=1, source_target_pairs={{0,64},{8,72},{16,80},{24,88},{32,96},{40,104},{48,112},{56,120},{... | collective-permute-start | bytes 2359304 | tf_op jit(solution)/shard_map/ppermute | solution.py:24
  14.0 15.5 %collective-permute-done.refs_5_ = bf16[256,1536]{1,0:T(8,128)(2,1)S(1)} collective-permute-done((bf16[256,1536]{1,0:T(8,128)(2,1)S(1)}, bf16[256,1536]{1,0:T(8,128)(2,1)S(1)}, u32[]{:S(2)}, u32[]{:S(2)}) %collective-permute-start) | collective-permute-done | bytes 786464 | tf_op jit(solution)/shard_map/ppermute | solution.py:24
  29.6 3.4 %collective-permute-start.1 = (bf16[256,1536]{1,0:T(8,128)(2,1)S(1)}, bf16[256,1536]{1,0:T(8,128)(2,1)S(1)}, u32[]{:S(2)}, u32[]{:S(2)}) collective-permute-start(bf16[256,1536]{1,0:T(8,128)(2,1)S(1)} %broadcast_select_fusion), channel_id=1, source_target_pairs={{0,4},{1,5},{2,6},{3,7},{4,0},{5,1},{6,2},{7,3},{8,12},{9,13},{10,... | collective-permute-start | bytes 2359304 | tf_op jit(solution)/shard_map/ppermute | solution.py:24
  34.5 2.8 collective-permute-start.2
  37.9 5.8 %dispatch.3 = bf16[1024,2048]{1,0:T(8,128)(2,1)} custom-call(s32[1]{0:T(128)} %bitcast.high_ref, s32[1,512]{1,0:T(1,128)} %bitcast_add_fusion.flat_ref, bf16[512,2048]{1,0:T(8,128)(2,1)} %bitcast.133), custom_call_target="tpu_custom_call" | custom-call | flops 2147483648 | bytes 6291456 | tf_op jit(solution)/shard_map/dispatch/pallas_call | solution.py:50
  44.9 4.3 %collective-permute-done.1 = bf16[256,1536]{1,0:T(8,128)(2,1)S(1)} collective-permute-done((bf16[256,1536]{1,0:T(8,128)(2,1)S(1)}, bf16[256,1536]{1,0:T(8,128)(2,1)S(1)}, u32[]{:S(2)}, u32[]{:S(2)}) %collective-permute-start.1) | collective-permute-done | bytes 786464 | tf_op jit(solution)/shard_map/ppermute | solution.py:24
  49.2 1.2 pad_maximum_fusion
  50.5 7.7 %all-to-all-start = ((bf16[16,64,2048]{2,1,0:T(8,128)(2,1)}), bf16[16,64,2048]{2,1,0:T(8,128)(2,1)}, u32[]{:S(2)}, u32[]{:S(2)}) async-start(bf16[16,64,2048]{2,1,0:T(8,128)(2,1)} %bitcast.121), calls=%async_computation | async-start | bytes 8388608 | tf_op jit(solution)/shard_map/all_to_all | solution.py:300
  58.2 2.7 collective-permute-start.3
  60.9 5.8 %dispatch.2 = bf16[1024,2048]{1,0:T(8,128)(2,1)} custom-call(s32[1]{0:T(128)} %bitcast.high_ref, s32[1,512]{1,0:T(1,128)} %bitcast_add_fusion.flat_ref, bf16[512,2048]{1,0:T(8,128)(2,1)} %bitcast.134), custom_call_target="tpu_custom_call" | custom-call | flops 2147483648 | bytes 6291456 | tf_op jit(solution)/shard_map/dispatch/pallas_call | solution.py:50
  66.7 37.8 %collective-permute-done.3 = bf16[256,768]{1,0:T(8,128)(2,1)S(1)} collective-permute-done((bf16[256,768]{1,0:T(8,128)(2,1)S(1)}, bf16[256,768]{1,0:T(8,128)(2,1)S(1)}, u32[]{:S(2)}, u32[]{:S(2)}) %collective-permute-start.3) | collective-permute-done | bytes 393248 | tf_op jit(solution)/shard_map/ppermute | solution.py:24
  104.6 6.5 %all-to-all-done = bf16[16,64,2048]{2,1,0:T(8,128)(2,1)} async-done(((bf16[16,64,2048]{2,1,0:T(8,128)(2,1)}), bf16[16,64,2048]{2,1,0:T(8,128)(2,1)}, u32[]{:S(2)}, u32[]{:S(2)}) %all-to-all-start) | async-done | bytes 4194336 | tf_op jit(solution)/shard_map/all_to_all | solution.py:300
  111.2 11.7 %all-to-all-start.1 = ((bf16[16,64,2048]{2,1,0:T(8,128)(2,1)}), bf16[16,64,2048]{2,1,0:T(8,128)(2,1)}, u32[]{:S(2)}, u32[]{:S(2)}) async-start(bf16[16,64,2048]{2,1,0:T(8,128)(2,1)} %bitcast.120), calls=%async_computation.1 | async-start | bytes 8388608 | tf_op jit(solution)/shard_map/all_to_all | solution.py:300
  123.1 1.5 copy-done.1
  124.7 1.5 collective-permute-start.4
  126.2 2.4 collective-permute-start.5
  129.5 12.2 %forward.1 = (bf16[1024,768]{1,0:T(8,128)(2,1)}, f32[1024,768]{1,0:T(8,128)}, f32[1024,768]{1,0:T(8,128)}) custom-call(bf16[1024,2048]{1,0:T(8,128)(2,1)} %bitcast.15.x_ref.a_ref, bf16[2048,1536]{1,0:T(8,128)(2,1)} %all-gather.2.cloned.1.call-done.gate_ref.up_ref, bf16[2048,1536]{1,0:T(8,128)(2,1)} %all-gather.2.cloned.1.call-done.gate_ref.up_ref), custom_call_target="tpu_custom_call" | custom-call | flops 6442450944 | bytes 20000000 | tf_op jit(solution)/shard_map/forward/pallas_call | solution.py:116
  141.6 4.8 %collective-permute-done.4.last_ref = bf16[512,768]{1,0:T(8,128)(2,1)S(1)} collective-permute-done((bf16[512,768]{1,0:T(8,128)(2,1)S(1)}, bf16[512,768]{1,0:T(8,128)(2,1)S(1)}, u32[]{:S(2)}, u32[]{:S(2)}) %collective-permute-start.4) | collective-permute-done | bytes 786464 | tf_op jit(solution)/shard_map/ppermute | solution.py:24
  146.9 1.8 slice.109
  148.7 2.3 collective-permute-start.7
  153.0 22.6 %all-to-all-done.1 = bf16[16,64,2048]{2,1,0:T(8,128)(2,1)} async-done(((bf16[16,64,2048]{2,1,0:T(8,128)(2,1)}), bf16[16,64,2048]{2,1,0:T(8,128)(2,1)}, u32[]{:S(2)}, u32[]{:S(2)}) %all-to-all-start.1) | async-done | bytes 4194336 | tf_op jit(solution)/shard_map/all_to_all | solution.py:300
  175.6 7.4 %grad_down.1 = bf16[2048,768]{1,0:T(8,128)(2,1)} custom-call(s32[1]{0:T(128)} %constant.47.clone.1.shift_ref, bf16[1024,2048]{1,0:T(8,128)(2,1)} %bitcast.17.dy_ref.a_ref, bf16[1024,768]{1,0:T(8,128)(2,1)} %get-tuple-element.88.b_ref), custom_call_target="tpu_custom_call" | custom-call | flops 3221225472 | bytes 9000000 | tf_op jit(solution)/shard_map/grad_down/pallas_call | solution.py:181
  183.0 4.5 %collective-permute-start.8 = (bf16[256,1536]{1,0:T(8,128)(2,1)S(1)}, bf16[256,1536]{1,0:T(8,128)(2,1)S(1)}, u32[]{:S(2)}, u32[]{:S(2)}) collective-permute-start(bf16[256,1536]{1,0:T(8,128)(2,1)S(1)} %get-tuple-element.76), channel_id=1, source_target_pairs={{0,64},{8,72},{16,80},{24,88},{32,96},{40,104},{48,112},{56,120},{... | collective-permute-start | bytes 2359304 | tf_op jit(solution)/shard_map/ppermute | solution.py:24
  187.5 9.0 %hidden_grads.1 = (bf16[1024,768]{1,0:T(8,128)(2,1)}, bf16[1024,768]{1,0:T(8,128)(2,1)}) custom-call(s32[1]{0:T(128)} %bitcast.6.z_ref.shift_ref, bf16[1024,2048]{1,0:T(8,128)(2,1)} %bitcast.17.dy_ref.a_ref, bf16[512,768]{1,0:T(8,128)(2,1)} %copy-done.7, bf16[512,768]{1,0:T(8,128)(2,1)} %collective-permute-done.5.next_ref, bf16[512,768]{1,0:T(8,128)(2,1)} %copy-done.8, ...), custom_call_target="tpu_custom_call" | custom-call | flops 3221225472 | bytes 17000000 | tf_op jit(solution)/shard_map/hidden_grads/pallas_call | solution.py:156
  196.5 10.7 %input_grad.1 = bf16[1024,2048]{1,0:T(8,128)(2,1)} custom-call(bf16[1024,768]{1,0:T(8,128)(2,1)} %get-tuple-element.78.dg_ref.b_ref, bf16[1024,768]{1,0:T(8,128)(2,1)} %get-tuple-element.81.du_ref.b_ref, bf16[2048,1536]{1,0:T(8,128)(2,1)} %all-gather.2.cloned.1.call-done.gate_ref.up_ref, bf16[2048,1536]{1,0:T(8,128)(2,1)} %all-gather.2.cloned.1.call-done.gate_ref.up_ref), custom_call_target="tpu_custom_call" | custom-call | flops 6442450944 | bytes 14000000 | tf_op jit(solution)/shard_map/input_grad/pallas_call | solution.py:212
  207.3 7.7 %grad_gate.1 = bf16[2048,768]{1,0:T(8,128)(2,1)} custom-call(s32[1]{0:T(128)} %bitcast.6.z_ref.shift_ref, bf16[1024,2048]{1,0:T(8,128)(2,1)} %bitcast.15.x_ref.a_ref, bf16[1024,768]{1,0:T(8,128)(2,1)} %get-tuple-element.78.dg_ref.b_ref), custom_call_target="tpu_custom_call" | custom-call | flops 3221225472 | bytes 9000000 | tf_op jit(solution)/shard_map/grad_gate/pallas_call | solution.py:181
  215.0 8.9 %all-to-all-start.2 = ((bf16[16,64,2048]{2,1,0:T(8,128)(2,1)}), bf16[16,64,2048]{2,1,0:T(8,128)(2,1)}, u32[]{:S(2)}, u32[]{:S(2)}) async-start(bf16[16,64,2048]{2,1,0:T(8,128)(2,1)} %bitcast.119), calls=%async_computation.2 | async-start | bytes 8388608 | tf_op jit(solution)/shard_map/all_to_all | solution.py:300
  224.0 3.8 %collective-permute-start.10 = (bf16[256,768]{1,0:T(8,128)(2,1)S(1)}, bf16[256,768]{1,0:T(8,128)(2,1)S(1)}, u32[]{:S(2)}, u32[]{:S(2)}) collective-permute-start(bf16[256,768]{1,0:T(8,128)(2,1)S(1)} %get-tuple-element.118), channel_id=1, source_target_pairs={{0,3},{1,0},{2,1},{3,2},{4,7},{5,4},{6,5},{7,6},{8,11},{9,8},{10,9... | collective-permute-start | bytes 1179656 | tf_op jit(solution)/shard_map/ppermute | solution.py:24
  227.8 7.4 %grad_up.1 = bf16[2048,768]{1,0:T(8,128)(2,1)} custom-call(s32[1]{0:T(128)} %bitcast.6.z_ref.shift_ref, bf16[1024,2048]{1,0:T(8,128)(2,1)} %bitcast.15.x_ref.a_ref, bf16[1024,768]{1,0:T(8,128)(2,1)} %get-tuple-element.81.du_ref.b_ref), custom_call_target="tpu_custom_call" | custom-call | flops 3221225472 | bytes 9000000 | tf_op jit(solution)/shard_map/grad_up/pallas_call | solution.py:181
  236.2 3.2 collective-permute-done.9
  242.3 2.7 collective-permute-start.12
  245.0 2.6 collective-permute-start.17
  247.6 20.2 %collective-permute-done.11 = bf16[256,768]{1,0:T(8,128)(2,1)S(1)} collective-permute-done((bf16[256,768]{1,0:T(8,128)(2,1)}, bf16[256,768]{1,0:T(8,128)(2,1)S(1)}, u32[]{:S(2)}, u32[]{:S(2)}) %collective-permute-start.11) | collective-permute-done | bytes 393248 | tf_op jit(solution)/shard_map/ppermute | solution.py:24
  267.8 2.4 collective-permute-start.21
  270.9 1.5 fusion.11
  272.7 1.5 collective-permute-start.15
  274.3 1.9 fusion.1
  277.8 12.2 %collective-permute-done.17.refs_7_ = bf16[256,768]{1,0:T(8,128)(2,1)S(1)} collective-permute-done((bf16[256,768]{1,0:T(8,128)(2,1)}, bf16[256,768]{1,0:T(8,128)(2,1)S(1)}, u32[]{:S(2)}, u32[]{:S(2)}) %collective-permute-start.17) | collective-permute-done | bytes 393248 | tf_op jit(solution)/shard_map/ppermute | solution.py:24
  289.9 2.6 collective-permute-start.22
  292.9 1.4 fusion.3
  295.1 2.6 collective-permute-start.18
  298.6 5.9 %combine.1 = bf16[512,2048]{1,0:T(8,128)(2,1)} custom-call(s32[1]{0:T(128)} %bitcast.high_ref, s32[512,1]{1,0:T(8,128)} %copy.21.flat_ref, bf16[1024,2048]{1,0:T(8,128)(2,1)} %bitcast.21.back_ref), custom_call_target="tpu_custom_call" | custom-call | flops 2147483648 | bytes 6291456 | tf_op jit(solution)/shard_map/combine/pallas_call | solution.py:81
  305.3 3.6 %adam.3 = (f32[256,2304]{1,0:T(8,128)}, f32[256,2304]{1,0:T(8,128)}, f32[256,2304]{1,0:T(8,128)}) custom-call(s32[1]{0:T(128)} %bitcast.23.keep_ref, bf16[256,768]{1,0:T(8,128)(2,1)} %get-tuple-element.129.refs_0_, bf16[256,768]{1,0:T(8,128)(2,1)} %copy-done.13, f32[256,2304]{1,0:T(8,128)} %bitcast.107, f32[256,2304]{1,0:T(8,128)} %bitcast.110, ...), custom_call_target="tpu_custom_call" | custom-call | flops 3932160 | bytes 6684672 | tf_op jit(solution)/shard_map/adam/pallas_call | solution.py:250
  309.9 3.6 %adam.4 = (f32[256,2304]{1,0:T(8,128)}, f32[256,2304]{1,0:T(8,128)}, f32[256,2304]{1,0:T(8,128)}) custom-call(s32[1]{0:T(128)} %bitcast.23.keep_ref, bf16[256,768]{1,0:T(8,128)(2,1)} %get-tuple-element.131.refs_0_, bf16[256,768]{1,0:T(8,128)(2,1)} %copy-done.16, f32[256,2304]{1,0:T(8,128)} %bitcast.108, ...), custom_call_target="tpu_custom_call", output_to_operand_aliasing={{0}: (9, {}), {1}: (10, {}), {2}: (11, {})} | custom-call | flops 3932160 | bytes 6684672 | tf_op jit(solution)/shard_map/adam/pallas_call | solution.py:250
  313.5 1.7 collective-permute-done.19.refs_6_.refs_7_
  315.2 2.3 collective-permute-done.18.refs_1_
  318.3 3.6 %adam.5 = (f32[256,2304]{1,0:T(8,128)}, f32[256,2304]{1,0:T(8,128)}, f32[256,2304]{1,0:T(8,128)}) custom-call(s32[1]{0:T(128)} %bitcast.23.keep_ref, bf16[256,768]{1,0:T(8,128)(2,1)} %get-tuple-element.133.refs_0_, bf16[256,768]{1,0:T(8,128)(2,1)} %copy-done.15, f32[256,2304]{1,0:T(8,128)} %bitcast.109, ...), custom_call_target="tpu_custom_call", output_to_operand_aliasing={{0}: (9, {}), {1}: (10, {}), {2}: (11, {})} | custom-call | flops 3932160 | bytes 6684672 | tf_op jit(solution)/shard_map/adam/pallas_call | solution.py:250
  (97 shorter events, 19.0 us)
Async XLA Ops:
  7.2 5.6 %copy-start.18 = (s32[16]{0:T(128)S(1)}, s32[16]{0:T(128)}, u32[]{:S(2)}) copy-start(s32[16]{0:T(128)} %param.10) | copy-start | bytes 196
  7.2 122.3 %all-gather.2.cloned.1.call-start = ((), (), s32[]{:S(2)}) async-start(), calls=%async_computation.4 | async-start | bytes 7864320 | tf_op jit(solution)/shard_map/all_gather | solution.py:304
  9.0 24.0 %copy-start.17 = (s32[1,512,1]{1,2,0:T(1,128)S(1)}, s32[1,512,1]{1,2,0:T(1,128)}, u32[]{:S(2)}) copy-start(s32[1,512,1]{1,2,0:T(1,128)} %param.9) | copy-start | bytes 6148
  9.1 20.4 %collective-permute-start = (bf16[256,1536]{1,0:T(8,128)(2,1)S(1)}, bf16[256,1536]{1,0:T(8,128)(2,1)S(1)}, u32[]{:S(2)}, u32[]{:S(2)}) collective-permute-start(bf16[256,1536]{1,0:T(8,128)(2,1)S(1)} %slice_bitcast_fusion), channel_id=1, source_target_pairs={{0,64},{8,72},{16,80},{24,88},{32,96},{40,104},{48,112},{56,120},{... | collective-permute-start | bytes 2359304 | tf_op jit(solution)/shard_map/ppermute | solution.py:24
  29.5 14.2 %copy-start.2 = (bf16[256,1536]{1,0:T(8,128)(2,1)}, bf16[256,1536]{1,0:T(8,128)(2,1)S(1)}, u32[]{:S(2)}) copy-start(bf16[256,1536]{1,0:T(8,128)(2,1)S(1)} %collective-permute-done.refs_5_) | copy-start | bytes 2359300
  29.6 19.6 %collective-permute-start.1 = (bf16[256,1536]{1,0:T(8,128)(2,1)S(1)}, bf16[256,1536]{1,0:T(8,128)(2,1)S(1)}, u32[]{:S(2)}, u32[]{:S(2)}) collective-permute-start(bf16[256,1536]{1,0:T(8,128)(2,1)S(1)} %broadcast_select_fusion), channel_id=1, source_target_pairs={{0,4},{1,5},{2,6},{3,7},{4,0},{5,1},{6,2},{7,3},{8,12},{9,13},{10,... | collective-permute-start | bytes 2359304 | tf_op jit(solution)/shard_map/ppermute | solution.py:24
  34.5 10.4 %collective-permute-start.2 = (bf16[256,768]{1,0:T(8,128)(2,1)S(1)}, bf16[256,768]{1,0:T(8,128)(2,1)S(1)}, u32[]{:S(2)}, u32[]{:S(2)}) collective-permute-start(bf16[256,768]{1,0:T(8,128)(2,1)S(1)} %slice_bitcast_fusion.5), channel_id=1, source_target_pairs={{0,64},{8,72},{16,80},{24,88},{32,96},{40,104},{48,112},{56,120},{... | collective-permute-start | bytes 1179656 | tf_op jit(solution)/shard_map/ppermute | solution.py:24
  44.9 13.3 %copy-start.9 = (bf16[256,768]{1,0:T(8,128)(2,1)}, bf16[256,768]{1,0:T(8,128)(2,1)S(1)}, u32[]{:S(2)}) copy-start(bf16[256,768]{1,0:T(8,128)(2,1)S(1)} %collective-permute-done.2.refs_5_) | copy-start | bytes 1179652
  50.5 60.7 %all-to-all-start = ((bf16[16,64,2048]{2,1,0:T(8,128)(2,1)}), bf16[16,64,2048]{2,1,0:T(8,128)(2,1)}, u32[]{:S(2)}, u32[]{:S(2)}) async-start(bf16[16,64,2048]{2,1,0:T(8,128)(2,1)} %bitcast.121), calls=%async_computation | async-start | bytes 8388608 | tf_op jit(solution)/shard_map/all_to_all | solution.py:300
  58.2 46.4 %collective-permute-start.3 = (bf16[256,768]{1,0:T(8,128)(2,1)S(1)}, bf16[256,768]{1,0:T(8,128)(2,1)S(1)}, u32[]{:S(2)}, u32[]{:S(2)}) collective-permute-start(bf16[256,768]{1,0:T(8,128)(2,1)S(1)} %broadcast_select_fusion.1), channel_id=1, source_target_pairs={{0,4},{1,5},{2,6},{3,7},{4,0},{5,1},{6,2},{7,3},{8,12},{9,13},{10,... | collective-permute-start | bytes 1179656 | tf_op jit(solution)/shard_map/ppermute | solution.py:24
  104.6 21.6 %copy-start.7 = (bf16[512,768]{1,0:T(8,128)(2,1)}, bf16[512,768]{1,0:T(8,128)(2,1)S(1)}, u32[]{:S(2)}) copy-start(bf16[512,768]{1,0:T(8,128)(2,1)S(1)} %pad_maximum_fusion.1.own_ref) | copy-start | bytes 2359300
  111.2 11.7 %copy-start = (f32[1,256,2304]{2,1,0:T(8,128)S(1)}, f32[1,256,2304]{2,1,0:T(8,128)}, u32[]{:S(2)}) copy-start(f32[1,256,2304]{2,1,0:T(8,128)} %param.12) | copy-start | bytes 7077892
  111.2 64.4 %all-to-all-start.1 = ((bf16[16,64,2048]{2,1,0:T(8,128)(2,1)}), bf16[16,64,2048]{2,1,0:T(8,128)(2,1)}, u32[]{:S(2)}, u32[]{:S(2)}) async-start(bf16[16,64,2048]{2,1,0:T(8,128)(2,1)} %bitcast.120), calls=%async_computation.1 | async-start | bytes 8388608 | tf_op jit(solution)/shard_map/all_to_all | solution.py:300
  122.9 148.1 %reduce-scatter.2.cloned.1.call-start = ((), (), s32[]{:S(2)}) async-start(), calls=%async_computation.5 | async-start | bytes 3932160 | tf_op jit(solution)/shard_map/reduce_scatter | solution.py:307
  122.9 1.7 copy-start.1
  124.7 21.7 %collective-permute-start.4 = (bf16[512,768]{1,0:T(8,128)(2,1)S(1)}, bf16[512,768]{1,0:T(8,128)(2,1)S(1)}, u32[]{:S(2)}, u32[]{:S(2)}) collective-permute-start(bf16[512,768]{1,0:T(8,128)(2,1)S(1)} %pad_maximum_fusion.1.own_ref), channel_id=1, source_target_pairs={{0,1},{1,2},{2,3},{3,0},{4,5},{5,6},{6,7},{7,4},{8,9},{9,10},{10,1... | collective-permute-start | bytes 2359304 | tf_op jit(solution)/shard_map/ppermute | solution.py:24
  126.2 20.2 %collective-permute-start.5 = (bf16[512,768]{1,0:T(8,128)(2,1)S(1)}, bf16[512,768]{1,0:T(8,128)(2,1)}, u32[]{:S(2)}, u32[]{:S(2)}) collective-permute-start(bf16[512,768]{1,0:T(8,128)(2,1)S(1)} %pad_maximum_fusion.1.own_ref), channel_id=1, source_target_pairs={{0,3},{1,0},{2,1},{3,2},{4,7},{5,4},{6,5},{7,6},{8,11},{9,8},{10,9... | collective-permute-start | bytes 2359304 | tf_op jit(solution)/shard_map/ppermute | solution.py:24
  141.6 10.3 %copy-start.10 = (bf16[256,768]{1,0:T(8,128)(2,1)S(1)}, bf16[256,768]{1,0:T(8,128)(2,1)}, u32[]{:S(2)}) copy-start(bf16[256,768]{1,0:T(8,128)(2,1)} %get-tuple-element.124) | copy-start | bytes 1179652
  146.4 6.6 %copy-start.8 = (bf16[512,768]{1,0:T(8,128)(2,1)}, bf16[512,768]{1,0:T(8,128)(2,1)S(1)}, u32[]{:S(2)}) copy-start(bf16[512,768]{1,0:T(8,128)(2,1)S(1)} %collective-permute-done.4.last_ref) | copy-start | bytes 2359300
  146.4 29.1 %collective-permute-start.6 = (bf16[256,768]{1,0:T(8,128)(2,1)S(1)}, bf16[256,768]{1,0:T(8,128)(2,1)}, u32[]{:S(2)}, u32[]{:S(2)}) collective-permute-start(bf16[256,768]{1,0:T(8,128)(2,1)S(1)} %slice.108), channel_id=1, source_target_pairs={{0,1},{1,2},{2,3},{3,0},{4,5},{5,6},{6,7},{7,4},{8,9},{9,10},{10,1... | collective-permute-start | bytes 1179656 | tf_op jit(solution)/shard_map/ppermute | solution.py:24
  148.7 26.9 %collective-permute-start.7 = (bf16[256,768]{1,0:T(8,128)(2,1)}, bf16[256,768]{1,0:T(8,128)(2,1)}, u32[]{:S(2)}, u32[]{:S(2)}) collective-permute-start(bf16[256,768]{1,0:T(8,128)(2,1)} %slice.109), channel_id=1, source_target_pairs={{0,3},{1,0},{2,1},{3,2},{4,7},{5,4},{6,5},{7,6},{8,11},{9,8},{10,9... | collective-permute-start | bytes 1179656 | tf_op jit(solution)/shard_map/ppermute | solution.py:24
  183.0 24.2 %collective-permute-start.8 = (bf16[256,1536]{1,0:T(8,128)(2,1)S(1)}, bf16[256,1536]{1,0:T(8,128)(2,1)S(1)}, u32[]{:S(2)}, u32[]{:S(2)}) collective-permute-start(bf16[256,1536]{1,0:T(8,128)(2,1)S(1)} %get-tuple-element.76), channel_id=1, source_target_pairs={{0,64},{8,72},{16,80},{24,88},{32,96},{40,104},{48,112},{56,120},{... | collective-permute-start | bytes 2359304 | tf_op jit(solution)/shard_map/ppermute | solution.py:24
  207.3 7.7 %copy-start.4 = (bf16[256,1536]{1,0:T(8,128)(2,1)}, bf16[256,1536]{1,0:T(8,128)(2,1)S(1)}, u32[]{:S(2)}) copy-start(bf16[256,1536]{1,0:T(8,128)(2,1)S(1)} %collective-permute-done.8.refs_6_) | copy-start | bytes 2359300
  215.0 8.9 %copy-start.6 = (bf16[2048,768]{1,0:T(8,128)(2,1)S(1)}, bf16[2048,768]{1,0:T(8,128)(2,1)}, u32[]{:S(2)}) copy-start(bf16[2048,768]{1,0:T(8,128)(2,1)} %grad_gate.1) | copy-start | bytes 9437188
  215.0 83.6 %all-to-all-start.2 = ((bf16[16,64,2048]{2,1,0:T(8,128)(2,1)}), bf16[16,64,2048]{2,1,0:T(8,128)(2,1)}, u32[]{:S(2)}, u32[]{:S(2)}) async-start(bf16[16,64,2048]{2,1,0:T(8,128)(2,1)} %bitcast.119), calls=%async_computation.2 | async-start | bytes 8388608 | tf_op jit(solution)/shard_map/all_to_all | solution.py:300
  224.0 12.2 %collective-permute-start.10 = (bf16[256,768]{1,0:T(8,128)(2,1)S(1)}, bf16[256,768]{1,0:T(8,128)(2,1)S(1)}, u32[]{:S(2)}, u32[]{:S(2)}) collective-permute-start(bf16[256,768]{1,0:T(8,128)(2,1)S(1)} %get-tuple-element.118), channel_id=1, source_target_pairs={{0,3},{1,0},{2,1},{3,2},{4,7},{5,4},{6,5},{7,6},{8,11},{9,8},{10,9... | collective-permute-start | bytes 1179656 | tf_op jit(solution)/shard_map/ppermute | solution.py:24
  227.8 11.6 %collective-permute-start.9 = (bf16[256,768]{1,0:T(8,128)(2,1)S(1)}, bf16[256,768]{1,0:T(8,128)(2,1)S(1)}, u32[]{:S(2)}, u32[]{:S(2)}) collective-permute-start(bf16[256,768]{1,0:T(8,128)(2,1)S(1)} %get-tuple-element.119), channel_id=1, source_target_pairs={{0,1},{1,2},{2,3},{3,0},{4,5},{5,6},{6,7},{7,4},{8,9},{9,10},{10,1... | collective-permute-start | bytes 1179656 | tf_op jit(solution)/shard_map/ppermute | solution.py:24
  239.6 1.9 copy-start.5
  239.7 31.3 %collective-permute-start.14 = (bf16[2,256,768]{2,1,0:T(8,128)(2,1)S(1)}, bf16[2,256,768]{2,1,0:T(8,128)(2,1)}, u32[]{:S(2)}, u32[]{:S(2)}) collective-permute-start(bf16[2,256,768]{2,1,0:T(8,128)(2,1)S(1)} %pad_maximum_fusion.5), channel_id=1, source_target_pairs={{0,3},{1,0},{2,1},{3,2},{4,7},{5,4},{6,5},{7,6},{8,11},{9,8},{10,9... | collective-permute-start | bytes 2359304 | tf_op jit(solution)/shard_map/ppermute | solution.py:24
  240.1 30.8 %collective-permute-start.13 = (bf16[2,256,768]{2,1,0:T(8,128)(2,1)S(1)}, bf16[2,256,768]{2,1,0:T(8,128)(2,1)}, u32[]{:S(2)}, u32[]{:S(2)}) collective-permute-start(bf16[2,256,768]{2,1,0:T(8,128)(2,1)S(1)} %pad_maximum_fusion.4), channel_id=1, source_target_pairs={{0,1},{1,2},{2,3},{3,0},{4,5},{5,6},{6,7},{7,4},{8,9},{9,10},{10,1... | collective-permute-start | bytes 2359304 | tf_op jit(solution)/shard_map/ppermute | solution.py:24
  242.3 25.4 %collective-permute-start.11 = (bf16[256,768]{1,0:T(8,128)(2,1)}, bf16[256,768]{1,0:T(8,128)(2,1)S(1)}, u32[]{:S(2)}, u32[]{:S(2)}) collective-permute-start(bf16[256,768]{1,0:T(8,128)(2,1)} %get-tuple-element.113), channel_id=1, source_target_pairs={{0,1},{1,2},{2,3},{3,0},{4,5},{5,6},{6,7},{7,4},{8,9},{9,10},{10,1... | collective-permute-start | bytes 1179656 | tf_op jit(solution)/shard_map/ppermute | solution.py:24
  242.3 27.9 %collective-permute-start.12 = (bf16[256,768]{1,0:T(8,128)(2,1)S(1)}, bf16[256,768]{1,0:T(8,128)(2,1)}, u32[]{:S(2)}, u32[]{:S(2)}) collective-permute-start(bf16[256,768]{1,0:T(8,128)(2,1)S(1)} %get-tuple-element.112), channel_id=1, source_target_pairs={{0,3},{1,0},{2,1},{3,2},{4,7},{5,4},{6,5},{7,6},{8,11},{9,8},{10,9... | collective-permute-start | bytes 1179656 | tf_op jit(solution)/shard_map/ppermute | solution.py:24
  245.0 44.9 %collective-permute-start.17 = (bf16[256,768]{1,0:T(8,128)(2,1)}, bf16[256,768]{1,0:T(8,128)(2,1)S(1)}, u32[]{:S(2)}, u32[]{:S(2)}) collective-permute-start(bf16[256,768]{1,0:T(8,128)(2,1)} %get-tuple-element.91), channel_id=1, source_target_pairs={{0,64},{8,72},{16,80},{24,88},{32,96},{40,104},{48,112},{56,120},{... | collective-permute-start | bytes 1179656 | tf_op jit(solution)/shard_map/ppermute | solution.py:24
  267.8 2.4 copy-start.14
  267.8 41.2 %collective-permute-start.21 = (bf16[256,768]{1,0:T(8,128)(2,1)}, bf16[256,768]{1,0:T(8,128)(2,1)}, u32[]{:S(2)}, u32[]{:S(2)}) collective-permute-start(bf16[256,768]{1,0:T(8,128)(2,1)} %get-tuple-element.98), channel_id=1, source_target_pairs={{0,64},{8,72},{16,80},{24,88},{32,96},{40,104},{48,112},{56,120},{... | collective-permute-start | bytes 1179656 | tf_op jit(solution)/shard_map/ppermute | solution.py:24
  270.2 45.0 %collective-permute-start.19 = (bf16[256,1536]{1,0:T(8,128)(2,1)}, bf16[256,1536]{1,0:T(8,128)(2,1)S(1)}, u32[]{:S(2)}, u32[]{:S(2)}) collective-permute-start(bf16[256,1536]{1,0:T(8,128)(2,1)} %get-tuple-element.94), channel_id=1, source_target_pairs={{0,64},{8,72},{16,80},{24,88},{32,96},{40,104},{48,112},{56,120},{... | collective-permute-start | bytes 2359304 | tf_op jit(solution)/shard_map/ppermute | solution.py:24
  272.6 20.0 %collective-permute-start.16 = (bf16[2,256,768]{2,1,0:T(8,128)(2,1)S(1)}, bf16[2,256,768]{2,1,0:T(8,128)(2,1)S(1)}, u32[]{:S(2)}, u32[]{:S(2)}) collective-permute-start(bf16[2,256,768]{2,1,0:T(8,128)(2,1)S(1)} %pad_maximum_fusion.7), channel_id=1, source_target_pairs={{0,3},{1,0},{2,1},{3,2},{4,7},{5,4},{6,5},{7,6},{8,11},{9,8},{10,9... | collective-permute-start | bytes 2359304 | tf_op jit(solution)/shard_map/ppermute | solution.py:24
  272.7 3.5 %copy-start.11 = (bf16[512,768]{1,0:T(8,128)(2,1)S(1)}, bf16[512,768]{1,0:T(8,128)(2,1)}, u32[]{:S(2)}) copy-start(bf16[512,768]{1,0:T(8,128)(2,1)} %reduce-scatter.2.cloned.1.call-done) | copy-start | bytes 2359300
  272.7 20.2 %collective-permute-start.15 = (bf16[2,256,768]{2,1,0:T(8,128)(2,1)S(1)}, bf16[2,256,768]{2,1,0:T(8,128)(2,1)S(1)}, u32[]{:S(2)}, u32[]{:S(2)}) collective-permute-start(bf16[2,256,768]{2,1,0:T(8,128)(2,1)S(1)} %pad_maximum_fusion.6), channel_id=1, source_target_pairs={{0,1},{1,2},{2,3},{3,0},{4,5},{5,6},{6,7},{7,4},{8,9},{9,10},{10,1... | collective-permute-start | bytes 2359304 | tf_op jit(solution)/shard_map/ppermute | solution.py:24
  289.9 5.2 %copy-start.12 = (bf16[256,768]{1,0:T(8,128)(2,1)}, bf16[256,768]{1,0:T(8,128)(2,1)S(1)}, u32[]{:S(2)}) copy-start(bf16[256,768]{1,0:T(8,128)(2,1)S(1)} %collective-permute-done.17.refs_7_) | copy-start | bytes 1179652
  289.9 14.6 %collective-permute-start.22 = (bf16[256,768]{1,0:T(8,128)(2,1)S(1)}, bf16[256,768]{1,0:T(8,128)(2,1)S(1)}, u32[]{:S(2)}, u32[]{:S(2)}) collective-permute-start(bf16[256,768]{1,0:T(8,128)(2,1)S(1)} %get-tuple-element.128), channel_id=1, source_target_pairs={{0,4},{1,5},{2,6},{3,7},{4,0},{5,1},{6,2},{7,3},{8,12},{9,13},{10,... | collective-permute-start | bytes 1179656 | tf_op jit(solution)/shard_map/ppermute | solution.py:24
  292.5 16.6 %collective-permute-start.20 = (bf16[256,768]{1,0:T(8,128)(2,1)S(1)}, bf16[256,768]{1,0:T(8,128)(2,1)S(1)}, u32[]{:S(2)}, u32[]{:S(2)}) collective-permute-start(bf16[256,768]{1,0:T(8,128)(2,1)S(1)} %get-tuple-element.130), channel_id=1, source_target_pairs={{0,4},{1,5},{2,6},{3,7},{4,0},{5,1},{6,2},{7,3},{8,12},{9,13},{10,... | collective-permute-start | bytes 1179656 | tf_op jit(solution)/shard_map/ppermute | solution.py:24
  295.1 22.4 %collective-permute-start.18 = (bf16[256,768]{1,0:T(8,128)(2,1)S(1)}, bf16[256,768]{1,0:T(8,128)(2,1)S(1)}, u32[]{:S(2)}, u32[]{:S(2)}) collective-permute-start(bf16[256,768]{1,0:T(8,128)(2,1)S(1)} %get-tuple-element.132), channel_id=1, source_target_pairs={{0,4},{1,5},{2,6},{3,7},{4,0},{5,1},{6,2},{7,3},{8,12},{9,13},{10,... | collective-permute-start | bytes 1179656 | tf_op jit(solution)/shard_map/ppermute | solution.py:24
  304.5 0.8 copy-start.13
  309.1 0.7 copy-start.16
  315.2 2.3 copy-start.3
  317.6 0.8 copy-start.15
Sparse Core Ops, SparseCore 0:
  50.6 69.9 all-gather.1
  183.1 46.1 reduce-scatter.1

commit v3 on v2

--- a/solution.py
+++ b/solution.py
@@ -194,6 +194,46 @@
         cost_estimate=cost(2 * rows * features * hidden, 9e6),
         name=name,
     )(shift, a, b)
+
+
+def ring_kernel(block_ref, first_ref, second_ref, b_ref, *out_refs):
+    half = first_ref.shape[1]
+    top = mm(first_ref[...], b_ref[...], ((0,), (0,))).astype(BF)
+    low = mm(second_ref[...], b_ref[...], ((0,), (0,))).astype(BF)
+    for k, out_ref in enumerate(out_refs):
+
+        @pl.when(pl.program_id(0) == k)
+        def _():
+            out_ref[:half, :] = top
+            out_ref[half:, :] = low
+
+
+RING_PARTS = (((2, 0), (1, 1)), ((2, 1), (3, 0)), ((1, 0), (3, 1)), ((0, 0), (0, 1)))
+
+
+def ring_grad(z, a, b, name):
+    rows, features = a.shape
+    hidden = b.shape[1]
+    width = features // (2 * ZN)
+    blocks = [(z + far) % ZN * 2 + r for pair in RING_PARTS for far, r in pair]
+    part = pl.BlockSpec((2 * width, hidden), lambda i, blocks: (0, 0))
+    return pl.pallas_call(
+        ring_kernel,
+        grid_spec=pltpu.PrefetchScalarGridSpec(
+            num_scalar_prefetch=1,
+            grid=(ZN,),
+            in_specs=[
+                pl.BlockSpec((rows, width), lambda i, blocks: (0, blocks[2 * i])),
+                pl.BlockSpec((rows, width), lambda i, blocks: (0, blocks[2 * i + 1])),
+                pl.BlockSpec((rows, hidden), lambda i, blocks: (0, 0)),
+            ],
+            out_specs=[part] * ZN,
+        ),
+        out_shape=[jax.ShapeDtypeStruct((2 * width, hidden), BF)] * ZN,
+        compiler_params=params(),
+        cost_estimate=cost(2 * rows * features * hidden, 9e6),
+        name=name,
+    )(jnp.concatenate(blocks), a, a, b)
 
 
 def input_kernel(dg_ref, du_ref, gate_ref, up_ref, out_ref):
@@ -238,21 +278,24 @@
 
 
 def adam(keep, sums, state, moved, k, before):
-    rows, hidden = sums[0].shape
+    rows, hidden = state[0].shape[0], sums[0][0].shape[1]
     tile = min(128, rows)
-    chunk = pl.BlockSpec((tile, hidden), lambda i, keep: (i, 0))
+    steps = rows // tile
     column = pl.BlockSpec((tile, hidden), lambda i, keep: (i, k))
     shape = jax.ShapeDtypeStruct(state[0].shape, F32)
 
     def at(block):
         return pl.BlockSpec((tile, hidden), lambda i, keep: (i, block))
 
+    def term(half):
+        return pl.BlockSpec((tile, hidden), lambda i, keep: (i + half * steps, 0))
+
     return pl.pallas_call(
         functools.partial(adam_kernel, len(sums)),
         grid_spec=pltpu.PrefetchScalarGridSpec(
             num_scalar_prefetch=1,
-            grid=(rows // tile,),
-            in_specs=[chunk] * len(sums)
+            grid=(steps,),
+            in_specs=[term(half) for _, half in sums]
             + [column] * 3
             + [at(block) for _, block in moved]
             + [pl.BlockSpec(memory_space=pl.ANY)] * len(before),
@@ -263,7 +306,7 @@
         compiler_params=params(),
         cost_estimate=cost(20 * rows * hidden, 34 * rows * hidden),
         name="adam",
-    )(keep, *sums, *state, *[v for v, _ in moved], *before)
+    )(keep, *[v for v, _ in sums], *state, *[v for v, _ in moved], *before)
 
 
 def per_device(tokens, cotangent, routes, owner, master, moment1, moment2):
@@ -338,29 +381,33 @@
     quarter = down_own.shape[0] // 2
     down = (down_own, down_next, down_last, to_next(down_last[:quarter]), to_last(down_next[quarter:]))
 
-    def ring_first(grad):
-        return to_next(grad[2, 0]), to_last(grad[2, 1])
-
-    def ring_second(grad, top, low):
-        top = (grad[1, 0].astype(F32) + top.astype(F32)).astype(BF)
-        low = (grad[ZN - 1, 1].astype(F32) + low.astype(F32)).astype(BF)
-        return to_next(jnp.stack([top, grad[1, 1]])), to_last(jnp.stack([grad[ZN - 1, 0], low]))
-
-    def ring_sum(grad, ahead, behind):
-        part = grad[0].astype(F32) + ahead.astype(F32) + behind.astype(F32)
-        return part.astype(BF)
-
-    def blocks(grad):
-        return grad.reshape(ZN, 2, -1, hidden)
+    def ring_first(parts):
+        return to_next(parts[0]), to_last(parts[1])
+
+    def ring_second(parts, ahead, behind):
+        size = ahead.shape[0] // 2
+        top = parts[2][:size].astype(F32) + ahead[:size].astype(F32)
+        low = parts[2][size:].astype(F32) + behind[:size].astype(F32)
+        return to_next(top.astype(BF)), to_last(low.astype(BF))
+
+    def ring_away(parts, ahead, behind, top, low):
+        size = top.shape[0]
+        away = parts[3][size:].astype(F32) + low.astype(F32) + ahead[size:].astype(F32)
+        return away.astype(BF)
+
+    def ring_near(parts, ahead, behind, top, low):
+        return (parts[3], 0), (top, 0), (behind, 1)
 
     together = lax.optimization_barrier
 
     m_all, v_all = moment1[0].astype(BF), moment2[0].astype(BF)
     m_own = jnp.concatenate([m_all[:, :hidden], m_all[:, split:]], axis=1)
-    v_own = [v_all[:, split:], v_all[:, :hidden]]
-    v_own.append(jnp.concatenate([m_all[:, hidden:split], v_all[:, hidden:split]], axis=1))
+    v_own = [
+        jnp.concatenate([v_all[:, split:], v_all[:, :hidden]], axis=1),
+        jnp.concatenate([m_all[:, hidden:split], v_all[:, hidden:split]], axis=1),
+    ]
     dy, m_own, *others = together((dy, m_own, *v_own, *down[3:]))
-    v_own, down = others[:3], (*down[:3], *others[3:])
+    v_own, down = others[:2], (*down[:3], *others[2:])
     part_down = scattered(weight_grad(nought, dy, h, "grad_down")).reshape(2, -1, hidden)
     m_other = over_owners(m_own)
     dg, du = hidden_grads(z, dy, down, p, s)
@@ -368,32 +415,41 @@
     send_back, m_other, dg, du = together((send_back, m_other, dg, du))
     returned = over_experts(send_back)
 
-    gate = blocks(weight_grad(z, x, dg, "grad_gate"))
+    gate = ring_grad(z, x, dg, "grad_gate")
     gate, du = together((gate, du))
-    first = ring_first(gate)
-    up = blocks(weight_grad(z, x, du, "grad_up"))
-    first, up, *v_own = together((first, up, *v_own))
-    second = ring_second(gate, *first)
-    first = ring_first(up)
-    first, second, part_down = together((first, second, part_down))
-    part_gate = ring_sum(gate, *second)
-    far_gate, far_down = over_high(part_gate[1]), over_high(part_down[1])
+    first_gate = ring_first(gate)
+    up = ring_grad(z, x, du, "grad_up")
+    first_up = ring_first(up)
+    first_gate, up, v_own = together((first_gate, up, v_own))
+    second_gate = ring_second(gate, *first_gate)
+    far_down = over_high(part_down[1])
+    token_grad = combine(high, flat, returned, count)
+    first_up, second_gate, far_down, token_grad = together(
+        (first_up, second_gate, far_down, token_grad)
+    )
+    far_gate = over_high(ring_away(gate, *first_gate, *second_gate))
     v_other = [over_owners(v) for v in v_own]
-    second = ring_second(up, *first)
-    second, v_other[0] = together((second, v_other[0]))
-    part_up = ring_sum(up, *second)
-    far_up = over_high(part_up[1])
-    token_grad = combine(high, flat, returned, count)
+    second_up = ring_second(up, *first_up)
+    second_up, v_other[0] = together((second_up, v_other[0]))
+    far_up = over_high(ring_away(up, *first_up, *second_up))
 
     state = (master[0], moment1[0], moment2[0])
     steps = (
-        (2, part_down[0], far_down, ((other_b, 0), (m_other, 1), (v_other[0], 0))),
-        (0, part_gate[0], far_gate, ((other_a, 0), (m_other, 0), (v_other[1], 0))),
-        (1, part_up[0], far_up, ((other_a, 1), (v_other[2], 0), (v_other[2], 1))),
+        (2, ((part_down[0], 0), (far_down, 0)), ((other_b, 0), (m_other, 1), (v_other[0], 0))),
+        (
+            0,
+            (*ring_near(gate, *first_gate, *second_gate), (far_gate, 0)),
+            ((other_a, 0), (m_other, 0), (v_other[0], 1)),
+        ),
+        (
+            1,
+            (*ring_near(up, *first_up, *second_up), (far_up, 0)),
+            ((other_a, 1), (v_other[1], 0), (v_other[1], 1)),
+        ),
     )
     new = ()
-    for k, near, far, moved in steps:
-        new = adam(info, (near, far), state, moved, k, new)
+    for k, sums, moved in steps:
+        new = adam(info, sums, state, moved, k, new)
     return (token_grad[None], new[0][None], new[1][None], new[2][None])
 
 

time: 332 us -> 324 us (0.976)
  waiting for transfers between devices: 134 us -> 119 us
  starting transfers between devices: 73 us -> 78.4 us
    ppermute x23 -> x22, waiting for transfers between devices: 104 us -> 85.9 us  [permuted(): lax.ppermute(value, axis, [(i, target(i)) for i in range(lax.axis_size(ax...]
    pallas_call x0 -> x2, Pallas kernels: none -> 17.4 us  [ring_grad(): pl.pallas_call(ring_kernel, grid_spec=pltpu.PrefetchScalarGridSpec(num_sc...]
    pallas_call x3 -> x1, Pallas kernels: 22.5 us -> 7.4 us  [weight_grad(): pl.pallas_call(weight_kernel, grid_spec=pltpu.PrefetchScalarGridSpec(num_...]
    ppermute x23 -> x22, starting transfers between devices: 44.6 us -> 50.2 us  [permuted(): lax.ppermute(value, axis, [(i, target(i)) for i in range(lax.axis_size(ax...]
    all_to_all x3, waiting for transfers between devices: 29.1 us -> 32.7 us  [over_experts(): lax.all_to_all(boxes, 'expert', split_axis=0, concat_axis=0, tiled=True)]
  transfers between devices with their start and end apart: 28 -> 27, of which waited for: 14 -> 12; matrix products, arithmetic and copies ran while one was open for 5% -> 5% of each run, Pallas kernels for 22% -> 23%
where the time goes in v3:
time: 324 us; the launch traced here: 320 us
  waiting for transfers between devices  119 us (37%)
  Pallas kernels  86.1 us (27%)
  starting transfers between devices  78.4 us (24%)
  between operations  15 us (5%)
  local copies, waits for them, and re-layouts  11.2 us (3%)
  other arithmetic  10.7 us (3%)
    ppermute x22, waiting for transfers between devices, permuted(): lax.ppermute(value, axis, [(i, target(i)) for i in range(lax.axis_size(ax...  85.9 us
    ppermute x22, starting transfers between devices, permuted(): lax.ppermute(value, axis, [(i, target(i)) for i in range(lax.axis_size(ax...  50.2 us
    all_to_all x3, waiting for transfers between devices, over_experts(): lax.all_to_all(boxes, 'expert', split_axis=0, concat_axis=0, tiled=True)  32.7 us
    all_to_all x3, starting transfers between devices, over_experts(): lax.all_to_all(boxes, 'expert', split_axis=0, concat_axis=0, tiled=True)  28.1 us
    pallas_call x2, Pallas kernels, ring_grad(): pl.pallas_call(ring_kernel, grid_spec=pltpu.PrefetchScalarGridSpec(num_sc...  17.4 us
    pallas_call x1, Pallas kernels, forward(): pl.pallas_call(forward_kernel, grid=(hidden // tile,), in_specs=[pl.Block...  12.3 us
    pallas_call x3, Pallas kernels, adam(): pl.pallas_call(functools.partial(adam_kernel, len(sums)), grid_spec=pltpu...  11.7 us
    pallas_call x2, Pallas kernels, dispatch(): pl.pallas_call(dispatch_kernel, grid_spec=pltpu.PrefetchScalarGridSpec(nu...  11.6 us
  transfers between devices with their start and end apart: 27, of which 12 were waited for; matrix products, arithmetic and copies ran while one was open for 5% of the time, Pallas kernels for 23%

profile of v3, /device:TPU:1, one launch (start us, length us, event | category | flops | bytes accessed | tf_op | source)
XLA Modules:
  0.0 320.0 jit_solution(12825874246016112203)
XLA Ops:
  7.2 1.8 convert.5
  9.1 3.7 %collective-permute-start = (bf16[256,1536]{1,0:T(8,128)(2,1)S(1)}, bf16[256,1536]{1,0:T(8,128)(2,1)S(1)}, u32[]{:S(2)}, u32[]{:S(2)}) collective-permute-start(bf16[256,1536]{1,0:T(8,128)(2,1)S(1)} %slice_bitcast_fusion), channel_id=1, source_target_pairs={{0,64},{8,72},{16,80},{24,88},{32,96},{40,104},{48,112},{56,120},{... | collective-permute-start | bytes 2359304 | tf_op jit(solution)/shard_map/ppermute | solution.py:24
  14.0 15.5 %collective-permute-done.refs_7_ = bf16[256,1536]{1,0:T(8,128)(2,1)S(1)} collective-permute-done((bf16[256,1536]{1,0:T(8,128)(2,1)S(1)}, bf16[256,1536]{1,0:T(8,128)(2,1)S(1)}, u32[]{:S(2)}, u32[]{:S(2)}) %collective-permute-start) | collective-permute-done | bytes 786464 | tf_op jit(solution)/shard_map/ppermute | solution.py:24
  29.6 3.4 %collective-permute-start.1 = (bf16[256,1536]{1,0:T(8,128)(2,1)S(1)}, bf16[256,1536]{1,0:T(8,128)(2,1)S(1)}, u32[]{:S(2)}, u32[]{:S(2)}) collective-permute-start(bf16[256,1536]{1,0:T(8,128)(2,1)S(1)} %broadcast_select_fusion), channel_id=1, source_target_pairs={{0,4},{1,5},{2,6},{3,7},{4,0},{5,1},{6,2},{7,3},{8,12},{9,13},{10,... | collective-permute-start | bytes 2359304 | tf_op jit(solution)/shard_map/ppermute | solution.py:24
  34.5 2.8 collective-permute-start.2
  37.9 5.8 %dispatch.3 = bf16[1024,2048]{1,0:T(8,128)(2,1)} custom-call(s32[1]{0:T(128)} %bitcast.1.high_ref, s32[1,512]{1,0:T(1,128)} %bitcast_add_fusion.1.flat_ref, bf16[512,2048]{1,0:T(8,128)(2,1)} %bitcast.69), custom_call_target="tpu_custom_call" | custom-call | flops 2147483648 | bytes 6291456 | tf_op jit(solution)/shard_map/dispatch/pallas_call | solution.py:50
  44.9 4.3 %collective-permute-done.1 = bf16[256,1536]{1,0:T(8,128)(2,1)S(1)} collective-permute-done((bf16[256,1536]{1,0:T(8,128)(2,1)S(1)}, bf16[256,1536]{1,0:T(8,128)(2,1)S(1)}, u32[]{:S(2)}, u32[]{:S(2)}) %collective-permute-start.1) | collective-permute-done | bytes 786464 | tf_op jit(solution)/shard_map/ppermute | solution.py:24
  50.5 7.7 %all-to-all-start = ((bf16[16,64,2048]{2,1,0:T(8,128)(2,1)}), bf16[16,64,2048]{2,1,0:T(8,128)(2,1)}, u32[]{:S(2)}, u32[]{:S(2)}) async-start(bf16[16,64,2048]{2,1,0:T(8,128)(2,1)} %bitcast.64), calls=%async_computation | async-start | bytes 8388608 | tf_op jit(solution)/shard_map/all_to_all | solution.py:343
  58.2 2.7 collective-permute-start.3
  60.9 5.8 %dispatch.2 = bf16[1024,2048]{1,0:T(8,128)(2,1)} custom-call(s32[1]{0:T(128)} %bitcast.1.high_ref, s32[1,512]{1,0:T(1,128)} %bitcast_add_fusion.1.flat_ref, bf16[512,2048]{1,0:T(8,128)(2,1)} %bitcast.70), custom_call_target="tpu_custom_call" | custom-call | flops 2147483648 | bytes 6291456 | tf_op jit(solution)/shard_map/dispatch/pallas_call | solution.py:50
  66.7 37.8 %collective-permute-done.3 = bf16[256,768]{1,0:T(8,128)(2,1)S(1)} collective-permute-done((bf16[256,768]{1,0:T(8,128)(2,1)S(1)}, bf16[256,768]{1,0:T(8,128)(2,1)S(1)}, u32[]{:S(2)}, u32[]{:S(2)}) %collective-permute-start.3) | collective-permute-done | bytes 393248 | tf_op jit(solution)/shard_map/ppermute | solution.py:24
  104.6 6.5 %all-to-all-done = bf16[16,64,2048]{2,1,0:T(8,128)(2,1)} async-done(((bf16[16,64,2048]{2,1,0:T(8,128)(2,1)}), bf16[16,64,2048]{2,1,0:T(8,128)(2,1)}, u32[]{:S(2)}, u32[]{:S(2)}) %all-to-all-start) | async-done | bytes 4194336 | tf_op jit(solution)/shard_map/all_to_all | solution.py:343
  111.2 11.7 %all-to-all-start.1 = ((bf16[16,64,2048]{2,1,0:T(8,128)(2,1)}), bf16[16,64,2048]{2,1,0:T(8,128)(2,1)}, u32[]{:S(2)}, u32[]{:S(2)}) async-start(bf16[16,64,2048]{2,1,0:T(8,128)(2,1)} %bitcast.63), calls=%async_computation.1 | async-start | bytes 8388608 | tf_op jit(solution)/shard_map/all_to_all | solution.py:343
  123.1 1.4 copy-done.1
  124.7 1.5 collective-permute-start.4
  126.2 2.4 collective-permute-start.5
  129.7 12.3 %forward.1 = (bf16[1024,768]{1,0:T(8,128)(2,1)}, f32[1024,768]{1,0:T(8,128)}, f32[1024,768]{1,0:T(8,128)}) custom-call(bf16[1024,2048]{1,0:T(8,128)(2,1)} %bitcast.13.x_ref.first_ref.second_ref, bf16[2048,1536]{1,0:T(8,128)(2,1)} %all-gather.2.cloned.1.call-done.gate_ref.up_ref, bf16[2048,1536]{1,0:T(8,128)(2,1)} %all-gather.2.cloned.1.call-done.gate_ref.up_ref), custom_call_target="tpu_custom_call" | custom-call | flops 6442450944 | bytes 20000000 | tf_op jit(solution)/shard_map/forward/pallas_call | solution.py:116
  142.0 4.4 %collective-permute-done.4.last_ref = bf16[512,768]{1,0:T(8,128)(2,1)S(1)} collective-permute-done((bf16[512,768]{1,0:T(8,128)(2,1)S(1)}, bf16[512,768]{1,0:T(8,128)(2,1)S(1)}, u32[]{:S(2)}, u32[]{:S(2)}) %collective-permute-start.4) | collective-permute-done | bytes 786464 | tf_op jit(solution)/shard_map/ppermute | solution.py:24
  148.4 2.2 collective-permute-start.7
  152.7 22.9 %all-to-all-done.1 = bf16[16,64,2048]{2,1,0:T(8,128)(2,1)} async-done(((bf16[16,64,2048]{2,1,0:T(8,128)(2,1)}), bf16[16,64,2048]{2,1,0:T(8,128)(2,1)}, u32[]{:S(2)}, u32[]{:S(2)}) %all-to-all-start.1) | async-done | bytes 4194336 | tf_op jit(solution)/shard_map/all_to_all | solution.py:343
  175.6 7.4 %grad_down.1 = bf16[2048,768]{1,0:T(8,128)(2,1)} custom-call(s32[1]{0:T(128)} %constant.113.clone.1.shift_ref, bf16[1024,2048]{1,0:T(8,128)(2,1)} %bitcast.15.dy_ref.a_ref, bf16[1024,768]{1,0:T(8,128)(2,1)} %get-tuple-element.106.b_ref), custom_call_target="tpu_custom_call" | custom-call | flops 3221225472 | bytes 9000000 | tf_op jit(solution)/shard_map/grad_down/pallas_call | solution.py:181
  183.0 4.3 %collective-permute-start.8 = (bf16[256,1536]{1,0:T(8,128)(2,1)S(1)}, bf16[256,1536]{1,0:T(8,128)(2,1)S(1)}, u32[]{:S(2)}, u32[]{:S(2)}) collective-permute-start(bf16[256,1536]{1,0:T(8,128)(2,1)S(1)} %get-tuple-element.87), channel_id=1, source_target_pairs={{0,64},{8,72},{16,80},{24,88},{32,96},{40,104},{48,112},{56,120},{... | collective-permute-start | bytes 2359304 | tf_op jit(solution)/shard_map/ppermute | solution.py:24
  187.3 9.0 %hidden_grads.1 = (bf16[1024,768]{1,0:T(8,128)(2,1)}, bf16[1024,768]{1,0:T(8,128)(2,1)}) custom-call(s32[1]{0:T(128)} %bitcast.z_ref, bf16[1024,2048]{1,0:T(8,128)(2,1)} %bitcast.15.dy_ref.a_ref, bf16[512,768]{1,0:T(8,128)(2,1)} %copy-done.6, bf16[512,768]{1,0:T(8,128)(2,1)} %copy-done.12, bf16[512,768]{1,0:T(8,128)(2,1)} %copy-done.11, ...), custom_call_target="tpu_custom_call" | custom-call | flops 3221225472 | bytes 17000000 | tf_op jit(solution)/shard_map/hidden_grads/pallas_call | solution.py:156
  196.3 10.8 %input_grad.1 = bf16[1024,2048]{1,0:T(8,128)(2,1)} custom-call(bf16[1024,768]{1,0:T(8,128)(2,1)} %get-tuple-element.88.dg_ref.b_ref, bf16[1024,768]{1,0:T(8,128)(2,1)} %get-tuple-element.94.du_ref.b_ref, bf16[2048,1536]{1,0:T(8,128)(2,1)} %all-gather.2.cloned.1.call-done.gate_ref.up_ref, bf16[2048,1536]{1,0:T(8,128)(2,1)} %all-gather.2.cloned.1.call-done.gate_ref.up_ref), custom_call_target="tpu_custom_call" | custom-call | flops 6442450944 | bytes 14000000 | tf_op jit(solution)/shard_map/input_grad/pallas_call | solution.py:252
  208.0 8.7 %all-to-all-start.2 = ((bf16[16,64,2048]{2,1,0:T(8,128)(2,1)}), bf16[16,64,2048]{2,1,0:T(8,128)(2,1)}, u32[]{:S(2)}, u32[]{:S(2)}) async-start(bf16[16,64,2048]{2,1,0:T(8,128)(2,1)} %bitcast.62), calls=%async_computation.3 | async-start | bytes 8388608 | tf_op jit(solution)/shard_map/all_to_all | solution.py:343
  217.3 8.8 %grad_gate.1 = (bf16[512,768]{1,0:T(8,128)(2,1)}, bf16[512,768]{1,0:T(8,128)(2,1)}, bf16[512,768]{1,0:T(8,128)(2,1)}, bf16[512,768]{1,0:T(8,128)(2,1)}) custom-call(s32[8]{0:T(128)} %concatenate.19.block_ref, bf16[1024,2048]{1,0:T(8,128)(2,1)} %bitcast.13.x_ref.first_ref.second_ref, bf16[1024,2048]{1,0:T(8,128)(2,1)} %bitcast.13.x_ref.first_ref.second_ref, ...), custom_call_target="tpu_custom_call" | custom-call | flops 3221225472 | bytes 9000000 | tf_op jit(solution)/shard_map/grad_gate/pallas_call | solution.py:220
  227.4 2.4 collective-permute-start.12
  229.8 8.7 %grad_up.1 = (bf16[512,768]{1,0:T(8,128)(2,1)}, bf16[512,768]{1,0:T(8,128)(2,1)}, bf16[512,768]{1,0:T(8,128)(2,1)}, bf16[512,768]{1,0:T(8,128)(2,1)}) custom-call(s32[8]{0:T(128)} %concatenate.19.block_ref, bf16[1024,2048]{1,0:T(8,128)(2,1)} %bitcast.13.x_ref.first_ref.second_ref, bf16[1024,2048]{1,0:T(8,128)(2,1)} %bitcast.13.x_ref.first_ref.second_ref, ...), custom_call_target="tpu_custom_call" | custom-call | flops 3221225472 | bytes 9000000 | tf_op jit(solution)/shard_map/grad_up/pallas_call | solution.py:220
  238.5 1.4 collective-permute-start.10
  239.9 7.8 %collective-permute-done.11 = bf16[512,768]{1,0:T(8,128)(2,1)S(1)} collective-permute-done((bf16[512,768]{1,0:T(8,128)(2,1)}, bf16[512,768]{1,0:T(8,128)(2,1)S(1)}, u32[]{:S(2)}, u32[]{:S(2)}) %collective-permute-start.11) | collective-permute-done | bytes 786464 | tf_op jit(solution)/shard_map/ppermute | solution.py:24
  249.3 2.3 collective-permute-start.14
  251.5 2.1 fusion.5
  253.6 2.6 collective-permute-start.15
  257.1 6.6 %collective-permute-done.10.refs_2_ = bf16[512,768]{1,0:T(8,128)(2,1)S(1)} collective-permute-done((bf16[512,768]{1,0:T(8,128)(2,1)}, bf16[512,768]{1,0:T(8,128)(2,1)S(1)}, u32[]{:S(2)}, u32[]{:S(2)}) %collective-permute-start.10) | collective-permute-done | bytes 786464 | tf_op jit(solution)/shard_map/ppermute | solution.py:24
  263.7 2.8 collective-permute-start.18
  266.5 3.2 %all-to-all-done.2 = bf16[16,64,2048]{2,1,0:T(8,128)(2,1)} async-done(((bf16[16,64,2048]{2,1,0:T(8,128)(2,1)}), bf16[16,64,2048]{2,1,0:T(8,128)(2,1)}, u32[]{:S(2)}, u32[]{:S(2)}) %all-to-all-start.2) | async-done | bytes 4194336 | tf_op jit(solution)/shard_map/all_to_all | solution.py:343
  269.8 6.0 %combine.1 = bf16[512,2048]{1,0:T(8,128)(2,1)} custom-call(s32[1]{0:T(128)} %bitcast.1.high_ref, s32[512,1]{1,0:T(8,128)} %copy.21.flat_ref, bf16[1024,2048]{1,0:T(8,128)(2,1)} %bitcast.21.back_ref), custom_call_target="tpu_custom_call" | custom-call | flops 2147483648 | bytes 6291456 | tf_op jit(solution)/shard_map/combine/pallas_call | solution.py:81
  276.0 1.6 collective-permute-start.16
  277.7 2.4 collective-permute-start.17
  280.1 4.0 %collective-permute-start.20 = (bf16[256,1536]{1,0:T(8,128)(2,1)}, bf16[256,1536]{1,0:T(8,128)(2,1)S(1)}, u32[]{:S(2)}, u32[]{:S(2)}) collective-permute-start(bf16[256,1536]{1,0:T(8,128)(2,1)} %get-tuple-element.116), channel_id=1, source_target_pairs={{0,64},{8,72},{16,80},{24,88},{32,96},{40,104},{48,112},{56,120},{... | collective-permute-start | bytes 2359304 | tf_op jit(solution)/shard_map/ppermute | solution.py:24
  284.1 1.9 add_convert_fusion
  286.0 2.6 collective-permute-start.21
  288.6 2.7 collective-permute-done.18.refs_7_.refs_9_
  292.1 2.8 collective-permute-start.19
  294.8 3.8 %adam.3 = (f32[256,2304]{1,0:T(8,128)}, f32[256,2304]{1,0:T(8,128)}, f32[256,2304]{1,0:T(8,128)}) custom-call(s32[1]{0:T(128)} %bitcast.23.keep_ref, bf16[256,768]{1,0:T(8,128)(2,1)} %get-tuple-element.138.refs_0_, bf16[256,768]{1,0:T(8,128)(2,1)} %copy-done.19, f32[256,2304]{1,0:T(8,128)} %bitcast.50, f32[256,2304]{1,0:T(8,128)} %bitcast.53, ...), custom_call_target="tpu_custom_call" | custom-call | flops 3932160 | bytes 6684672 | tf_op jit(solution)/shard_map/adam/pallas_call | solution.py:293
  298.6 4.0 %adam.4 = (f32[256,2304]{1,0:T(8,128)}, f32[256,2304]{1,0:T(8,128)}, f32[256,2304]{1,0:T(8,128)}) custom-call(s32[1]{0:T(128)} %bitcast.23.keep_ref, bf16[512,768]{1,0:T(8,128)(2,1)} %get-tuple-element.117.refs_0_, bf16[256,768]{1,0:T(8,128)(2,1)} %collective-permute-done.13.refs_1_, ...), custom_call_target="tpu_custom_call", output_to_operand_aliasing={{0}: (11, {}), {1}: (12, {}), {2}: (13, {})} | custom-call | flops 3932160 | bytes 6684672 | tf_op jit(solution)/shard_map/adam/pallas_call | solution.py:293
  302.6 5.6 %collective-permute-done.20.refs_8_.refs_9_ = bf16[256,1536]{1,0:T(8,128)(2,1)S(1)} collective-permute-done((bf16[256,1536]{1,0:T(8,128)(2,1)}, bf16[256,1536]{1,0:T(8,128)(2,1)S(1)}, u32[]{:S(2)}, u32[]{:S(2)}) %collective-permute-start.20) | collective-permute-done | bytes 786464 | tf_op jit(solution)/shard_map/ppermute | solution.py:24
  309.2 4.0 %adam.5 = (f32[256,2304]{1,0:T(8,128)}, f32[256,2304]{1,0:T(8,128)}, f32[256,2304]{1,0:T(8,128)}) custom-call(s32[1]{0:T(128)} %bitcast.23.keep_ref, bf16[512,768]{1,0:T(8,128)(2,1)} %get-tuple-element.109.refs_0_, bf16[256,768]{1,0:T(8,128)(2,1)} %copy-done.20, ...), custom_call_target="tpu_custom_call", output_to_operand_aliasing={{0}: (11, {}), {1}: (12, {}), {2}: (13, {})} | custom-call | flops 3932160 | bytes 6684672 | tf_op jit(solution)/shard_map/adam/pallas_call | solution.py:293
  (99 shorter events, 18.3 us)
Async XLA Ops:
  7.2 5.6 %copy-start.23 = (s32[16]{0:T(128)S(1)}, s32[16]{0:T(128)}, u32[]{:S(2)}) copy-start(s32[16]{0:T(128)} %param.10) | copy-start | bytes 196
  7.2 122.5 %all-gather.2.cloned.1.call-start = ((), (), s32[]{:S(2)}) async-start(), calls=%async_computation.4 | async-start | bytes 7864320 | tf_op jit(solution)/shard_map/all_gather | solution.py:347
  9.0 24.0 %copy-start.22 = (s32[1,512,1]{1,2,0:T(1,128)S(1)}, s32[1,512,1]{1,2,0:T(1,128)}, u32[]{:S(2)}) copy-start(s32[1,512,1]{1,2,0:T(1,128)} %param.9) | copy-start | bytes 6148
  9.1 20.4 %collective-permute-start = (bf16[256,1536]{1,0:T(8,128)(2,1)S(1)}, bf16[256,1536]{1,0:T(8,128)(2,1)S(1)}, u32[]{:S(2)}, u32[]{:S(2)}) collective-permute-start(bf16[256,1536]{1,0:T(8,128)(2,1)S(1)} %slice_bitcast_fusion), channel_id=1, source_target_pairs={{0,64},{8,72},{16,80},{24,88},{32,96},{40,104},{48,112},{56,120},{... | collective-permute-start | bytes 2359304 | tf_op jit(solution)/shard_map/ppermute | solution.py:24
  29.5 14.2 %copy-start.2 = (bf16[256,1536]{1,0:T(8,128)(2,1)}, bf16[256,1536]{1,0:T(8,128)(2,1)S(1)}, u32[]{:S(2)}) copy-start(bf16[256,1536]{1,0:T(8,128)(2,1)S(1)} %collective-permute-done.refs_7_) | copy-start | bytes 2359300
  29.6 19.6 %collective-permute-start.1 = (bf16[256,1536]{1,0:T(8,128)(2,1)S(1)}, bf16[256,1536]{1,0:T(8,128)(2,1)S(1)}, u32[]{:S(2)}, u32[]{:S(2)}) collective-permute-start(bf16[256,1536]{1,0:T(8,128)(2,1)S(1)} %broadcast_select_fusion), channel_id=1, source_target_pairs={{0,4},{1,5},{2,6},{3,7},{4,0},{5,1},{6,2},{7,3},{8,12},{9,13},{10,... | collective-permute-start | bytes 2359304 | tf_op jit(solution)/shard_map/ppermute | solution.py:24
  34.5 10.4 %collective-permute-start.2 = (bf16[256,768]{1,0:T(8,128)(2,1)S(1)}, bf16[256,768]{1,0:T(8,128)(2,1)S(1)}, u32[]{:S(2)}, u32[]{:S(2)}) collective-permute-start(bf16[256,768]{1,0:T(8,128)(2,1)S(1)} %slice_bitcast_fusion.1), channel_id=1, source_target_pairs={{0,64},{8,72},{16,80},{24,88},{32,96},{40,104},{48,112},{56,120},{... | collective-permute-start | bytes 1179656 | tf_op jit(solution)/shard_map/ppermute | solution.py:24
  44.9 13.3 %copy-start.13 = (bf16[256,768]{1,0:T(8,128)(2,1)}, bf16[256,768]{1,0:T(8,128)(2,1)S(1)}, u32[]{:S(2)}) copy-start(bf16[256,768]{1,0:T(8,128)(2,1)S(1)} %collective-permute-done.2.refs_5_) | copy-start | bytes 1179652
  50.5 60.7 %all-to-all-start = ((bf16[16,64,2048]{2,1,0:T(8,128)(2,1)}), bf16[16,64,2048]{2,1,0:T(8,128)(2,1)}, u32[]{:S(2)}, u32[]{:S(2)}) async-start(bf16[16,64,2048]{2,1,0:T(8,128)(2,1)} %bitcast.64), calls=%async_computation | async-start | bytes 8388608 | tf_op jit(solution)/shard_map/all_to_all | solution.py:343
  58.2 46.4 %collective-permute-start.3 = (bf16[256,768]{1,0:T(8,128)(2,1)S(1)}, bf16[256,768]{1,0:T(8,128)(2,1)S(1)}, u32[]{:S(2)}, u32[]{:S(2)}) collective-permute-start(bf16[256,768]{1,0:T(8,128)(2,1)S(1)} %broadcast_select_fusion.1), channel_id=1, source_target_pairs={{0,4},{1,5},{2,6},{3,7},{4,0},{5,1},{6,2},{7,3},{8,12},{9,13},{10,... | collective-permute-start | bytes 1179656 | tf_op jit(solution)/shard_map/ppermute | solution.py:24
  104.6 21.6 %copy-start.6 = (bf16[512,768]{1,0:T(8,128)(2,1)}, bf16[512,768]{1,0:T(8,128)(2,1)S(1)}, u32[]{:S(2)}) copy-start(bf16[512,768]{1,0:T(8,128)(2,1)S(1)} %pad_maximum_fusion.1.own_ref) | copy-start | bytes 2359300
  111.2 11.7 %copy-start = (f32[1,256,2304]{2,1,0:T(8,128)S(1)}, f32[1,256,2304]{2,1,0:T(8,128)}, u32[]{:S(2)}) copy-start(f32[1,256,2304]{2,1,0:T(8,128)} %param.12) | copy-start | bytes 7077892
  111.2 64.4 %all-to-all-start.1 = ((bf16[16,64,2048]{2,1,0:T(8,128)(2,1)}), bf16[16,64,2048]{2,1,0:T(8,128)(2,1)}, u32[]{:S(2)}, u32[]{:S(2)}) async-start(bf16[16,64,2048]{2,1,0:T(8,128)(2,1)} %bitcast.63), calls=%async_computation.1 | async-start | bytes 8388608 | tf_op jit(solution)/shard_map/all_to_all | solution.py:343
  122.9 128.7 %reduce-scatter.2.cloned.1.call-start = ((), (), s32[]{:S(2)}) async-start(), calls=%async_computation.5 | async-start | bytes 3932160 | tf_op jit(solution)/shard_map/reduce_scatter | solution.py:350
  122.9 1.7 copy-start.1
  124.7 21.7 %collective-permute-start.4 = (bf16[512,768]{1,0:T(8,128)(2,1)S(1)}, bf16[512,768]{1,0:T(8,128)(2,1)S(1)}, u32[]{:S(2)}, u32[]{:S(2)}) collective-permute-start(bf16[512,768]{1,0:T(8,128)(2,1)S(1)} %pad_maximum_fusion.1.own_ref), channel_id=1, source_target_pairs={{0,1},{1,2},{2,3},{3,0},{4,5},{5,6},{6,7},{7,4},{8,9},{9,10},{10,1... | collective-permute-start | bytes 2359304 | tf_op jit(solution)/shard_map/ppermute | solution.py:24
  126.2 20.2 %collective-permute-start.5 = (bf16[512,768]{1,0:T(8,128)(2,1)S(1)}, bf16[512,768]{1,0:T(8,128)(2,1)S(1)}, u32[]{:S(2)}, u32[]{:S(2)}) collective-permute-start(bf16[512,768]{1,0:T(8,128)(2,1)S(1)} %pad_maximum_fusion.1.own_ref), channel_id=1, source_target_pairs={{0,3},{1,0},{2,1},{3,2},{4,7},{5,4},{6,5},{7,6},{8,11},{9,8},{10,9... | collective-permute-start | bytes 2359304 | tf_op jit(solution)/shard_map/ppermute | solution.py:24
  129.7 21.0 %copy-start.15 = (bf16[256,768]{1,0:T(8,128)(2,1)S(1)}, bf16[256,768]{1,0:T(8,128)(2,1)}, u32[]{:S(2)}) copy-start(bf16[256,768]{1,0:T(8,128)(2,1)} %get-tuple-element.136) | copy-start | bytes 1179652
  129.7 21.0 %copy-start.16 = (bf16[256,768]{1,0:T(8,128)(2,1)S(1)}, bf16[256,768]{1,0:T(8,128)(2,1)}, u32[]{:S(2)}) copy-start(bf16[256,768]{1,0:T(8,128)(2,1)} %get-tuple-element.137) | copy-start | bytes 1179652
  142.0 9.7 %copy-start.14 = (bf16[256,768]{1,0:T(8,128)(2,1)S(1)}, bf16[256,768]{1,0:T(8,128)(2,1)}, u32[]{:S(2)}) copy-start(bf16[256,768]{1,0:T(8,128)(2,1)} %get-tuple-element.135) | copy-start | bytes 1179652
  146.4 6.3 %copy-start.11 = (bf16[512,768]{1,0:T(8,128)(2,1)}, bf16[512,768]{1,0:T(8,128)(2,1)S(1)}, u32[]{:S(2)}) copy-start(bf16[512,768]{1,0:T(8,128)(2,1)S(1)} %collective-permute-done.4.last_ref) | copy-start | bytes 2359300
  146.4 6.3 %copy-start.12 = (bf16[512,768]{1,0:T(8,128)(2,1)}, bf16[512,768]{1,0:T(8,128)(2,1)S(1)}, u32[]{:S(2)}) copy-start(bf16[512,768]{1,0:T(8,128)(2,1)S(1)} %collective-permute-done.5.next_ref) | copy-start | bytes 2359300
  147.2 28.4 %collective-permute-start.6 = (bf16[256,768]{1,0:T(8,128)(2,1)}, bf16[256,768]{1,0:T(8,128)(2,1)}, u32[]{:S(2)}, u32[]{:S(2)}) collective-permute-start(bf16[256,768]{1,0:T(8,128)(2,1)} %slice.92), channel_id=1, source_target_pairs={{0,1},{1,2},{2,3},{3,0},{4,5},{5,6},{6,7},{7,4},{8,9},{9,10},{10,1... | collective-permute-start | bytes 1179656 | tf_op jit(solution)/shard_map/ppermute | solution.py:24
  148.4 27.2 %collective-permute-start.7 = (bf16[256,768]{1,0:T(8,128)(2,1)}, bf16[256,768]{1,0:T(8,128)(2,1)}, u32[]{:S(2)}, u32[]{:S(2)}) collective-permute-start(bf16[256,768]{1,0:T(8,128)(2,1)} %slice.93), channel_id=1, source_target_pairs={{0,3},{1,0},{2,1},{3,2},{4,7},{5,4},{6,5},{7,6},{8,11},{9,8},{10,9... | collective-permute-start | bytes 1179656 | tf_op jit(solution)/shard_map/ppermute | solution.py:24
  183.0 24.1 %collective-permute-start.8 = (bf16[256,1536]{1,0:T(8,128)(2,1)S(1)}, bf16[256,1536]{1,0:T(8,128)(2,1)S(1)}, u32[]{:S(2)}, u32[]{:S(2)}) collective-permute-start(bf16[256,1536]{1,0:T(8,128)(2,1)S(1)} %get-tuple-element.87), channel_id=1, source_target_pairs={{0,64},{8,72},{16,80},{24,88},{32,96},{40,104},{48,112},{56,120},{... | collective-permute-start | bytes 2359304 | tf_op jit(solution)/shard_map/ppermute | solution.py:24
  208.0 61.8 %all-to-all-start.2 = ((bf16[16,64,2048]{2,1,0:T(8,128)(2,1)}), bf16[16,64,2048]{2,1,0:T(8,128)(2,1)}, u32[]{:S(2)}, u32[]{:S(2)}) async-start(bf16[16,64,2048]{2,1,0:T(8,128)(2,1)} %bitcast.62), calls=%async_computation.3 | async-start | bytes 8388608 | tf_op jit(solution)/shard_map/all_to_all | solution.py:343
  226.1 21.6 %copy-start.18 = (bf16[512,768]{1,0:T(8,128)(2,1)S(1)}, bf16[512,768]{1,0:T(8,128)(2,1)}, u32[]{:S(2)}) copy-start(bf16[512,768]{1,0:T(8,128)(2,1)} %get-tuple-element.97) | copy-start | bytes 2359300
  226.1 21.6 %collective-permute-start.11 = (bf16[512,768]{1,0:T(8,128)(2,1)}, bf16[512,768]{1,0:T(8,128)(2,1)S(1)}, u32[]{:S(2)}, u32[]{:S(2)}) collective-permute-start(bf16[512,768]{1,0:T(8,128)(2,1)} %get-tuple-element.98), channel_id=1, source_target_pairs={{0,1},{1,2},{2,3},{3,0},{4,5},{5,6},{6,7},{7,4},{8,9},{9,10},{10,1... | collective-permute-start | bytes 2359304 | tf_op jit(solution)/shard_map/ppermute | solution.py:24
  227.4 20.3 %collective-permute-start.12 = (bf16[512,768]{1,0:T(8,128)(2,1)}, bf16[512,768]{1,0:T(8,128)(2,1)S(1)}, u32[]{:S(2)}, u32[]{:S(2)}) collective-permute-start(bf16[512,768]{1,0:T(8,128)(2,1)} %get-tuple-element.99), channel_id=1, source_target_pairs={{0,3},{1,0},{2,1},{3,2},{4,7},{5,4},{6,5},{7,6},{8,11},{9,8},{10,9... | collective-permute-start | bytes 2359304 | tf_op jit(solution)/shard_map/ppermute | solution.py:24
  238.5 25.2 %collective-permute-start.10 = (bf16[512,768]{1,0:T(8,128)(2,1)}, bf16[512,768]{1,0:T(8,128)(2,1)S(1)}, u32[]{:S(2)}, u32[]{:S(2)}) collective-permute-start(bf16[512,768]{1,0:T(8,128)(2,1)} %get-tuple-element.96), channel_id=1, source_target_pairs={{0,3},{1,0},{2,1},{3,2},{4,7},{5,4},{6,5},{7,6},{8,11},{9,8},{10,9... | collective-permute-start | bytes 2359304 | tf_op jit(solution)/shard_map/ppermute | solution.py:24
  239.9 35.9 %collective-permute-start.9 = (bf16[512,768]{1,0:T(8,128)(2,1)}, bf16[512,768]{1,0:T(8,128)(2,1)S(1)}, u32[]{:S(2)}, u32[]{:S(2)}) collective-permute-start(bf16[512,768]{1,0:T(8,128)(2,1)} %get-tuple-element.95), channel_id=1, source_target_pairs={{0,1},{1,2},{2,3},{3,0},{4,5},{5,6},{6,7},{7,4},{8,9},{9,10},{10,1... | collective-permute-start | bytes 2359304 | tf_op jit(solution)/shard_map/ppermute | solution.py:24
  247.7 9.4 %copy-start.8 = (bf16[512,768]{1,0:T(8,128)(2,1)}, bf16[512,768]{1,0:T(8,128)(2,1)S(1)}, u32[]{:S(2)}) copy-start(bf16[512,768]{1,0:T(8,128)(2,1)S(1)} %collective-permute-done.12.refs_2_) | copy-start | bytes 2359300
  248.9 26.9 %collective-permute-start.13 = (bf16[256,768]{1,0:T(8,128)(2,1)}, bf16[256,768]{1,0:T(8,128)(2,1)}, u32[]{:S(2)}, u32[]{:S(2)}) collective-permute-start(bf16[256,768]{1,0:T(8,128)(2,1)} %get-tuple-element.143), channel_id=1, source_target_pairs={{0,1},{1,2},{2,3},{3,0},{4,5},{5,6},{6,7},{7,4},{8,9},{9,10},{10,1... | collective-permute-start | bytes 1179656 | tf_op jit(solution)/shard_map/ppermute | solution.py:24
  249.3 26.5 %collective-permute-start.14 = (bf16[256,768]{1,0:T(8,128)(2,1)}, bf16[256,768]{1,0:T(8,128)(2,1)}, u32[]{:S(2)}, u32[]{:S(2)}) collective-permute-start(bf16[256,768]{1,0:T(8,128)(2,1)} %get-tuple-element.142), channel_id=1, source_target_pairs={{0,3},{1,0},{2,1},{3,2},{4,7},{5,4},{6,5},{7,6},{8,11},{9,8},{10,9... | collective-permute-start | bytes 1179656 | tf_op jit(solution)/shard_map/ppermute | solution.py:24
  253.6 22.2 %collective-permute-start.15 = (bf16[256,768]{1,0:T(8,128)(2,1)}, bf16[256,768]{1,0:T(8,128)(2,1)S(1)}, u32[]{:S(2)}, u32[]{:S(2)}) collective-permute-start(bf16[256,768]{1,0:T(8,128)(2,1)} %get-tuple-element.139), channel_id=1, source_target_pairs={{0,4},{1,5},{2,6},{3,7},{4,0},{5,1},{6,2},{7,3},{8,12},{9,13},{10,... | collective-permute-start | bytes 1179656 | tf_op jit(solution)/shard_map/ppermute | solution.py:24
  263.7 12.1 %copy-start.7 = (bf16[512,768]{1,0:T(8,128)(2,1)}, bf16[512,768]{1,0:T(8,128)(2,1)S(1)}, u32[]{:S(2)}) copy-start(bf16[512,768]{1,0:T(8,128)(2,1)S(1)} %collective-permute-done.10.refs_2_) | copy-start | bytes 2359300
  263.7 27.6 %collective-permute-start.18 = (bf16[256,1536]{1,0:T(8,128)(2,1)}, bf16[256,1536]{1,0:T(8,128)(2,1)S(1)}, u32[]{:S(2)}, u32[]{:S(2)}) collective-permute-start(bf16[256,1536]{1,0:T(8,128)(2,1)} %pad_maximum_fusion.3), channel_id=1, source_target_pairs={{0,64},{8,72},{16,80},{24,88},{32,96},{40,104},{48,112},{56,120},{... | collective-permute-start | bytes 2359304 | tf_op jit(solution)/shard_map/ppermute | solution.py:24
  269.8 6.0 %copy-start.17 = (bf16[512,768]{1,0:T(8,128)(2,1)S(1)}, bf16[512,768]{1,0:T(8,128)(2,1)}, u32[]{:S(2)}) copy-start(bf16[512,768]{1,0:T(8,128)(2,1)} %get-tuple-element.110) | copy-start | bytes 2359300
  275.8 8.3 %copy-start.10 = (bf16[512,768]{1,0:T(8,128)(2,1)S(1)}, bf16[512,768]{1,0:T(8,128)(2,1)}, u32[]{:S(2)}) copy-start(bf16[512,768]{1,0:T(8,128)(2,1)} %get-tuple-element.117.refs_0_) | copy-start | bytes 2359300
  275.8 15.6 %copy-start.9 = (bf16[512,768]{1,0:T(8,128)(2,1)S(1)}, bf16[512,768]{1,0:T(8,128)(2,1)}, u32[]{:S(2)}) copy-start(bf16[512,768]{1,0:T(8,128)(2,1)} %get-tuple-element.109.refs_0_) | copy-start | bytes 2359300
  275.8 15.7 %copy-start.19 = (bf16[256,768]{1,0:T(8,128)(2,1)}, bf16[256,768]{1,0:T(8,128)(2,1)S(1)}, u32[]{:S(2)}) copy-start(bf16[256,768]{1,0:T(8,128)(2,1)S(1)} %collective-permute-done.15.refs_1_) | copy-start | bytes 1179652
  276.0 15.3 %collective-permute-start.16 = (bf16[256,768]{1,0:T(8,128)(2,1)S(1)}, bf16[256,768]{1,0:T(8,128)(2,1)S(1)}, u32[]{:S(2)}, u32[]{:S(2)}) collective-permute-start(bf16[256,768]{1,0:T(8,128)(2,1)S(1)} %get-tuple-element.141), channel_id=1, source_target_pairs={{0,1},{1,2},{2,3},{3,0},{4,5},{5,6},{6,7},{7,4},{8,9},{9,10},{10,1... | collective-permute-start | bytes 1179656 | tf_op jit(solution)/shard_map/ppermute | solution.py:24
  277.7 13.6 %collective-permute-start.17 = (bf16[256,768]{1,0:T(8,128)(2,1)S(1)}, bf16[256,768]{1,0:T(8,128)(2,1)S(1)}, u32[]{:S(2)}, u32[]{:S(2)}) collective-permute-start(bf16[256,768]{1,0:T(8,128)(2,1)S(1)} %get-tuple-element.140), channel_id=1, source_target_pairs={{0,3},{1,0},{2,1},{3,2},{4,7},{5,4},{6,5},{7,6},{8,11},{9,8},{10,9... | collective-permute-start | bytes 1179656 | tf_op jit(solution)/shard_map/ppermute | solution.py:24
  280.1 28.1 %collective-permute-start.20 = (bf16[256,1536]{1,0:T(8,128)(2,1)}, bf16[256,1536]{1,0:T(8,128)(2,1)S(1)}, u32[]{:S(2)}, u32[]{:S(2)}) collective-permute-start(bf16[256,1536]{1,0:T(8,128)(2,1)} %get-tuple-element.116), channel_id=1, source_target_pairs={{0,64},{8,72},{16,80},{24,88},{32,96},{40,104},{48,112},{56,120},{... | collective-permute-start | bytes 2359304 | tf_op jit(solution)/shard_map/ppermute | solution.py:24
  286.0 12.6 %collective-permute-start.21 = (bf16[256,768]{1,0:T(8,128)(2,1)}, bf16[256,768]{1,0:T(8,128)(2,1)}, u32[]{:S(2)}, u32[]{:S(2)}) collective-permute-start(bf16[256,768]{1,0:T(8,128)(2,1)} %add_convert_fusion), channel_id=1, source_target_pairs={{0,4},{1,5},{2,6},{3,7},{4,0},{5,1},{6,2},{7,3},{8,12},{9,13},{10,... | collective-permute-start | bytes 1179656 | tf_op jit(solution)/shard_map/ppermute | solution.py:24
  291.3 3.5 %copy-start.5 = (bf16[256,1536]{1,0:T(8,128)(2,1)}, bf16[256,1536]{1,0:T(8,128)(2,1)S(1)}, u32[]{:S(2)}) copy-start(bf16[256,1536]{1,0:T(8,128)(2,1)S(1)} %collective-permute-done.18.refs_7_.refs_9_) | copy-start | bytes 2359300
  292.1 16.1 %collective-permute-start.19 = (bf16[256,768]{1,0:T(8,128)(2,1)S(1)}, bf16[256,768]{1,0:T(8,128)(2,1)S(1)}, u32[]{:S(2)}, u32[]{:S(2)}) collective-permute-start(bf16[256,768]{1,0:T(8,128)(2,1)S(1)} %add_convert_fusion.1), channel_id=1, source_target_pairs={{0,4},{1,5},{2,6},{3,7},{4,0},{5,1},{6,2},{7,3},{8,12},{9,13},{10,... | collective-permute-start | bytes 1179656 | tf_op jit(solution)/shard_map/ppermute | solution.py:24
  308.2 1.0 copy-start.21
  (3 other events, 2.6 us)
Sparse Core Ops, SparseCore 0:
  50.6 69.9 all-gather.1
  183.1 46.1 reduce-scatter.1

commit v4 on v3

--- a/solution.py
+++ b/solution.py
@@ -412,8 +412,9 @@
     m_other = over_owners(m_own)
     dg, du = hidden_grads(z, dy, down, p, s)
     send_back = input_grad(dg, du, gate_up)
-    send_back, m_other, dg, du = together((send_back, m_other, dg, du))
+    send_back, dg, du = together((send_back, dg, du))
     returned = over_experts(send_back)
+    dg, du, m_other = together((dg, du, m_other))
 
     gate = ring_grad(z, x, dg, "grad_gate")
     gate, du = together((gate, du))

time: 324 us -> 387 us (1.19)
  waiting for transfers between devices: 119 us -> 187 us
  starting transfers between devices: 78.4 us -> 72.2 us
    ppermute x22, waiting for transfers between devices: 85.9 us -> 157 us  [permuted(): lax.ppermute(value, axis, [(i, target(i)) for i in range(lax.axis_size(ax...]
    ppermute x22, starting transfers between devices: 50.2 us -> 41 us  [permuted(): lax.ppermute(value, axis, [(i, target(i)) for i in range(lax.axis_size(ax...]
  transfers between devices with their start and end apart: 27 -> 27, of which waited for: 12 -> 14; matrix products, arithmetic and copies ran while one was open for 5% -> 4% of each run, Pallas kernels for 23% -> 20%
where the time goes in v4:
time: 387 us; the launch traced here: 381 us
  waiting for transfers between devices  187 us (48%)
  Pallas kernels  86.3 us (22%)
  starting transfers between devices  72.2 us (19%)
  between operations  15 us (4%)
  other arithmetic  10.7 us (3%)
  local copies, waits for them, and re-layouts  10.3 us (3%)
    ppermute x22, waiting for transfers between devices, permuted(): lax.ppermute(value, axis, [(i, target(i)) for i in range(lax.axis_size(ax...  157 us
    ppermute x22, starting transfers between devices, permuted(): lax.ppermute(value, axis, [(i, target(i)) for i in range(lax.axis_size(ax...  41 us
    all_to_all x3, starting transfers between devices, over_experts(): lax.all_to_all(boxes, 'expert', split_axis=0, concat_axis=0, tiled=True)  31.2 us
    all_to_all x3, waiting for transfers between devices, over_experts(): lax.all_to_all(boxes, 'expert', split_axis=0, concat_axis=0, tiled=True)  29.4 us
    pallas_call x2, Pallas kernels, ring_grad(): pl.pallas_call(ring_kernel, grid_spec=pltpu.PrefetchScalarGridSpec(num_sc...  17.3 us
    pallas_call x1, Pallas kernels, forward(): pl.pallas_call(forward_kernel, grid=(hidden // tile,), in_specs=[pl.Block...  12.3 us
    pallas_call x3, Pallas kernels, adam(): pl.pallas_call(functools.partial(adam_kernel, len(sums)), grid_spec=pltpu...  11.7 us
    pallas_call x2, Pallas kernels, dispatch(): pl.pallas_call(dispatch_kernel, grid_spec=pltpu.PrefetchScalarGridSpec(nu...  11.6 us
  transfers between devices with their start and end apart: 27, of which 14 were waited for; matrix products, arithmetic and copies ran while one was open for 4% of the time, Pallas kernels for 20%

profile of v4, /device:TPU:1, one launch (start us, length us, event | category | flops | bytes accessed | tf_op | source)
XLA Modules:
  0.0 381.3 jit_solution(16626225442943039098)
XLA Ops:
  7.2 1.8 convert.5
  9.1 3.7 collective-permute-start
  14.0 15.5 %collective-permute-done.refs_7_ = bf16[256,1536]{1,0:T(8,128)(2,1)S(1)} collective-permute-done((bf16[256,1536]{1,0:T(8,128)(2,1)S(1)}, bf16[256,1536]{1,0:T(8,128)(2,1)S(1)}, u32[]{:S(2)}, u32[]{:S(2)}) %collective-permute-start) | collective-permute-done | bytes 786464 | tf_op jit(solution)/shard_map/ppermute | solution.py:24
  29.6 3.4 collective-permute-start.1
  34.5 2.8 collective-permute-start.2
  37.9 5.8 %dispatch.3 = bf16[1024,2048]{1,0:T(8,128)(2,1)} custom-call(s32[1]{0:T(128)} %bitcast.1.high_ref, s32[1,512]{1,0:T(1,128)} %bitcast_add_fusion.1.flat_ref, bf16[512,2048]{1,0:T(8,128)(2,1)} %bitcast.69), custom_call_target="tpu_custom_call" | custom-call | flops 2147483648 | bytes 6291456 | tf_op jit(solution)/shard_map/dispatch/pallas_call | solution.py:50
  44.9 4.3 %collective-permute-done.1 = bf16[256,1536]{1,0:T(8,128)(2,1)S(1)} collective-permute-done((bf16[256,1536]{1,0:T(8,128)(2,1)S(1)}, bf16[256,1536]{1,0:T(8,128)(2,1)S(1)}, u32[]{:S(2)}, u32[]{:S(2)}) %collective-permute-start.1) | collective-permute-done | bytes 786464 | tf_op jit(solution)/shard_map/ppermute | solution.py:24
  49.2 1.2 pad_maximum_fusion
  50.5 7.7 %all-to-all-start = ((bf16[16,64,2048]{2,1,0:T(8,128)(2,1)}), bf16[16,64,2048]{2,1,0:T(8,128)(2,1)}, u32[]{:S(2)}, u32[]{:S(2)}) async-start(bf16[16,64,2048]{2,1,0:T(8,128)(2,1)} %bitcast.64), calls=%async_computation | async-start | bytes 8388608 | tf_op jit(solution)/shard_map/all_to_all | solution.py:343
  58.2 2.7 collective-permute-start.3
  60.9 5.8 %dispatch.2 = bf16[1024,2048]{1,0:T(8,128)(2,1)} custom-call(s32[1]{0:T(128)} %bitcast.1.high_ref, s32[1,512]{1,0:T(1,128)} %bitcast_add_fusion.1.flat_ref, bf16[512,2048]{1,0:T(8,128)(2,1)} %bitcast.70), custom_call_target="tpu_custom_call" | custom-call | flops 2147483648 | bytes 6291456 | tf_op jit(solution)/shard_map/dispatch/pallas_call | solution.py:50
  66.7 37.8 %collective-permute-done.3 = bf16[256,768]{1,0:T(8,128)(2,1)S(1)} collective-permute-done((bf16[256,768]{1,0:T(8,128)(2,1)S(1)}, bf16[256,768]{1,0:T(8,128)(2,1)S(1)}, u32[]{:S(2)}, u32[]{:S(2)}) %collective-permute-start.3) | collective-permute-done | bytes 393248 | tf_op jit(solution)/shard_map/ppermute | solution.py:24
  104.6 6.5 %all-to-all-done = bf16[16,64,2048]{2,1,0:T(8,128)(2,1)} async-done(((bf16[16,64,2048]{2,1,0:T(8,128)(2,1)}), bf16[16,64,2048]{2,1,0:T(8,128)(2,1)}, u32[]{:S(2)}, u32[]{:S(2)}) %all-to-all-start) | async-done | bytes 4194336 | tf_op jit(solution)/shard_map/all_to_all | solution.py:343
  111.2 11.7 %all-to-all-start.1 = ((bf16[16,64,2048]{2,1,0:T(8,128)(2,1)}), bf16[16,64,2048]{2,1,0:T(8,128)(2,1)}, u32[]{:S(2)}, u32[]{:S(2)}) async-start(bf16[16,64,2048]{2,1,0:T(8,128)(2,1)} %bitcast.63), calls=%async_computation.1 | async-start | bytes 8388608 | tf_op jit(solution)/shard_map/all_to_all | solution.py:343
  123.1 1.4 copy-done.1
  124.7 1.5 collective-permute-start.4
  126.2 2.4 collective-permute-start.5
  129.7 12.3 %forward.1 = (bf16[1024,768]{1,0:T(8,128)(2,1)}, f32[1024,768]{1,0:T(8,128)}, f32[1024,768]{1,0:T(8,128)}) custom-call(bf16[1024,2048]{1,0:T(8,128)(2,1)} %bitcast.13.x_ref.first_ref.second_ref, bf16[2048,1536]{1,0:T(8,128)(2,1)} %all-gather.2.cloned.1.call-done.gate_ref.up_ref, bf16[2048,1536]{1,0:T(8,128)(2,1)} %all-gather.2.cloned.1.call-done.gate_ref.up_ref), custom_call_target="tpu_custom_call" | custom-call | flops 6442450944 | bytes 20000000 | tf_op jit(solution)/shard_map/forward/pallas_call | solution.py:116
  142.0 4.4 %collective-permute-done.4.last_ref = bf16[512,768]{1,0:T(8,128)(2,1)S(1)} collective-permute-done((bf16[512,768]{1,0:T(8,128)(2,1)S(1)}, bf16[512,768]{1,0:T(8,128)(2,1)S(1)}, u32[]{:S(2)}, u32[]{:S(2)}) %collective-permute-start.4) | collective-permute-done | bytes 786464 | tf_op jit(solution)/shard_map/ppermute | solution.py:24
  148.4 2.2 collective-permute-start.7
  152.7 22.9 %all-to-all-done.1 = bf16[16,64,2048]{2,1,0:T(8,128)(2,1)} async-done(((bf16[16,64,2048]{2,1,0:T(8,128)(2,1)}), bf16[16,64,2048]{2,1,0:T(8,128)(2,1)}, u32[]{:S(2)}, u32[]{:S(2)}) %all-to-all-start.1) | async-done | bytes 4194336 | tf_op jit(solution)/shard_map/all_to_all | solution.py:343
  175.6 7.4 %grad_down.1 = bf16[2048,768]{1,0:T(8,128)(2,1)} custom-call(s32[1]{0:T(128)} %constant.113.clone.1.shift_ref, bf16[1024,2048]{1,0:T(8,128)(2,1)} %bitcast.15.dy_ref.a_ref, bf16[1024,768]{1,0:T(8,128)(2,1)} %get-tuple-element.110.b_ref), custom_call_target="tpu_custom_call" | custom-call | flops 3221225472 | bytes 9000000 | tf_op jit(solution)/shard_map/grad_down/pallas_call | solution.py:181
  183.0 9.0 %hidden_grads.1 = (bf16[1024,768]{1,0:T(8,128)(2,1)}, bf16[1024,768]{1,0:T(8,128)(2,1)}) custom-call(s32[1]{0:T(128)} %bitcast.z_ref, bf16[1024,2048]{1,0:T(8,128)(2,1)} %bitcast.15.dy_ref.a_ref, bf16[512,768]{1,0:T(8,128)(2,1)} %copy-done.6, bf16[512,768]{1,0:T(8,128)(2,1)} %copy-done.12, bf16[512,768]{1,0:T(8,128)(2,1)} %copy-done.11, ...), custom_call_target="tpu_custom_call" | custom-call | flops 3221225472 | bytes 17000000 | tf_op jit(solution)/shard_map/hidden_grads/pallas_call | solution.py:156
  192.0 10.8 %input_grad.1 = bf16[1024,2048]{1,0:T(8,128)(2,1)} custom-call(bf16[1024,768]{1,0:T(8,128)(2,1)} %get-tuple-element.92.dg_ref.b_ref, bf16[1024,768]{1,0:T(8,128)(2,1)} %get-tuple-element.98.du_ref.b_ref, bf16[2048,1536]{1,0:T(8,128)(2,1)} %all-gather.2.cloned.1.call-done.gate_ref.up_ref, bf16[2048,1536]{1,0:T(8,128)(2,1)} %all-gather.2.cloned.1.call-done.gate_ref.up_ref), custom_call_target="tpu_custom_call" | custom-call | flops 6442450944 | bytes 14000000 | tf_op jit(solution)/shard_map/input_grad/pallas_call | solution.py:252
  202.8 11.8 %all-to-all-start.2 = ((bf16[16,64,2048]{2,1,0:T(8,128)(2,1)}), bf16[16,64,2048]{2,1,0:T(8,128)(2,1)}, u32[]{:S(2)}, u32[]{:S(2)}) async-start(bf16[16,64,2048]{2,1,0:T(8,128)(2,1)} %bitcast.62), calls=%async_computation.3 | async-start | bytes 8388608 | tf_op jit(solution)/shard_map/all_to_all | solution.py:343
  214.6 2.9 collective-permute-start.8
  218.2 70.9 %collective-permute-done.8.refs_6_.refs_8_ = bf16[256,1536]{1,0:T(8,128)(2,1)S(1)} collective-permute-done((bf16[256,1536]{1,0:T(8,128)(2,1)S(1)}, bf16[256,1536]{1,0:T(8,128)(2,1)S(1)}, u32[]{:S(2)}, u32[]{:S(2)}) %collective-permute-start.8) | collective-permute-done | bytes 786464 | tf_op jit(solution)/shard_map/ppermute | solution.py:24
  289.1 8.6 %grad_gate.1 = (bf16[512,768]{1,0:T(8,128)(2,1)}, bf16[512,768]{1,0:T(8,128)(2,1)}, bf16[512,768]{1,0:T(8,128)(2,1)}, bf16[512,768]{1,0:T(8,128)(2,1)}) custom-call(s32[8]{0:T(128)} %concatenate.19.block_ref, bf16[1024,2048]{1,0:T(8,128)(2,1)} %bitcast.13.x_ref.first_ref.second_ref, bf16[1024,2048]{1,0:T(8,128)(2,1)} %bitcast.13.x_ref.first_ref.second_ref, ...), custom_call_target="tpu_custom_call" | custom-call | flops 3221225472 | bytes 9000000 | tf_op jit(solution)/shard_map/grad_gate/pallas_call | solution.py:220
  297.7 1.6 collective-permute-start.11
  299.3 2.5 collective-permute-start.12
  301.8 8.7 %grad_up.1 = (bf16[512,768]{1,0:T(8,128)(2,1)}, bf16[512,768]{1,0:T(8,128)(2,1)}, bf16[512,768]{1,0:T(8,128)(2,1)}, bf16[512,768]{1,0:T(8,128)(2,1)}) custom-call(s32[8]{0:T(128)} %concatenate.19.block_ref, bf16[1024,2048]{1,0:T(8,128)(2,1)} %bitcast.13.x_ref.first_ref.second_ref, bf16[1024,2048]{1,0:T(8,128)(2,1)} %bitcast.13.x_ref.first_ref.second_ref, ...), custom_call_target="tpu_custom_call" | custom-call | flops 3221225472 | bytes 9000000 | tf_op jit(solution)/shard_map/grad_up/pallas_call | solution.py:220
  310.5 1.4 collective-permute-start.10
  311.9 7.0 %collective-permute-done.11 = bf16[512,768]{1,0:T(8,128)(2,1)S(1)} collective-permute-done((bf16[512,768]{1,0:T(8,128)(2,1)}, bf16[512,768]{1,0:T(8,128)(2,1)S(1)}, u32[]{:S(2)}, u32[]{:S(2)}) %collective-permute-start.11) | collective-permute-done | bytes 786464 | tf_op jit(solution)/shard_map/ppermute | solution.py:24
  320.4 2.4 collective-permute-start.14
  322.8 2.1 fusion.5
  324.9 2.5 collective-permute-start.15
  328.3 6.7 %collective-permute-done.10.refs_2_ = bf16[512,768]{1,0:T(8,128)(2,1)S(1)} collective-permute-done((bf16[512,768]{1,0:T(8,128)(2,1)}, bf16[512,768]{1,0:T(8,128)(2,1)S(1)}, u32[]{:S(2)}, u32[]{:S(2)}) %collective-permute-start.10) | collective-permute-done | bytes 786464 | tf_op jit(solution)/shard_map/ppermute | solution.py:24
  335.0 6.2 %combine.1 = bf16[512,2048]{1,0:T(8,128)(2,1)} custom-call(s32[1]{0:T(128)} %bitcast.1.high_ref, s32[512,1]{1,0:T(8,128)} %copy.21.flat_ref, bf16[1024,2048]{1,0:T(8,128)(2,1)} %bitcast.21.back_ref), custom_call_target="tpu_custom_call" | custom-call | flops 2147483648 | bytes 6291456 | tf_op jit(solution)/shard_map/combine/pallas_call | solution.py:81
  341.2 3.2 collective-permute-done.13.refs_1_
  344.9 2.4 collective-permute-start.17
  347.6 1.9 add_convert_fusion
  349.5 2.6 collective-permute-start.21
  352.6 2.4 collective-permute-done.16.refs_1_
  355.8 2.5 collective-permute-start.19
  358.3 3.8 adam.3
  362.1 4.0 %adam.4 = (f32[256,2304]{1,0:T(8,128)}, f32[256,2304]{1,0:T(8,128)}, f32[256,2304]{1,0:T(8,128)}) custom-call(s32[1]{0:T(128)} %bitcast.23.keep_ref, bf16[512,768]{1,0:T(8,128)(2,1)} %get-tuple-element.121.refs_0_, bf16[256,768]{1,0:T(8,128)(2,1)} %collective-permute-done.13.refs_1_, ...), custom_call_target="tpu_custom_call", output_to_operand_aliasing={{0}: (11, {}), {1}: (12, {}), {2}: (13, {})} | custom-call | flops 3932160 | bytes 6684672 | tf_op jit(solution)/shard_map/adam/pallas_call | solution.py:293
  366.1 3.4 collective-permute-done.20.refs_8_.refs_9_
  370.5 4.0 %adam.5 = (f32[256,2304]{1,0:T(8,128)}, f32[256,2304]{1,0:T(8,128)}, f32[256,2304]{1,0:T(8,128)}) custom-call(s32[1]{0:T(128)} %bitcast.23.keep_ref, bf16[512,768]{1,0:T(8,128)(2,1)} %get-tuple-element.113.refs_0_, bf16[256,768]{1,0:T(8,128)(2,1)} %copy-done.20, ...), custom_call_target="tpu_custom_call", output_to_operand_aliasing={{0}: (11, {}), {1}: (12, {}), {2}: (13, {})} | custom-call | flops 3932160 | bytes 6684672 | tf_op jit(solution)/shard_map/adam/pallas_call | solution.py:293
  (99 shorter events, 15.8 us)
Async XLA Ops:
  7.2 5.6 %copy-start.23 = (s32[16]{0:T(128)S(1)}, s32[16]{0:T(128)}, u32[]{:S(2)}) copy-start(s32[16]{0:T(128)} %param.10) | copy-start | bytes 196
  7.2 122.5 %all-gather.2.cloned.1.call-start = ((), (), s32[]{:S(2)}) async-start(), calls=%async_computation.4 | async-start | bytes 7864320 | tf_op jit(solution)/shard_map/all_gather | solution.py:347
  9.0 24.0 %copy-start.22 = (s32[1,512,1]{1,2,0:T(1,128)S(1)}, s32[1,512,1]{1,2,0:T(1,128)}, u32[]{:S(2)}) copy-start(s32[1,512,1]{1,2,0:T(1,128)} %param.9) | copy-start | bytes 6148
  9.1 20.4 %collective-permute-start = (bf16[256,1536]{1,0:T(8,128)(2,1)S(1)}, bf16[256,1536]{1,0:T(8,128)(2,1)S(1)}, u32[]{:S(2)}, u32[]{:S(2)}) collective-permute-start(bf16[256,1536]{1,0:T(8,128)(2,1)S(1)} %slice_bitcast_fusion), channel_id=1, source_target_pairs={{0,64},{8,72},{16,80},{24,88},{32,96},{40,104},{48,112},{56,120},{... | collective-permute-start | bytes 2359304 | tf_op jit(solution)/shard_map/ppermute | solution.py:24
  29.5 14.2 %copy-start.2 = (bf16[256,1536]{1,0:T(8,128)(2,1)}, bf16[256,1536]{1,0:T(8,128)(2,1)S(1)}, u32[]{:S(2)}) copy-start(bf16[256,1536]{1,0:T(8,128)(2,1)S(1)} %collective-permute-done.refs_7_) | copy-start | bytes 2359300
  29.6 19.6 %collective-permute-start.1 = (bf16[256,1536]{1,0:T(8,128)(2,1)S(1)}, bf16[256,1536]{1,0:T(8,128)(2,1)S(1)}, u32[]{:S(2)}, u32[]{:S(2)}) collective-permute-start(bf16[256,1536]{1,0:T(8,128)(2,1)S(1)} %broadcast_select_fusion), channel_id=1, source_target_pairs={{0,4},{1,5},{2,6},{3,7},{4,0},{5,1},{6,2},{7,3},{8,12},{9,13},{10,... | collective-permute-start | bytes 2359304 | tf_op jit(solution)/shard_map/ppermute | solution.py:24
  34.5 10.4 %collective-permute-start.2 = (bf16[256,768]{1,0:T(8,128)(2,1)S(1)}, bf16[256,768]{1,0:T(8,128)(2,1)S(1)}, u32[]{:S(2)}, u32[]{:S(2)}) collective-permute-start(bf16[256,768]{1,0:T(8,128)(2,1)S(1)} %slice_bitcast_fusion.1), channel_id=1, source_target_pairs={{0,64},{8,72},{16,80},{24,88},{32,96},{40,104},{48,112},{56,120},{... | collective-permute-start | bytes 1179656 | tf_op jit(solution)/shard_map/ppermute | solution.py:24
  44.9 13.3 %copy-start.13 = (bf16[256,768]{1,0:T(8,128)(2,1)}, bf16[256,768]{1,0:T(8,128)(2,1)S(1)}, u32[]{:S(2)}) copy-start(bf16[256,768]{1,0:T(8,128)(2,1)S(1)} %collective-permute-done.2.refs_5_) | copy-start | bytes 1179652
  50.5 60.7 %all-to-all-start = ((bf16[16,64,2048]{2,1,0:T(8,128)(2,1)}), bf16[16,64,2048]{2,1,0:T(8,128)(2,1)}, u32[]{:S(2)}, u32[]{:S(2)}) async-start(bf16[16,64,2048]{2,1,0:T(8,128)(2,1)} %bitcast.64), calls=%async_computation | async-start | bytes 8388608 | tf_op jit(solution)/shard_map/all_to_all | solution.py:343
  58.2 46.4 %collective-permute-start.3 = (bf16[256,768]{1,0:T(8,128)(2,1)S(1)}, bf16[256,768]{1,0:T(8,128)(2,1)S(1)}, u32[]{:S(2)}, u32[]{:S(2)}) collective-permute-start(bf16[256,768]{1,0:T(8,128)(2,1)S(1)} %broadcast_select_fusion.1), channel_id=1, source_target_pairs={{0,4},{1,5},{2,6},{3,7},{4,0},{5,1},{6,2},{7,3},{8,12},{9,13},{10,... | collective-permute-start | bytes 1179656 | tf_op jit(solution)/shard_map/ppermute | solution.py:24
  104.6 21.6 %copy-start.6 = (bf16[512,768]{1,0:T(8,128)(2,1)}, bf16[512,768]{1,0:T(8,128)(2,1)S(1)}, u32[]{:S(2)}) copy-start(bf16[512,768]{1,0:T(8,128)(2,1)S(1)} %pad_maximum_fusion.1.own_ref) | copy-start | bytes 2359300
  111.2 11.7 %copy-start = (f32[1,256,2304]{2,1,0:T(8,128)S(1)}, f32[1,256,2304]{2,1,0:T(8,128)}, u32[]{:S(2)}) copy-start(f32[1,256,2304]{2,1,0:T(8,128)} %param.12) | copy-start | bytes 7077892
  111.2 64.4 %all-to-all-start.1 = ((bf16[16,64,2048]{2,1,0:T(8,128)(2,1)}), bf16[16,64,2048]{2,1,0:T(8,128)(2,1)}, u32[]{:S(2)}, u32[]{:S(2)}) async-start(bf16[16,64,2048]{2,1,0:T(8,128)(2,1)} %bitcast.63), calls=%async_computation.1 | async-start | bytes 8388608 | tf_op jit(solution)/shard_map/all_to_all | solution.py:343
  122.9 199.9 %reduce-scatter.2.cloned.1.call-start = ((), (), s32[]{:S(2)}) async-start(), calls=%async_computation.5 | async-start | bytes 3932160 | tf_op jit(solution)/shard_map/reduce_scatter | solution.py:350
  122.9 1.7 copy-start.1
  124.7 21.7 %collective-permute-start.4 = (bf16[512,768]{1,0:T(8,128)(2,1)S(1)}, bf16[512,768]{1,0:T(8,128)(2,1)S(1)}, u32[]{:S(2)}, u32[]{:S(2)}) collective-permute-start(bf16[512,768]{1,0:T(8,128)(2,1)S(1)} %pad_maximum_fusion.1.own_ref), channel_id=1, source_target_pairs={{0,1},{1,2},{2,3},{3,0},{4,5},{5,6},{6,7},{7,4},{8,9},{9,10},{10,1... | collective-permute-start | bytes 2359304 | tf_op jit(solution)/shard_map/ppermute | solution.py:24
  126.2 20.2 %collective-permute-start.5 = (bf16[512,768]{1,0:T(8,128)(2,1)S(1)}, bf16[512,768]{1,0:T(8,128)(2,1)S(1)}, u32[]{:S(2)}, u32[]{:S(2)}) collective-permute-start(bf16[512,768]{1,0:T(8,128)(2,1)S(1)} %pad_maximum_fusion.1.own_ref), channel_id=1, source_target_pairs={{0,3},{1,0},{2,1},{3,2},{4,7},{5,4},{6,5},{7,6},{8,11},{9,8},{10,9... | collective-permute-start | bytes 2359304 | tf_op jit(solution)/shard_map/ppermute | solution.py:24
  129.7 21.0 %copy-start.15 = (bf16[256,768]{1,0:T(8,128)(2,1)S(1)}, bf16[256,768]{1,0:T(8,128)(2,1)}, u32[]{:S(2)}) copy-start(bf16[256,768]{1,0:T(8,128)(2,1)} %get-tuple-element.140) | copy-start | bytes 1179652
  129.7 21.0 %copy-start.16 = (bf16[256,768]{1,0:T(8,128)(2,1)S(1)}, bf16[256,768]{1,0:T(8,128)(2,1)}, u32[]{:S(2)}) copy-start(bf16[256,768]{1,0:T(8,128)(2,1)} %get-tuple-element.141) | copy-start | bytes 1179652
  142.0 9.7 %copy-start.14 = (bf16[256,768]{1,0:T(8,128)(2,1)S(1)}, bf16[256,768]{1,0:T(8,128)(2,1)}, u32[]{:S(2)}) copy-start(bf16[256,768]{1,0:T(8,128)(2,1)} %get-tuple-element.139) | copy-start | bytes 1179652
  146.4 6.3 %copy-start.11 = (bf16[512,768]{1,0:T(8,128)(2,1)}, bf16[512,768]{1,0:T(8,128)(2,1)S(1)}, u32[]{:S(2)}) copy-start(bf16[512,768]{1,0:T(8,128)(2,1)S(1)} %collective-permute-done.4.last_ref) | copy-start | bytes 2359300
  146.4 6.3 %copy-start.12 = (bf16[512,768]{1,0:T(8,128)(2,1)}, bf16[512,768]{1,0:T(8,128)(2,1)S(1)}, u32[]{:S(2)}) copy-start(bf16[512,768]{1,0:T(8,128)(2,1)S(1)} %collective-permute-done.5.next_ref) | copy-start | bytes 2359300
  147.2 28.4 %collective-permute-start.6 = (bf16[256,768]{1,0:T(8,128)(2,1)}, bf16[256,768]{1,0:T(8,128)(2,1)}, u32[]{:S(2)}, u32[]{:S(2)}) collective-permute-start(bf16[256,768]{1,0:T(8,128)(2,1)} %slice.92), channel_id=1, source_target_pairs={{0,1},{1,2},{2,3},{3,0},{4,5},{5,6},{6,7},{7,4},{8,9},{9,10},{10,1... | collective-permute-start | bytes 1179656 | tf_op jit(solution)/shard_map/ppermute | solution.py:24
  148.4 27.2 %collective-permute-start.7 = (bf16[256,768]{1,0:T(8,128)(2,1)}, bf16[256,768]{1,0:T(8,128)(2,1)}, u32[]{:S(2)}, u32[]{:S(2)}) collective-permute-start(bf16[256,768]{1,0:T(8,128)(2,1)} %slice.93), channel_id=1, source_target_pairs={{0,3},{1,0},{2,1},{3,2},{4,7},{5,4},{6,5},{7,6},{8,11},{9,8},{10,9... | collective-permute-start | bytes 1179656 | tf_op jit(solution)/shard_map/ppermute | solution.py:24
  202.8 132.1 %all-to-all-start.2 = ((bf16[16,64,2048]{2,1,0:T(8,128)(2,1)}), bf16[16,64,2048]{2,1,0:T(8,128)(2,1)}, u32[]{:S(2)}, u32[]{:S(2)}) async-start(bf16[16,64,2048]{2,1,0:T(8,128)(2,1)} %bitcast.62), calls=%async_computation.3 | async-start | bytes 8388608 | tf_op jit(solution)/shard_map/all_to_all | solution.py:343
  214.6 74.4 %collective-permute-start.8 = (bf16[256,1536]{1,0:T(8,128)(2,1)S(1)}, bf16[256,1536]{1,0:T(8,128)(2,1)S(1)}, u32[]{:S(2)}, u32[]{:S(2)}) collective-permute-start(bf16[256,1536]{1,0:T(8,128)(2,1)S(1)} %get-tuple-element.91), channel_id=1, source_target_pairs={{0,64},{8,72},{16,80},{24,88},{32,96},{40,104},{48,112},{56,120},{... | collective-permute-start | bytes 2359304 | tf_op jit(solution)/shard_map/ppermute | solution.py:24
  289.1 8.6 %copy-start.4 = (bf16[256,1536]{1,0:T(8,128)(2,1)}, bf16[256,1536]{1,0:T(8,128)(2,1)S(1)}, u32[]{:S(2)}) copy-start(bf16[256,1536]{1,0:T(8,128)(2,1)S(1)} %collective-permute-done.8.refs_6_.refs_8_) | copy-start | bytes 2359300
  297.7 21.3 %copy-start.18 = (bf16[512,768]{1,0:T(8,128)(2,1)S(1)}, bf16[512,768]{1,0:T(8,128)(2,1)}, u32[]{:S(2)}) copy-start(bf16[512,768]{1,0:T(8,128)(2,1)} %get-tuple-element.101) | copy-start | bytes 2359300
  297.7 21.3 %collective-permute-start.11 = (bf16[512,768]{1,0:T(8,128)(2,1)}, bf16[512,768]{1,0:T(8,128)(2,1)S(1)}, u32[]{:S(2)}, u32[]{:S(2)}) collective-permute-start(bf16[512,768]{1,0:T(8,128)(2,1)} %get-tuple-element.102), channel_id=1, source_target_pairs={{0,1},{1,2},{2,3},{3,0},{4,5},{5,6},{6,7},{7,4},{8,9},{9,10},{10,1... | collective-permute-start | bytes 2359304 | tf_op jit(solution)/shard_map/ppermute | solution.py:24
  299.3 19.6 %collective-permute-start.12 = (bf16[512,768]{1,0:T(8,128)(2,1)}, bf16[512,768]{1,0:T(8,128)(2,1)S(1)}, u32[]{:S(2)}, u32[]{:S(2)}) collective-permute-start(bf16[512,768]{1,0:T(8,128)(2,1)} %get-tuple-element.103), channel_id=1, source_target_pairs={{0,3},{1,0},{2,1},{3,2},{4,7},{5,4},{6,5},{7,6},{8,11},{9,8},{10,9... | collective-permute-start | bytes 2359304 | tf_op jit(solution)/shard_map/ppermute | solution.py:24
  310.5 24.5 %collective-permute-start.10 = (bf16[512,768]{1,0:T(8,128)(2,1)}, bf16[512,768]{1,0:T(8,128)(2,1)S(1)}, u32[]{:S(2)}, u32[]{:S(2)}) collective-permute-start(bf16[512,768]{1,0:T(8,128)(2,1)} %get-tuple-element.100), channel_id=1, source_target_pairs={{0,3},{1,0},{2,1},{3,2},{4,7},{5,4},{6,5},{7,6},{8,11},{9,8},{10,9... | collective-permute-start | bytes 2359304 | tf_op jit(solution)/shard_map/ppermute | solution.py:24
  311.8 29.3 %collective-permute-start.9 = (bf16[512,768]{1,0:T(8,128)(2,1)}, bf16[512,768]{1,0:T(8,128)(2,1)S(1)}, u32[]{:S(2)}, u32[]{:S(2)}) collective-permute-start(bf16[512,768]{1,0:T(8,128)(2,1)} %get-tuple-element.99), channel_id=1, source_target_pairs={{0,1},{1,2},{2,3},{3,0},{4,5},{5,6},{6,7},{7,4},{8,9},{9,10},{10,1... | collective-permute-start | bytes 2359304 | tf_op jit(solution)/shard_map/ppermute | solution.py:24
  319.0 9.3 %copy-start.8 = (bf16[512,768]{1,0:T(8,128)(2,1)}, bf16[512,768]{1,0:T(8,128)(2,1)S(1)}, u32[]{:S(2)}) copy-start(bf16[512,768]{1,0:T(8,128)(2,1)S(1)} %collective-permute-done.12.refs_2_) | copy-start | bytes 2359300
  320.1 24.2 %collective-permute-start.13 = (bf16[256,768]{1,0:T(8,128)(2,1)}, bf16[256,768]{1,0:T(8,128)(2,1)}, u32[]{:S(2)}, u32[]{:S(2)}) collective-permute-start(bf16[256,768]{1,0:T(8,128)(2,1)} %get-tuple-element.147), channel_id=1, source_target_pairs={{0,1},{1,2},{2,3},{3,0},{4,5},{5,6},{6,7},{7,4},{8,9},{9,10},{10,1... | collective-permute-start | bytes 1179656 | tf_op jit(solution)/shard_map/ppermute | solution.py:24
  320.4 24.0 %collective-permute-start.14 = (bf16[256,768]{1,0:T(8,128)(2,1)}, bf16[256,768]{1,0:T(8,128)(2,1)}, u32[]{:S(2)}, u32[]{:S(2)}) collective-permute-start(bf16[256,768]{1,0:T(8,128)(2,1)} %get-tuple-element.146), channel_id=1, source_target_pairs={{0,3},{1,0},{2,1},{3,2},{4,7},{5,4},{6,5},{7,6},{8,11},{9,8},{10,9... | collective-permute-start | bytes 1179656 | tf_op jit(solution)/shard_map/ppermute | solution.py:24
  324.9 19.5 %collective-permute-start.15 = (bf16[256,768]{1,0:T(8,128)(2,1)}, bf16[256,768]{1,0:T(8,128)(2,1)S(1)}, u32[]{:S(2)}, u32[]{:S(2)}) collective-permute-start(bf16[256,768]{1,0:T(8,128)(2,1)} %get-tuple-element.143), channel_id=1, source_target_pairs={{0,4},{1,5},{2,6},{3,7},{4,0},{5,1},{6,2},{7,3},{8,12},{9,13},{10,... | collective-permute-start | bytes 1179656 | tf_op jit(solution)/shard_map/ppermute | solution.py:24
  334.9 9.4 %copy-start.7 = (bf16[512,768]{1,0:T(8,128)(2,1)}, bf16[512,768]{1,0:T(8,128)(2,1)S(1)}, u32[]{:S(2)}) copy-start(bf16[512,768]{1,0:T(8,128)(2,1)S(1)} %collective-permute-done.10.refs_2_) | copy-start | bytes 2359300
  335.0 17.6 %collective-permute-start.18 = (bf16[256,1536]{1,0:T(8,128)(2,1)}, bf16[256,1536]{1,0:T(8,128)(2,1)S(1)}, u32[]{:S(2)}, u32[]{:S(2)}) collective-permute-start(bf16[256,1536]{1,0:T(8,128)(2,1)} %pad_maximum_fusion.3), channel_id=1, source_target_pairs={{0,64},{8,72},{16,80},{24,88},{32,96},{40,104},{48,112},{56,120},{... | collective-permute-start | bytes 2359304 | tf_op jit(solution)/shard_map/ppermute | solution.py:24
  335.0 9.4 %copy-start.17 = (bf16[512,768]{1,0:T(8,128)(2,1)S(1)}, bf16[512,768]{1,0:T(8,128)(2,1)}, u32[]{:S(2)}) copy-start(bf16[512,768]{1,0:T(8,128)(2,1)} %get-tuple-element.114) | copy-start | bytes 2359300
  341.2 6.5 %copy-start.10 = (bf16[512,768]{1,0:T(8,128)(2,1)S(1)}, bf16[512,768]{1,0:T(8,128)(2,1)}, u32[]{:S(2)}) copy-start(bf16[512,768]{1,0:T(8,128)(2,1)} %get-tuple-element.121.refs_0_) | copy-start | bytes 2359300
  341.2 13.8 %copy-start.9 = (bf16[512,768]{1,0:T(8,128)(2,1)S(1)}, bf16[512,768]{1,0:T(8,128)(2,1)}, u32[]{:S(2)}) copy-start(bf16[512,768]{1,0:T(8,128)(2,1)} %get-tuple-element.113.refs_0_) | copy-start | bytes 2359300
  344.4 10.8 %copy-start.19 = (bf16[256,768]{1,0:T(8,128)(2,1)}, bf16[256,768]{1,0:T(8,128)(2,1)S(1)}, u32[]{:S(2)}) copy-start(bf16[256,768]{1,0:T(8,128)(2,1)S(1)} %collective-permute-done.15.refs_1_) | copy-start | bytes 1179652
  344.6 10.4 %collective-permute-start.16 = (bf16[256,768]{1,0:T(8,128)(2,1)S(1)}, bf16[256,768]{1,0:T(8,128)(2,1)S(1)}, u32[]{:S(2)}, u32[]{:S(2)}) collective-permute-start(bf16[256,768]{1,0:T(8,128)(2,1)S(1)} %get-tuple-element.145), channel_id=1, source_target_pairs={{0,1},{1,2},{2,3},{3,0},{4,5},{5,6},{6,7},{7,4},{8,9},{9,10},{10,1... | collective-permute-start | bytes 1179656 | tf_op jit(solution)/shard_map/ppermute | solution.py:24
  344.9 10.1 %collective-permute-start.17 = (bf16[256,768]{1,0:T(8,128)(2,1)S(1)}, bf16[256,768]{1,0:T(8,128)(2,1)S(1)}, u32[]{:S(2)}, u32[]{:S(2)}) collective-permute-start(bf16[256,768]{1,0:T(8,128)(2,1)S(1)} %get-tuple-element.144), channel_id=1, source_target_pairs={{0,3},{1,0},{2,1},{3,2},{4,7},{5,4},{6,5},{7,6},{8,11},{9,8},{10,9... | collective-permute-start | bytes 1179656 | tf_op jit(solution)/shard_map/ppermute | solution.py:24
  347.3 22.1 %collective-permute-start.20 = (bf16[256,1536]{1,0:T(8,128)(2,1)}, bf16[256,1536]{1,0:T(8,128)(2,1)S(1)}, u32[]{:S(2)}, u32[]{:S(2)}) collective-permute-start(bf16[256,1536]{1,0:T(8,128)(2,1)} %get-tuple-element.120), channel_id=1, source_target_pairs={{0,64},{8,72},{16,80},{24,88},{32,96},{40,104},{48,112},{56,120},{... | collective-permute-start | bytes 2359304 | tf_op jit(solution)/shard_map/ppermute | solution.py:24
  349.5 12.6 %collective-permute-start.21 = (bf16[256,768]{1,0:T(8,128)(2,1)}, bf16[256,768]{1,0:T(8,128)(2,1)}, u32[]{:S(2)}, u32[]{:S(2)}) collective-permute-start(bf16[256,768]{1,0:T(8,128)(2,1)} %add_convert_fusion), channel_id=1, source_target_pairs={{0,4},{1,5},{2,6},{3,7},{4,0},{5,1},{6,2},{7,3},{8,12},{9,13},{10,... | collective-permute-start | bytes 1179656 | tf_op jit(solution)/shard_map/ppermute | solution.py:24
  352.6 5.8 %copy-start.5 = (bf16[256,1536]{1,0:T(8,128)(2,1)}, bf16[256,1536]{1,0:T(8,128)(2,1)S(1)}, u32[]{:S(2)}) copy-start(bf16[256,1536]{1,0:T(8,128)(2,1)S(1)} %collective-permute-done.18.refs_7_.refs_9_) | copy-start | bytes 2359300
  355.8 13.7 %collective-permute-start.19 = (bf16[256,768]{1,0:T(8,128)(2,1)S(1)}, bf16[256,768]{1,0:T(8,128)(2,1)S(1)}, u32[]{:S(2)}, u32[]{:S(2)}) collective-permute-start(bf16[256,768]{1,0:T(8,128)(2,1)S(1)} %add_convert_fusion.1), channel_id=1, source_target_pairs={{0,4},{1,5},{2,6},{3,7},{4,0},{5,1},{6,2},{7,3},{8,12},{9,13},{10,... | collective-permute-start | bytes 1179656 | tf_op jit(solution)/shard_map/ppermute | solution.py:24
  (3 other events, 2.7 us)
Sparse Core Ops, SparseCore 0:
  50.6 69.9 all-gather.1
  183.1 46.1 reduce-scatter.1

commit v5 on v3

--- a/solution.py
+++ b/solution.py
@@ -170,30 +170,27 @@
     )(z, dy, *down, p, s)
 
 
-def weight_kernel(shift_ref, a_ref, b_ref, out_ref):
+def weight_kernel(a_ref, b_ref, out_ref):
     out_ref[...] = mm(a_ref[...], b_ref[...], ((0,), (0,))).astype(BF)
 
 
-def weight_grad(shift, a, b, name):
+def weight_grad(a, b, name):
     rows, features = a.shape
     hidden = b.shape[1]
-    tile = features // ZN
+    tile = features // 2
     return pl.pallas_call(
         weight_kernel,
-        grid_spec=pltpu.PrefetchScalarGridSpec(
-            num_scalar_prefetch=1,
-            grid=(ZN,),
-            in_specs=[
-                pl.BlockSpec((rows, tile), lambda i, shift: (0, (i + shift[0]) % ZN)),
-                pl.BlockSpec((rows, hidden), lambda i, shift: (0, 0)),
-            ],
-            out_specs=pl.BlockSpec((tile, hidden), lambda i, shift: (i, 0)),
-        ),
+        grid=(features // tile,),
+        in_specs=[
+            pl.BlockSpec((rows, tile), lambda i: (0, i)),
+            pl.BlockSpec((rows, hidden), lambda i: (0, 0)),
+        ],
+        out_specs=pl.BlockSpec((tile, hidden), lambda i: (i, 0)),
         out_shape=jax.ShapeDtypeStruct((features, hidden), BF),
         compiler_params=params(),
         cost_estimate=cost(2 * rows * features * hidden, 9e6),
         name=name,
-    )(shift, a, b)
+    )(a, b)
 
 
 def ring_kernel(block_ref, first_ref, second_ref, b_ref, *out_refs):
@@ -358,7 +355,6 @@
         return permuted(value, "dp", lambda i: i // ZN * ZN + (i - 1) % ZN)
 
     z = (lax.axis_index("dp") % ZN).astype(jnp.int32).reshape(1)
-    nought = jnp.zeros((1,), jnp.int32)
 
     split = 2 * hidden
     own_a, own_b = master[0, :, :split].astype(BF), master[0, :, split:].astype(BF)
@@ -408,7 +404,7 @@
     ]
     dy, m_own, *others = together((dy, m_own, *v_own, *down[3:]))
     v_own, down = others[:2], (*down[:3], *others[2:])
-    part_down = scattered(weight_grad(nought, dy, h, "grad_down")).reshape(2, -1, hidden)
+    part_down = scattered(weight_grad(dy, h, "grad_down")).reshape(2, -1, hidden)
     m_other = over_owners(m_own)
     dg, du = hidden_grads(z, dy, down, p, s)
     send_back = input_grad(dg, du, gate_up)

time: 324 us -> 323 us (level)
  no operation moved by 1% of the time
where the time goes in v5:
time: 323 us; the launch traced here: 320 us
  waiting for transfers between devices  119 us (37%)
  Pallas kernels  85.7 us (27%)
  starting transfers between devices  78.6 us (24%)
  between operations  15 us (5%)
  local copies, waits for them, and re-layouts  11.2 us (3%)
  other arithmetic  10.7 us (3%)
    ppermute x22, waiting for transfers between devices, permuted(): lax.ppermute(value, axis, [(i, target(i)) for i in range(lax.axis_size(ax...  85.9 us
    ppermute x22, starting transfers between devices, permuted(): lax.ppermute(value, axis, [(i, target(i)) for i in range(lax.axis_size(ax...  50.5 us
    all_to_all x3, waiting for transfers between devices, over_experts(): lax.all_to_all(boxes, 'expert', split_axis=0, concat_axis=0, tiled=True)  32.6 us
    all_to_all x3, starting transfers between devices, over_experts(): lax.all_to_all(boxes, 'expert', split_axis=0, concat_axis=0, tiled=True)  28.1 us
    pallas_call x2, Pallas kernels, ring_grad(): pl.pallas_call(ring_kernel, grid_spec=pltpu.PrefetchScalarGridSpec(num_sc...  17.4 us
    pallas_call x1, Pallas kernels, forward(): pl.pallas_call(forward_kernel, grid=(hidden // tile,), in_specs=[pl.Block...  12.3 us
    pallas_call x3, Pallas kernels, adam(): pl.pallas_call(functools.partial(adam_kernel, len(sums)), grid_spec=pltpu...  11.7 us
    pallas_call x2, Pallas kernels, dispatch(): pl.pallas_call(dispatch_kernel, grid_spec=pltpu.PrefetchScalarGridSpec(nu...  11.6 us
  transfers between devices with their start and end apart: 27, of which 12 were waited for; matrix products, arithmetic and copies ran while one was open for 5% of the time, Pallas kernels for 23%

profile of v5, /device:TPU:1, one launch (start us, length us, event | category | flops | bytes accessed | tf_op | source)
XLA Modules:
  0.0 319.8 jit_solution(5315760915498621355)
XLA Ops:
  7.2 1.8 convert.5
  9.1 3.7 %collective-permute-start = (bf16[256,1536]{1,0:T(8,128)(2,1)S(1)}, bf16[256,1536]{1,0:T(8,128)(2,1)S(1)}, u32[]{:S(2)}, u32[]{:S(2)}) collective-permute-start(bf16[256,1536]{1,0:T(8,128)(2,1)S(1)} %slice_bitcast_fusion), channel_id=1, source_target_pairs={{0,64},{8,72},{16,80},{24,88},{32,96},{40,104},{48,112},{56,120},{... | collective-permute-start | bytes 2359304 | tf_op jit(solution)/shard_map/ppermute | solution.py:24
  14.0 15.5 %collective-permute-done.refs_7_ = bf16[256,1536]{1,0:T(8,128)(2,1)S(1)} collective-permute-done((bf16[256,1536]{1,0:T(8,128)(2,1)S(1)}, bf16[256,1536]{1,0:T(8,128)(2,1)S(1)}, u32[]{:S(2)}, u32[]{:S(2)}) %collective-permute-start) | collective-permute-done | bytes 786464 | tf_op jit(solution)/shard_map/ppermute | solution.py:24
  29.6 3.4 %collective-permute-start.1 = (bf16[256,1536]{1,0:T(8,128)(2,1)S(1)}, bf16[256,1536]{1,0:T(8,128)(2,1)S(1)}, u32[]{:S(2)}, u32[]{:S(2)}) collective-permute-start(bf16[256,1536]{1,0:T(8,128)(2,1)S(1)} %broadcast_select_fusion), channel_id=1, source_target_pairs={{0,4},{1,5},{2,6},{3,7},{4,0},{5,1},{6,2},{7,3},{8,12},{9,13},{10,... | collective-permute-start | bytes 2359304 | tf_op jit(solution)/shard_map/ppermute | solution.py:24
  34.5 2.8 collective-permute-start.2
  37.9 5.8 %dispatch.3 = bf16[1024,2048]{1,0:T(8,128)(2,1)} custom-call(s32[1]{0:T(128)} %bitcast.1.high_ref, s32[1,512]{1,0:T(1,128)} %bitcast_add_fusion.1.flat_ref, bf16[512,2048]{1,0:T(8,128)(2,1)} %bitcast.69), custom_call_target="tpu_custom_call" | custom-call | flops 2147483648 | bytes 6291456 | tf_op jit(solution)/shard_map/dispatch/pallas_call | solution.py:50
  44.9 4.3 %collective-permute-done.1 = bf16[256,1536]{1,0:T(8,128)(2,1)S(1)} collective-permute-done((bf16[256,1536]{1,0:T(8,128)(2,1)S(1)}, bf16[256,1536]{1,0:T(8,128)(2,1)S(1)}, u32[]{:S(2)}, u32[]{:S(2)}) %collective-permute-start.1) | collective-permute-done | bytes 786464 | tf_op jit(solution)/shard_map/ppermute | solution.py:24
  50.5 7.7 %all-to-all-start = ((bf16[16,64,2048]{2,1,0:T(8,128)(2,1)}), bf16[16,64,2048]{2,1,0:T(8,128)(2,1)}, u32[]{:S(2)}, u32[]{:S(2)}) async-start(bf16[16,64,2048]{2,1,0:T(8,128)(2,1)} %bitcast.64), calls=%async_computation | async-start | bytes 8388608 | tf_op jit(solution)/shard_map/all_to_all | solution.py:340
  58.2 2.7 collective-permute-start.3
  60.9 5.8 %dispatch.2 = bf16[1024,2048]{1,0:T(8,128)(2,1)} custom-call(s32[1]{0:T(128)} %bitcast.1.high_ref, s32[1,512]{1,0:T(1,128)} %bitcast_add_fusion.1.flat_ref, bf16[512,2048]{1,0:T(8,128)(2,1)} %bitcast.70), custom_call_target="tpu_custom_call" | custom-call | flops 2147483648 | bytes 6291456 | tf_op jit(solution)/shard_map/dispatch/pallas_call | solution.py:50
  66.7 37.8 %collective-permute-done.3 = bf16[256,768]{1,0:T(8,128)(2,1)S(1)} collective-permute-done((bf16[256,768]{1,0:T(8,128)(2,1)S(1)}, bf16[256,768]{1,0:T(8,128)(2,1)S(1)}, u32[]{:S(2)}, u32[]{:S(2)}) %collective-permute-start.3) | collective-permute-done | bytes 393248 | tf_op jit(solution)/shard_map/ppermute | solution.py:24
  104.6 6.5 %all-to-all-done = bf16[16,64,2048]{2,1,0:T(8,128)(2,1)} async-done(((bf16[16,64,2048]{2,1,0:T(8,128)(2,1)}), bf16[16,64,2048]{2,1,0:T(8,128)(2,1)}, u32[]{:S(2)}, u32[]{:S(2)}) %all-to-all-start) | async-done | bytes 4194336 | tf_op jit(solution)/shard_map/all_to_all | solution.py:340
  111.2 11.7 %all-to-all-start.1 = ((bf16[16,64,2048]{2,1,0:T(8,128)(2,1)}), bf16[16,64,2048]{2,1,0:T(8,128)(2,1)}, u32[]{:S(2)}, u32[]{:S(2)}) async-start(bf16[16,64,2048]{2,1,0:T(8,128)(2,1)} %bitcast.63), calls=%async_computation.1 | async-start | bytes 8388608 | tf_op jit(solution)/shard_map/all_to_all | solution.py:340
  123.1 1.4 copy-done.1
  124.7 1.5 collective-permute-start.4
  126.2 2.4 collective-permute-start.5
  129.7 12.3 %forward.1 = (bf16[1024,768]{1,0:T(8,128)(2,1)}, f32[1024,768]{1,0:T(8,128)}, f32[1024,768]{1,0:T(8,128)}) custom-call(bf16[1024,2048]{1,0:T(8,128)(2,1)} %bitcast.13.x_ref.first_ref.second_ref, bf16[2048,1536]{1,0:T(8,128)(2,1)} %all-gather.2.cloned.1.call-done.gate_ref.up_ref, bf16[2048,1536]{1,0:T(8,128)(2,1)} %all-gather.2.cloned.1.call-done.gate_ref.up_ref), custom_call_target="tpu_custom_call" | custom-call | flops 6442450944 | bytes 20000000 | tf_op jit(solution)/shard_map/forward/pallas_call | solution.py:116
  142.0 4.4 %collective-permute-done.4.last_ref = bf16[512,768]{1,0:T(8,128)(2,1)S(1)} collective-permute-done((bf16[512,768]{1,0:T(8,128)(2,1)S(1)}, bf16[512,768]{1,0:T(8,128)(2,1)S(1)}, u32[]{:S(2)}, u32[]{:S(2)}) %collective-permute-start.4) | collective-permute-done | bytes 786464 | tf_op jit(solution)/shard_map/ppermute | solution.py:24
  148.4 2.2 collective-permute-start.7
  152.7 22.9 %all-to-all-done.1 = bf16[16,64,2048]{2,1,0:T(8,128)(2,1)} async-done(((bf16[16,64,2048]{2,1,0:T(8,128)(2,1)}), bf16[16,64,2048]{2,1,0:T(8,128)(2,1)}, u32[]{:S(2)}, u32[]{:S(2)}) %all-to-all-start.1) | async-done | bytes 4194336 | tf_op jit(solution)/shard_map/all_to_all | solution.py:340
  175.6 7.0 %grad_down.1 = bf16[2048,768]{1,0:T(8,128)(2,1)} custom-call(bf16[1024,2048]{1,0:T(8,128)(2,1)} %bitcast.15.dy_ref.a_ref, bf16[1024,768]{1,0:T(8,128)(2,1)} %get-tuple-element.106.b_ref), custom_call_target="tpu_custom_call" | custom-call | flops 3221225472 | bytes 9000000 | tf_op jit(solution)/shard_map/grad_down/pallas_call | solution.py:181
  182.6 4.5 %collective-permute-start.8 = (bf16[256,1536]{1,0:T(8,128)(2,1)S(1)}, bf16[256,1536]{1,0:T(8,128)(2,1)S(1)}, u32[]{:S(2)}, u32[]{:S(2)}) collective-permute-start(bf16[256,1536]{1,0:T(8,128)(2,1)S(1)} %get-tuple-element.87), channel_id=1, source_target_pairs={{0,64},{8,72},{16,80},{24,88},{32,96},{40,104},{48,112},{56,120},{... | collective-permute-start | bytes 2359304 | tf_op jit(solution)/shard_map/ppermute | solution.py:24
  187.1 9.0 %hidden_grads.1 = (bf16[1024,768]{1,0:T(8,128)(2,1)}, bf16[1024,768]{1,0:T(8,128)(2,1)}) custom-call(s32[1]{0:T(128)} %bitcast.z_ref, bf16[1024,2048]{1,0:T(8,128)(2,1)} %bitcast.15.dy_ref.a_ref, bf16[512,768]{1,0:T(8,128)(2,1)} %copy-done.6, bf16[512,768]{1,0:T(8,128)(2,1)} %copy-done.12, bf16[512,768]{1,0:T(8,128)(2,1)} %copy-done.11, ...), custom_call_target="tpu_custom_call" | custom-call | flops 3221225472 | bytes 17000000 | tf_op jit(solution)/shard_map/hidden_grads/pallas_call | solution.py:156
  196.1 10.8 %input_grad.1 = bf16[1024,2048]{1,0:T(8,128)(2,1)} custom-call(bf16[1024,768]{1,0:T(8,128)(2,1)} %get-tuple-element.88.dg_ref.b_ref, bf16[1024,768]{1,0:T(8,128)(2,1)} %get-tuple-element.94.du_ref.b_ref, bf16[2048,1536]{1,0:T(8,128)(2,1)} %all-gather.2.cloned.1.call-done.gate_ref.up_ref, bf16[2048,1536]{1,0:T(8,128)(2,1)} %all-gather.2.cloned.1.call-done.gate_ref.up_ref), custom_call_target="tpu_custom_call" | custom-call | flops 6442450944 | bytes 14000000 | tf_op jit(solution)/shard_map/input_grad/pallas_call | solution.py:249
  207.8 8.7 %all-to-all-start.2 = ((bf16[16,64,2048]{2,1,0:T(8,128)(2,1)}), bf16[16,64,2048]{2,1,0:T(8,128)(2,1)}, u32[]{:S(2)}, u32[]{:S(2)}) async-start(bf16[16,64,2048]{2,1,0:T(8,128)(2,1)} %bitcast.62), calls=%async_computation.3 | async-start | bytes 8388608 | tf_op jit(solution)/shard_map/all_to_all | solution.py:340
  217.1 8.7 %grad_gate.1 = (bf16[512,768]{1,0:T(8,128)(2,1)}, bf16[512,768]{1,0:T(8,128)(2,1)}, bf16[512,768]{1,0:T(8,128)(2,1)}, bf16[512,768]{1,0:T(8,128)(2,1)}) custom-call(s32[8]{0:T(128)} %concatenate.19.block_ref, bf16[1024,2048]{1,0:T(8,128)(2,1)} %bitcast.13.x_ref.first_ref.second_ref, bf16[1024,2048]{1,0:T(8,128)(2,1)} %bitcast.13.x_ref.first_ref.second_ref, ...), custom_call_target="tpu_custom_call" | custom-call | flops 3221225472 | bytes 9000000 | tf_op jit(solution)/shard_map/grad_gate/pallas_call | solution.py:217
  227.2 2.4 collective-permute-start.12
  229.6 8.7 %grad_up.1 = (bf16[512,768]{1,0:T(8,128)(2,1)}, bf16[512,768]{1,0:T(8,128)(2,1)}, bf16[512,768]{1,0:T(8,128)(2,1)}, bf16[512,768]{1,0:T(8,128)(2,1)}) custom-call(s32[8]{0:T(128)} %concatenate.19.block_ref, bf16[1024,2048]{1,0:T(8,128)(2,1)} %bitcast.13.x_ref.first_ref.second_ref, bf16[1024,2048]{1,0:T(8,128)(2,1)} %bitcast.13.x_ref.first_ref.second_ref, ...), custom_call_target="tpu_custom_call" | custom-call | flops 3221225472 | bytes 9000000 | tf_op jit(solution)/shard_map/grad_up/pallas_call | solution.py:217
  238.3 1.4 collective-permute-start.10
  239.8 7.7 %collective-permute-done.11 = bf16[512,768]{1,0:T(8,128)(2,1)S(1)} collective-permute-done((bf16[512,768]{1,0:T(8,128)(2,1)}, bf16[512,768]{1,0:T(8,128)(2,1)S(1)}, u32[]{:S(2)}, u32[]{:S(2)}) %collective-permute-start.11) | collective-permute-done | bytes 786464 | tf_op jit(solution)/shard_map/ppermute | solution.py:24
  249.1 2.2 collective-permute-start.14
  251.3 2.1 fusion.5
  253.4 2.7 collective-permute-start.15
  256.9 6.6 %collective-permute-done.10.refs_2_ = bf16[512,768]{1,0:T(8,128)(2,1)S(1)} collective-permute-done((bf16[512,768]{1,0:T(8,128)(2,1)}, bf16[512,768]{1,0:T(8,128)(2,1)S(1)}, u32[]{:S(2)}, u32[]{:S(2)}) %collective-permute-start.10) | collective-permute-done | bytes 786464 | tf_op jit(solution)/shard_map/ppermute | solution.py:24
  263.6 2.8 collective-permute-start.18
  266.3 3.2 all-to-all-done.2
  269.5 6.0 %combine.1 = bf16[512,2048]{1,0:T(8,128)(2,1)} custom-call(s32[1]{0:T(128)} %bitcast.1.high_ref, s32[512,1]{1,0:T(8,128)} %copy.21.flat_ref, bf16[1024,2048]{1,0:T(8,128)(2,1)} %bitcast.21.back_ref), custom_call_target="tpu_custom_call" | custom-call | flops 2147483648 | bytes 6291456 | tf_op jit(solution)/shard_map/combine/pallas_call | solution.py:81
  275.8 1.7 collective-permute-start.16
  277.4 2.4 collective-permute-start.17
  279.8 4.0 %collective-permute-start.20 = (bf16[256,1536]{1,0:T(8,128)(2,1)}, bf16[256,1536]{1,0:T(8,128)(2,1)S(1)}, u32[]{:S(2)}, u32[]{:S(2)}) collective-permute-start(bf16[256,1536]{1,0:T(8,128)(2,1)} %get-tuple-element.116), channel_id=1, source_target_pairs={{0,64},{8,72},{16,80},{24,88},{32,96},{40,104},{48,112},{56,120},{... | collective-permute-start | bytes 2359304 | tf_op jit(solution)/shard_map/ppermute | solution.py:24
  283.9 1.9 add_convert_fusion
  285.8 2.6 collective-permute-start.21
  288.4 2.7 collective-permute-done.18.refs_7_.refs_9_
  291.9 2.8 collective-permute-start.19
  294.6 3.8 %adam.3 = (f32[256,2304]{1,0:T(8,128)}, f32[256,2304]{1,0:T(8,128)}, f32[256,2304]{1,0:T(8,128)}) custom-call(s32[1]{0:T(128)} %bitcast.23.keep_ref, bf16[256,768]{1,0:T(8,128)(2,1)} %get-tuple-element.138.refs_0_, bf16[256,768]{1,0:T(8,128)(2,1)} %copy-done.19, f32[256,2304]{1,0:T(8,128)} %bitcast.50, f32[256,2304]{1,0:T(8,128)} %bitcast.53, ...), custom_call_target="tpu_custom_call" | custom-call | flops 3932160 | bytes 6684672 | tf_op jit(solution)/shard_map/adam/pallas_call | solution.py:290
  298.4 4.0 %adam.4 = (f32[256,2304]{1,0:T(8,128)}, f32[256,2304]{1,0:T(8,128)}, f32[256,2304]{1,0:T(8,128)}) custom-call(s32[1]{0:T(128)} %bitcast.23.keep_ref, bf16[512,768]{1,0:T(8,128)(2,1)} %get-tuple-element.117.refs_0_, bf16[256,768]{1,0:T(8,128)(2,1)} %collective-permute-done.13.refs_1_, ...), custom_call_target="tpu_custom_call", output_to_operand_aliasing={{0}: (11, {}), {1}: (12, {}), {2}: (13, {})} | custom-call | flops 3932160 | bytes 6684672 | tf_op jit(solution)/shard_map/adam/pallas_call | solution.py:290
  302.4 5.6 %collective-permute-done.20.refs_8_.refs_9_ = bf16[256,1536]{1,0:T(8,128)(2,1)S(1)} collective-permute-done((bf16[256,1536]{1,0:T(8,128)(2,1)}, bf16[256,1536]{1,0:T(8,128)(2,1)S(1)}, u32[]{:S(2)}, u32[]{:S(2)}) %collective-permute-start.20) | collective-permute-done | bytes 786464 | tf_op jit(solution)/shard_map/ppermute | solution.py:24
  309.0 4.0 %adam.5 = (f32[256,2304]{1,0:T(8,128)}, f32[256,2304]{1,0:T(8,128)}, f32[256,2304]{1,0:T(8,128)}) custom-call(s32[1]{0:T(128)} %bitcast.23.keep_ref, bf16[512,768]{1,0:T(8,128)(2,1)} %get-tuple-element.109.refs_0_, bf16[256,768]{1,0:T(8,128)(2,1)} %copy-done.20, ...), custom_call_target="tpu_custom_call", output_to_operand_aliasing={{0}: (11, {}), {1}: (12, {}), {2}: (13, {})} | custom-call | flops 3932160 | bytes 6684672 | tf_op jit(solution)/shard_map/adam/pallas_call | solution.py:290
  (99 shorter events, 18.3 us)
Async XLA Ops:
  7.2 5.6 %copy-start.23 = (s32[16]{0:T(128)S(1)}, s32[16]{0:T(128)}, u32[]{:S(2)}) copy-start(s32[16]{0:T(128)} %param.10) | copy-start | bytes 196
  7.2 122.5 %all-gather.2.cloned.1.call-start = ((), (), s32[]{:S(2)}) async-start(), calls=%async_computation.4 | async-start | bytes 7864320 | tf_op jit(solution)/shard_map/all_gather | solution.py:344
  9.0 24.0 %copy-start.22 = (s32[1,512,1]{1,2,0:T(1,128)S(1)}, s32[1,512,1]{1,2,0:T(1,128)}, u32[]{:S(2)}) copy-start(s32[1,512,1]{1,2,0:T(1,128)} %param.9) | copy-start | bytes 6148
  9.1 20.4 %collective-permute-start = (bf16[256,1536]{1,0:T(8,128)(2,1)S(1)}, bf16[256,1536]{1,0:T(8,128)(2,1)S(1)}, u32[]{:S(2)}, u32[]{:S(2)}) collective-permute-start(bf16[256,1536]{1,0:T(8,128)(2,1)S(1)} %slice_bitcast_fusion), channel_id=1, source_target_pairs={{0,64},{8,72},{16,80},{24,88},{32,96},{40,104},{48,112},{56,120},{... | collective-permute-start | bytes 2359304 | tf_op jit(solution)/shard_map/ppermute | solution.py:24
  29.5 14.2 %copy-start.2 = (bf16[256,1536]{1,0:T(8,128)(2,1)}, bf16[256,1536]{1,0:T(8,128)(2,1)S(1)}, u32[]{:S(2)}) copy-start(bf16[256,1536]{1,0:T(8,128)(2,1)S(1)} %collective-permute-done.refs_7_) | copy-start | bytes 2359300
  29.6 19.6 %collective-permute-start.1 = (bf16[256,1536]{1,0:T(8,128)(2,1)S(1)}, bf16[256,1536]{1,0:T(8,128)(2,1)S(1)}, u32[]{:S(2)}, u32[]{:S(2)}) collective-permute-start(bf16[256,1536]{1,0:T(8,128)(2,1)S(1)} %broadcast_select_fusion), channel_id=1, source_target_pairs={{0,4},{1,5},{2,6},{3,7},{4,0},{5,1},{6,2},{7,3},{8,12},{9,13},{10,... | collective-permute-start | bytes 2359304 | tf_op jit(solution)/shard_map/ppermute | solution.py:24
  34.5 10.4 %collective-permute-start.2 = (bf16[256,768]{1,0:T(8,128)(2,1)S(1)}, bf16[256,768]{1,0:T(8,128)(2,1)S(1)}, u32[]{:S(2)}, u32[]{:S(2)}) collective-permute-start(bf16[256,768]{1,0:T(8,128)(2,1)S(1)} %slice_bitcast_fusion.1), channel_id=1, source_target_pairs={{0,64},{8,72},{16,80},{24,88},{32,96},{40,104},{48,112},{56,120},{... | collective-permute-start | bytes 1179656 | tf_op jit(solution)/shard_map/ppermute | solution.py:24
  44.9 13.3 %copy-start.13 = (bf16[256,768]{1,0:T(8,128)(2,1)}, bf16[256,768]{1,0:T(8,128)(2,1)S(1)}, u32[]{:S(2)}) copy-start(bf16[256,768]{1,0:T(8,128)(2,1)S(1)} %collective-permute-done.2.refs_5_) | copy-start | bytes 1179652
  50.5 60.7 %all-to-all-start = ((bf16[16,64,2048]{2,1,0:T(8,128)(2,1)}), bf16[16,64,2048]{2,1,0:T(8,128)(2,1)}, u32[]{:S(2)}, u32[]{:S(2)}) async-start(bf16[16,64,2048]{2,1,0:T(8,128)(2,1)} %bitcast.64), calls=%async_computation | async-start | bytes 8388608 | tf_op jit(solution)/shard_map/all_to_all | solution.py:340
  58.2 46.4 %collective-permute-start.3 = (bf16[256,768]{1,0:T(8,128)(2,1)S(1)}, bf16[256,768]{1,0:T(8,128)(2,1)S(1)}, u32[]{:S(2)}, u32[]{:S(2)}) collective-permute-start(bf16[256,768]{1,0:T(8,128)(2,1)S(1)} %broadcast_select_fusion.1), channel_id=1, source_target_pairs={{0,4},{1,5},{2,6},{3,7},{4,0},{5,1},{6,2},{7,3},{8,12},{9,13},{10,... | collective-permute-start | bytes 1179656 | tf_op jit(solution)/shard_map/ppermute | solution.py:24
  104.6 21.6 %copy-start.6 = (bf16[512,768]{1,0:T(8,128)(2,1)}, bf16[512,768]{1,0:T(8,128)(2,1)S(1)}, u32[]{:S(2)}) copy-start(bf16[512,768]{1,0:T(8,128)(2,1)S(1)} %pad_maximum_fusion.1.own_ref) | copy-start | bytes 2359300
  111.2 11.7 %copy-start = (f32[1,256,2304]{2,1,0:T(8,128)S(1)}, f32[1,256,2304]{2,1,0:T(8,128)}, u32[]{:S(2)}) copy-start(f32[1,256,2304]{2,1,0:T(8,128)} %param.12) | copy-start | bytes 7077892
  111.2 64.4 %all-to-all-start.1 = ((bf16[16,64,2048]{2,1,0:T(8,128)(2,1)}), bf16[16,64,2048]{2,1,0:T(8,128)(2,1)}, u32[]{:S(2)}, u32[]{:S(2)}) async-start(bf16[16,64,2048]{2,1,0:T(8,128)(2,1)} %bitcast.63), calls=%async_computation.1 | async-start | bytes 8388608 | tf_op jit(solution)/shard_map/all_to_all | solution.py:340
  122.9 128.5 %reduce-scatter.2.cloned.1.call-start = ((), (), s32[]{:S(2)}) async-start(), calls=%async_computation.5 | async-start | bytes 3932160 | tf_op jit(solution)/shard_map/reduce_scatter | solution.py:347
  122.9 1.7 copy-start.1
  124.7 21.7 %collective-permute-start.4 = (bf16[512,768]{1,0:T(8,128)(2,1)S(1)}, bf16[512,768]{1,0:T(8,128)(2,1)S(1)}, u32[]{:S(2)}, u32[]{:S(2)}) collective-permute-start(bf16[512,768]{1,0:T(8,128)(2,1)S(1)} %pad_maximum_fusion.1.own_ref), channel_id=1, source_target_pairs={{0,1},{1,2},{2,3},{3,0},{4,5},{5,6},{6,7},{7,4},{8,9},{9,10},{10,1... | collective-permute-start | bytes 2359304 | tf_op jit(solution)/shard_map/ppermute | solution.py:24
  126.2 20.2 %collective-permute-start.5 = (bf16[512,768]{1,0:T(8,128)(2,1)S(1)}, bf16[512,768]{1,0:T(8,128)(2,1)S(1)}, u32[]{:S(2)}, u32[]{:S(2)}) collective-permute-start(bf16[512,768]{1,0:T(8,128)(2,1)S(1)} %pad_maximum_fusion.1.own_ref), channel_id=1, source_target_pairs={{0,3},{1,0},{2,1},{3,2},{4,7},{5,4},{6,5},{7,6},{8,11},{9,8},{10,9... | collective-permute-start | bytes 2359304 | tf_op jit(solution)/shard_map/ppermute | solution.py:24
  129.7 21.0 %copy-start.15 = (bf16[256,768]{1,0:T(8,128)(2,1)S(1)}, bf16[256,768]{1,0:T(8,128)(2,1)}, u32[]{:S(2)}) copy-start(bf16[256,768]{1,0:T(8,128)(2,1)} %get-tuple-element.136) | copy-start | bytes 1179652
  129.7 21.0 %copy-start.16 = (bf16[256,768]{1,0:T(8,128)(2,1)S(1)}, bf16[256,768]{1,0:T(8,128)(2,1)}, u32[]{:S(2)}) copy-start(bf16[256,768]{1,0:T(8,128)(2,1)} %get-tuple-element.137) | copy-start | bytes 1179652
  142.0 9.7 %copy-start.14 = (bf16[256,768]{1,0:T(8,128)(2,1)S(1)}, bf16[256,768]{1,0:T(8,128)(2,1)}, u32[]{:S(2)}) copy-start(bf16[256,768]{1,0:T(8,128)(2,1)} %get-tuple-element.135) | copy-start | bytes 1179652
  146.4 6.3 %copy-start.11 = (bf16[512,768]{1,0:T(8,128)(2,1)}, bf16[512,768]{1,0:T(8,128)(2,1)S(1)}, u32[]{:S(2)}) copy-start(bf16[512,768]{1,0:T(8,128)(2,1)S(1)} %collective-permute-done.4.last_ref) | copy-start | bytes 2359300
  146.4 6.3 %copy-start.12 = (bf16[512,768]{1,0:T(8,128)(2,1)}, bf16[512,768]{1,0:T(8,128)(2,1)S(1)}, u32[]{:S(2)}) copy-start(bf16[512,768]{1,0:T(8,128)(2,1)S(1)} %collective-permute-done.5.next_ref) | copy-start | bytes 2359300
  147.2 28.4 %collective-permute-start.6 = (bf16[256,768]{1,0:T(8,128)(2,1)}, bf16[256,768]{1,0:T(8,128)(2,1)}, u32[]{:S(2)}, u32[]{:S(2)}) collective-permute-start(bf16[256,768]{1,0:T(8,128)(2,1)} %slice.92), channel_id=1, source_target_pairs={{0,1},{1,2},{2,3},{3,0},{4,5},{5,6},{6,7},{7,4},{8,9},{9,10},{10,1... | collective-permute-start | bytes 1179656 | tf_op jit(solution)/shard_map/ppermute | solution.py:24
  148.4 27.2 %collective-permute-start.7 = (bf16[256,768]{1,0:T(8,128)(2,1)}, bf16[256,768]{1,0:T(8,128)(2,1)}, u32[]{:S(2)}, u32[]{:S(2)}) collective-permute-start(bf16[256,768]{1,0:T(8,128)(2,1)} %slice.93), channel_id=1, source_target_pairs={{0,3},{1,0},{2,1},{3,2},{4,7},{5,4},{6,5},{7,6},{8,11},{9,8},{10,9... | collective-permute-start | bytes 1179656 | tf_op jit(solution)/shard_map/ppermute | solution.py:24
  182.6 24.2 %collective-permute-start.8 = (bf16[256,1536]{1,0:T(8,128)(2,1)S(1)}, bf16[256,1536]{1,0:T(8,128)(2,1)S(1)}, u32[]{:S(2)}, u32[]{:S(2)}) collective-permute-start(bf16[256,1536]{1,0:T(8,128)(2,1)S(1)} %get-tuple-element.87), channel_id=1, source_target_pairs={{0,64},{8,72},{16,80},{24,88},{32,96},{40,104},{48,112},{56,120},{... | collective-permute-start | bytes 2359304 | tf_op jit(solution)/shard_map/ppermute | solution.py:24
  207.8 61.8 %all-to-all-start.2 = ((bf16[16,64,2048]{2,1,0:T(8,128)(2,1)}), bf16[16,64,2048]{2,1,0:T(8,128)(2,1)}, u32[]{:S(2)}, u32[]{:S(2)}) async-start(bf16[16,64,2048]{2,1,0:T(8,128)(2,1)} %bitcast.62), calls=%async_computation.3 | async-start | bytes 8388608 | tf_op jit(solution)/shard_map/all_to_all | solution.py:340
  225.8 21.7 %copy-start.18 = (bf16[512,768]{1,0:T(8,128)(2,1)S(1)}, bf16[512,768]{1,0:T(8,128)(2,1)}, u32[]{:S(2)}) copy-start(bf16[512,768]{1,0:T(8,128)(2,1)} %get-tuple-element.97) | copy-start | bytes 2359300
  225.8 21.7 %collective-permute-start.11 = (bf16[512,768]{1,0:T(8,128)(2,1)}, bf16[512,768]{1,0:T(8,128)(2,1)S(1)}, u32[]{:S(2)}, u32[]{:S(2)}) collective-permute-start(bf16[512,768]{1,0:T(8,128)(2,1)} %get-tuple-element.98), channel_id=1, source_target_pairs={{0,1},{1,2},{2,3},{3,0},{4,5},{5,6},{6,7},{7,4},{8,9},{9,10},{10,1... | collective-permute-start | bytes 2359304 | tf_op jit(solution)/shard_map/ppermute | solution.py:24
  227.2 20.3 %collective-permute-start.12 = (bf16[512,768]{1,0:T(8,128)(2,1)}, bf16[512,768]{1,0:T(8,128)(2,1)S(1)}, u32[]{:S(2)}, u32[]{:S(2)}) collective-permute-start(bf16[512,768]{1,0:T(8,128)(2,1)} %get-tuple-element.99), channel_id=1, source_target_pairs={{0,3},{1,0},{2,1},{3,2},{4,7},{5,4},{6,5},{7,6},{8,11},{9,8},{10,9... | collective-permute-start | bytes 2359304 | tf_op jit(solution)/shard_map/ppermute | solution.py:24
  238.3 25.3 %collective-permute-start.10 = (bf16[512,768]{1,0:T(8,128)(2,1)}, bf16[512,768]{1,0:T(8,128)(2,1)S(1)}, u32[]{:S(2)}, u32[]{:S(2)}) collective-permute-start(bf16[512,768]{1,0:T(8,128)(2,1)} %get-tuple-element.96), channel_id=1, source_target_pairs={{0,3},{1,0},{2,1},{3,2},{4,7},{5,4},{6,5},{7,6},{8,11},{9,8},{10,9... | collective-permute-start | bytes 2359304 | tf_op jit(solution)/shard_map/ppermute | solution.py:24
  239.7 35.8 %collective-permute-start.9 = (bf16[512,768]{1,0:T(8,128)(2,1)}, bf16[512,768]{1,0:T(8,128)(2,1)S(1)}, u32[]{:S(2)}, u32[]{:S(2)}) collective-permute-start(bf16[512,768]{1,0:T(8,128)(2,1)} %get-tuple-element.95), channel_id=1, source_target_pairs={{0,1},{1,2},{2,3},{3,0},{4,5},{5,6},{6,7},{7,4},{8,9},{9,10},{10,1... | collective-permute-start | bytes 2359304 | tf_op jit(solution)/shard_map/ppermute | solution.py:24
  247.5 9.4 %copy-start.8 = (bf16[512,768]{1,0:T(8,128)(2,1)}, bf16[512,768]{1,0:T(8,128)(2,1)S(1)}, u32[]{:S(2)}) copy-start(bf16[512,768]{1,0:T(8,128)(2,1)S(1)} %collective-permute-done.12.refs_2_) | copy-start | bytes 2359300
  248.7 26.9 %collective-permute-start.13 = (bf16[256,768]{1,0:T(8,128)(2,1)}, bf16[256,768]{1,0:T(8,128)(2,1)}, u32[]{:S(2)}, u32[]{:S(2)}) collective-permute-start(bf16[256,768]{1,0:T(8,128)(2,1)} %get-tuple-element.143), channel_id=1, source_target_pairs={{0,1},{1,2},{2,3},{3,0},{4,5},{5,6},{6,7},{7,4},{8,9},{9,10},{10,1... | collective-permute-start | bytes 1179656 | tf_op jit(solution)/shard_map/ppermute | solution.py:24
  249.1 26.4 %collective-permute-start.14 = (bf16[256,768]{1,0:T(8,128)(2,1)}, bf16[256,768]{1,0:T(8,128)(2,1)}, u32[]{:S(2)}, u32[]{:S(2)}) collective-permute-start(bf16[256,768]{1,0:T(8,128)(2,1)} %get-tuple-element.142), channel_id=1, source_target_pairs={{0,3},{1,0},{2,1},{3,2},{4,7},{5,4},{6,5},{7,6},{8,11},{9,8},{10,9... | collective-permute-start | bytes 1179656 | tf_op jit(solution)/shard_map/ppermute | solution.py:24
  253.4 22.2 %collective-permute-start.15 = (bf16[256,768]{1,0:T(8,128)(2,1)}, bf16[256,768]{1,0:T(8,128)(2,1)S(1)}, u32[]{:S(2)}, u32[]{:S(2)}) collective-permute-start(bf16[256,768]{1,0:T(8,128)(2,1)} %get-tuple-element.139), channel_id=1, source_target_pairs={{0,4},{1,5},{2,6},{3,7},{4,0},{5,1},{6,2},{7,3},{8,12},{9,13},{10,... | collective-permute-start | bytes 1179656 | tf_op jit(solution)/shard_map/ppermute | solution.py:24
  263.6 12.0 %copy-start.7 = (bf16[512,768]{1,0:T(8,128)(2,1)}, bf16[512,768]{1,0:T(8,128)(2,1)S(1)}, u32[]{:S(2)}) copy-start(bf16[512,768]{1,0:T(8,128)(2,1)S(1)} %collective-permute-done.10.refs_2_) | copy-start | bytes 2359300
  263.6 27.5 %collective-permute-start.18 = (bf16[256,1536]{1,0:T(8,128)(2,1)}, bf16[256,1536]{1,0:T(8,128)(2,1)S(1)}, u32[]{:S(2)}, u32[]{:S(2)}) collective-permute-start(bf16[256,1536]{1,0:T(8,128)(2,1)} %pad_maximum_fusion.3), channel_id=1, source_target_pairs={{0,64},{8,72},{16,80},{24,88},{32,96},{40,104},{48,112},{56,120},{... | collective-permute-start | bytes 2359304 | tf_op jit(solution)/shard_map/ppermute | solution.py:24
  269.5 6.0 %copy-start.17 = (bf16[512,768]{1,0:T(8,128)(2,1)S(1)}, bf16[512,768]{1,0:T(8,128)(2,1)}, u32[]{:S(2)}) copy-start(bf16[512,768]{1,0:T(8,128)(2,1)} %get-tuple-element.110) | copy-start | bytes 2359300
  275.5 8.4 %copy-start.10 = (bf16[512,768]{1,0:T(8,128)(2,1)S(1)}, bf16[512,768]{1,0:T(8,128)(2,1)}, u32[]{:S(2)}) copy-start(bf16[512,768]{1,0:T(8,128)(2,1)} %get-tuple-element.117.refs_0_) | copy-start | bytes 2359300
  275.5 15.6 %copy-start.9 = (bf16[512,768]{1,0:T(8,128)(2,1)S(1)}, bf16[512,768]{1,0:T(8,128)(2,1)}, u32[]{:S(2)}) copy-start(bf16[512,768]{1,0:T(8,128)(2,1)} %get-tuple-element.109.refs_0_) | copy-start | bytes 2359300
  275.6 15.7 %copy-start.19 = (bf16[256,768]{1,0:T(8,128)(2,1)}, bf16[256,768]{1,0:T(8,128)(2,1)S(1)}, u32[]{:S(2)}) copy-start(bf16[256,768]{1,0:T(8,128)(2,1)S(1)} %collective-permute-done.15.refs_1_) | copy-start | bytes 1179652
  275.8 15.3 %collective-permute-start.16 = (bf16[256,768]{1,0:T(8,128)(2,1)S(1)}, bf16[256,768]{1,0:T(8,128)(2,1)S(1)}, u32[]{:S(2)}, u32[]{:S(2)}) collective-permute-start(bf16[256,768]{1,0:T(8,128)(2,1)S(1)} %get-tuple-element.141), channel_id=1, source_target_pairs={{0,1},{1,2},{2,3},{3,0},{4,5},{5,6},{6,7},{7,4},{8,9},{9,10},{10,1... | collective-permute-start | bytes 1179656 | tf_op jit(solution)/shard_map/ppermute | solution.py:24
  277.4 13.6 %collective-permute-start.17 = (bf16[256,768]{1,0:T(8,128)(2,1)S(1)}, bf16[256,768]{1,0:T(8,128)(2,1)S(1)}, u32[]{:S(2)}, u32[]{:S(2)}) collective-permute-start(bf16[256,768]{1,0:T(8,128)(2,1)S(1)} %get-tuple-element.140), channel_id=1, source_target_pairs={{0,3},{1,0},{2,1},{3,2},{4,7},{5,4},{6,5},{7,6},{8,11},{9,8},{10,9... | collective-permute-start | bytes 1179656 | tf_op jit(solution)/shard_map/ppermute | solution.py:24
  279.8 28.1 %collective-permute-start.20 = (bf16[256,1536]{1,0:T(8,128)(2,1)}, bf16[256,1536]{1,0:T(8,128)(2,1)S(1)}, u32[]{:S(2)}, u32[]{:S(2)}) collective-permute-start(bf16[256,1536]{1,0:T(8,128)(2,1)} %get-tuple-element.116), channel_id=1, source_target_pairs={{0,64},{8,72},{16,80},{24,88},{32,96},{40,104},{48,112},{56,120},{... | collective-permute-start | bytes 2359304 | tf_op jit(solution)/shard_map/ppermute | solution.py:24
  285.8 12.6 %collective-permute-start.21 = (bf16[256,768]{1,0:T(8,128)(2,1)}, bf16[256,768]{1,0:T(8,128)(2,1)}, u32[]{:S(2)}, u32[]{:S(2)}) collective-permute-start(bf16[256,768]{1,0:T(8,128)(2,1)} %add_convert_fusion), channel_id=1, source_target_pairs={{0,4},{1,5},{2,6},{3,7},{4,0},{5,1},{6,2},{7,3},{8,12},{9,13},{10,... | collective-permute-start | bytes 1179656 | tf_op jit(solution)/shard_map/ppermute | solution.py:24
  291.1 3.5 %copy-start.5 = (bf16[256,1536]{1,0:T(8,128)(2,1)}, bf16[256,1536]{1,0:T(8,128)(2,1)S(1)}, u32[]{:S(2)}) copy-start(bf16[256,1536]{1,0:T(8,128)(2,1)S(1)} %collective-permute-done.18.refs_7_.refs_9_) | copy-start | bytes 2359300
  291.9 16.1 %collective-permute-start.19 = (bf16[256,768]{1,0:T(8,128)(2,1)S(1)}, bf16[256,768]{1,0:T(8,128)(2,1)S(1)}, u32[]{:S(2)}, u32[]{:S(2)}) collective-permute-start(bf16[256,768]{1,0:T(8,128)(2,1)S(1)} %add_convert_fusion.1), channel_id=1, source_target_pairs={{0,4},{1,5},{2,6},{3,7},{4,0},{5,1},{6,2},{7,3},{8,12},{9,13},{10,... | collective-permute-start | bytes 1179656 | tf_op jit(solution)/shard_map/ppermute | solution.py:24
  307.9 1.0 copy-start.21
  (3 other events, 2.6 us)
Sparse Core Ops, SparseCore 0:
  50.6 69.9 all-gather.1
  182.7 46.1 reduce-scatter.1
